TPU v7x, 32 devices: a whole 2x2x4 slice. The times are simulated.
32 devices in a mesh: ctx: 16 (over z, x, core), head: 2 (over y).
Axes of the slice: x: 2, y: 2, z: 4, core: 2. Of those that a mesh axis runs over, the one named last changes fastest.
Arguments:
- absorbed_query: bfloat16 [64, 128, 576], P('ctx', 'head'), may hold values from -20 to 20
- index_query: bfloat16 [64, 64, 128], P('ctx', 'head'), may hold values from -20 to 20
- index_weight: bfloat16 [64, 64], P('ctx', 'head'), may hold values from -2 to 2
- kv_cache: bfloat16 [65536, 576], P('ctx'), may hold values from -4 to 4
- index_keys: bfloat16 [65536, 128], P('ctx'), may hold values from -4 to 4
- lengths: int32 [64], replicated, may hold values from 16384 to 65536
Outputs:
- target: float32 [64, 65536], P('head', 'ctx')
- gradient: float32 [64, 65536], P('head', 'ctx')
All inputs are finite; a program needn't handle non-finite values.
Results may differ from a plain program's by a relative error of at most 0.0003.
Values may be sent and summed in bfloat16 or wider, within the bound.
No kernel may reach another device: no remote copies, remote signals or barrier semaphores. Data moves between devices by JAX's collectives and lax.ppermute only.
A program may use at most 192 MiB of HBM per device.

v0:
```python
import jax
import jax.numpy as jnp
from jax import lax
from jax.sharding import PartitionSpec as P

attention_scale = 192.0 ** (-0.5)
far_below = -1e30


def merged(part, axis, combine):
    gathered = jax.tree.map(lambda a: lax.all_gather(a, axis), part)

    def take(source):
        return jax.tree.map(lambda a: lax.dynamic_index_in_dim(a, source, 0, False), gathered)

    return lax.fori_loop(
        1, lax.axis_size(axis), lambda source, state: combine(state, take(source)), take(0)
    )


def block_scores(
    flat_query, kv_cache, row_lengths, key_start, block_index, block_keys, row_count, head_count
):
    cached = lax.dynamic_slice_in_dim(kv_cache, block_index * block_keys, block_keys, 0)
    scores = (
        jnp.einsum("qd,kd->qk", flat_query, cached, preferred_element_type=jnp.float32)
        * attention_scale
    )
    scores = scores.reshape(row_count, head_count, block_keys)
    key_index = key_start + block_index * block_keys + jnp.arange(block_keys, dtype=jnp.int32)
    visible = key_index[None, :] < row_lengths[:, None]
    return jnp.where(visible[:, None, :], scores, -jnp.inf)


def first_sweep(queries, idx_query, idx_weight, kv_cache, index_keys, row_lengths, key_start):
    row_count, head_count, latent_width = queries.shape
    ctx_keys = kv_cache.shape[0]
    block_keys = min(1024, ctx_keys)
    flat_query = queries.reshape(row_count * head_count, latent_width)
    weight_full = idx_weight.astype(jnp.float32)
    index_scale = idx_query.shape[-1] ** (-0.5)

    def advance(block_index, carry):
        att_max, att_total, logits, kept = carry
        scores = block_scores(
            flat_query,
            kv_cache,
            row_lengths,
            key_start,
            block_index,
            block_keys,
            row_count,
            head_count,
        )
        kept = lax.dynamic_update_slice_in_dim(kept, scores, block_index * block_keys, 2)
        new_max = jnp.maximum(att_max, jnp.max(scores, axis=-1))
        att_total = att_total * jnp.exp(att_max - new_max) + jnp.sum(
            jnp.exp(scores - new_max[..., None]), axis=-1
        )
        idx_cached = lax.dynamic_slice_in_dim(index_keys, block_index * block_keys, block_keys, 0)
        inner = jnp.einsum("rgd,kd->rgk", idx_query, idx_cached, preferred_element_type=jnp.float32)
        piece = (
            jnp.einsum(
                "rg,rgk->rk", weight_full, jnp.maximum(inner, 0.0), precision=lax.Precision.HIGHEST
            )
            * index_scale
        )
        logits = lax.dynamic_update_slice_in_dim(logits, piece, block_index * block_keys, 1)
        return (new_max, att_total, logits, kept)

    start = (
        jnp.full((row_count, head_count), far_below, jnp.float32),
        jnp.zeros((row_count, head_count), jnp.float32),
        jnp.zeros((row_count, ctx_keys), jnp.float32),
        jnp.zeros((row_count, head_count, ctx_keys), jnp.float32),
    )
    return lax.fori_loop(0, ctx_keys // block_keys, advance, start)


def second_sweep(kept, att_max, att_total):
    weights = jnp.exp(kept - att_max[..., None]) / att_total[..., None]
    return jnp.sum(weights, axis=1)


def combine_pairs(first, second):
    outputs = []
    for place in range(0, len(first), 2):
        larger = jnp.maximum(first[place], second[place])
        total = first[place + 1] * jnp.exp(first[place] - larger) + second[place + 1] * jnp.exp(
            second[place] - larger
        )
        outputs.append(larger)
        outputs.append(total)
    return tuple(outputs)


def body(absorbed_query, index_query, index_weight, kv_cache, index_keys, lengths):
    gathered = (
        lax.all_gather(absorbed_query, "ctx", axis=0, tiled=True),
        lax.all_gather(index_query, "ctx", axis=0, tiled=True),
        lax.all_gather(index_weight, "ctx", axis=0, tiled=True),
    )
    ctx_keys = kv_cache.shape[0]
    key_start = lax.axis_index("ctx") * ctx_keys
    keys_total = ctx_keys * lax.axis_size("ctx")
    heads_total = absorbed_query.shape[1] * lax.axis_size("head")
    own_rows = absorbed_query.shape[0] * lax.axis_size("ctx") // lax.axis_size("head")
    own_lengths = lax.dynamic_slice_in_dim(lengths, lax.axis_index("head") * own_rows, own_rows)
    queries, idx_query, idx_weight = gathered
    att_max, att_total, logits, kept = first_sweep(
        queries, idx_query, idx_weight, kv_cache, index_keys, lengths, key_start
    )
    logits = lax.psum_scatter(logits, "head", scatter_dimension=0, tiled=True)
    key_index = key_start + jnp.arange(ctx_keys, dtype=jnp.int32)
    logits = jnp.where(key_index[None, :] < own_lengths[:, None], logits, -jnp.inf)
    idx_max = jnp.maximum(jnp.max(logits, axis=-1), far_below)
    idx_total = jnp.sum(jnp.exp(logits - idx_max[:, None]), axis=-1)
    att_max, att_total, idx_max, idx_total = merged(
        (att_max, att_total, idx_max, idx_total), "ctx", combine_pairs
    )
    summed = second_sweep(kept, att_max, att_total)
    summed = lax.psum_scatter(summed, "head", scatter_dimension=0, tiled=True)
    summed = summed / heads_total
    predicted = jnp.exp(logits - idx_max[:, None]) / idx_total[:, None]
    return (keys_total * summed, keys_total * (predicted - summed))


def solution(mesh):
    return jax.shard_map(
        body,
        mesh=mesh,
        in_specs=(
            P("ctx", "head", None),
            P("ctx", "head", None),
            P("ctx", "head"),
            P("ctx", None),
            P("ctx", None),
            P(),
        ),
        out_specs=(P("head", "ctx"), P("head", "ctx")),
        check_vma=False,
    )
```

profile of v0, /device:TPU:0, one launch (start us, length us, event | category | flops | bytes accessed | tf_op | source)
XLA Modules:
  0.0 513.2 jit_solution(5937231811211355522)
XLA Ops:
  8.0 25.8 %all_gather.32 = bf16[64,32,128]{2,1,0:T(8,128)(2,1)S(1)} all-gather(bf16[4,32,128]{2,1,0:T(8,128)(2,1)} %param.11), channel_id=1, replica_groups=mesh['ctx'=16,'head'=2] {'ctx'}, dimensions={0}, use_global_device_ids=true | all-gather | bytes 557056 | tf_op jit(solution)/shard_map/all_gather | solution.py:100
  34.0 17.8 %all-gather.4 = bf16[16,4,32]{2,1,0:T(4,128)(2,1)S(1)} all-gather(bf16[1,4,32]{2,1,0:T(4,128)(2,1)} %bitcast.79), channel_id=1, replica_groups=mesh['ctx'=16,'head'=2] {'ctx'}, dimensions={0}, use_global_device_ids=true | all-gather | bytes 4352 | tf_op jit(solution)/shard_map/all_gather | solution.py:101
  51.8 18.4 %all-gather.7.cloned.1.call-done = bf16[64,64,576]{2,1,0:T(8,128)(2,1)} async-done(((bf16[4,64,576]{2,1,0:T(8,128)(2,1)}), bf16[64,64,576]{2,1,0:T(8,128)(2,1)}) %all-gather.7.cloned.1.call-update) | async-done | bytes 4718608 | tf_op jit(solution)/shard_map/all_gather | solution.py:99
  70.2 21.2 %broadcast_in_dim.68 = f32[64,64,4096]{2,1,0:T(8,128)} broadcast(f32[]{:T(128)} %constant.131.clone.1), dimensions={} | broadcast | bytes 67108864 | tf_op jit(solution)/shard_map/broadcast_in_dim | solution.py:75
  91.5 295.7 %while.42 = (s32[]{:T(128)}, f32[64,64]{1,0:T(8,128)S(1)}, f32[64,64]{1,0:T(8,128)S(1)}, f32[64,4096]{1,0:T(8,128)S(1)}, f32[64,64,4096]{2,1,0:T(8,128)}, /*inde...) while((s32[]{:T(128)}, f32[64,64]{1,0:T(8,128)S(1)}, ...), condition=%wide.region_3.4_spmd.clone, body=%wide.region_0.3_spmd.clone.sunk | while | flops 5425484800 | bytes 146932208 | solution.py:77
  92.7 7.1 %copy.25 = pred[4096,1024]{0,1:T(32,128)(4,1)} copy(pred[4096,1024]{1,0:T(32,128)(4,1)S(1)} %bitcast.74) | data formatting | bytes 8388608 | tf_op jit(solution)/shard_map/while/body/eval_jaxpr/jit(_where)/broadcast_in_dim | solution.py:32
  99.7 13.3 %fusion.42 = (f32[4096]{0:T(1024)S(1)}, f32[4096,1024]{0,1:T(8,128)}) fusion(pred[4096,1024]{0,1:T(32,128)(4,1)} %copy.25, bf16[4096,576]{1,0:T(8,128)(2,1)} %get-tuple-element.720, bf16[4096,576]{0,1:T(8,128)(2,1)} %get-tuple-element.719, s32[]{:T(128)S(6)} %select_n.79), kind=kOutput, calls=%fused_computation.19.clone.1 | convolution fusion | flops 4844417024 | bytes 27410436 | tf_op jit(solution)/shard_map/while/body/eval_jaxpr/qd,kd->qk/dot_general | solution.py:26
  113.2 10.9 %exponential_reduce_fusion.3 = f32[4096]{0:T(1024)S(1)} fusion(f32[4096]{0:T(1024)S(1)} %sub.141, pred[4096,1024]{0,1:T(32,128)(4,1)} %copy.25, f32[4096,1024]{0,1:T(8,128)} %get-tuple-element.679), kind=kLoop, calls=%fused_computation.13.clone.1 | loop fusion | flops 12578816 | bytes 21004288 | tf_op jit(solution)/shard_map/while/body/eval_jaxpr/reduce_sum | solution.py:57
  126.4 9.1 %fusion.44 = f32[64,1,1024]{2,1,0:T(1,128)S(1)} fusion(f32[64,32,1]{1,2,0:T(1,128)S(1)} %bitcast.75, f32[64,32,1024]{2,0,1:T(8,128)S(1)} %maximum_bitcast_fusion.2), kind=kOutput, calls=%fused_computation.15.clone.1 | convolution fusion | flops 25165824 | bytes 8658944 | tf_op jit(solution)/shard_map/while/body/eval_jaxpr/rg,rgk->rk/dot_general | solution.py:63
  135.6 17.4 %copy.26 = f32[4096,1024]{1,0:T(8,128)} copy(f32[4096,1024]{0,1:T(8,128)} %get-tuple-element.679) | data formatting | bytes 33554432 | tf_op jit(solution)/shard_map/while/body/eval_jaxpr/mul | solution.py:26
  153.0 12.4 %select_dynamic-update-slice_fusion.2 = f32[64,64,4096]{2,1,0:T(8,128)} fusion(f32[64,64,4096]{2,1,0:T(8,128)} %get-tuple-element.700, s32[]{:T(128)S(6)} %select_n.79, f32[64,64,1024]{2,1,0:T(8,128)} %bitcast.73, pred[64,1024]{1,0:T(8,128)(4,1)S(1)} %broadcast_compare_fusion.2), kind=kLoop, calls=%fused_computation.12.clone.1 | loop fusion | flops 4194304 | bytes 33619972 | tf_op jit(solution)/shard_map/while/body/eval_jaxpr/dynamic_update_slice | solution.py:55
  166.6 7.1 %copy.25 = pred[4096,1024]{0,1:T(32,128)(4,1)} copy(pred[4096,1024]{1,0:T(32,128)(4,1)S(1)} %bitcast.74) | data formatting | bytes 8388608 | tf_op jit(solution)/shard_map/while/body/eval_jaxpr/jit(_where)/broadcast_in_dim | solution.py:32
  173.6 13.3 %fusion.42 = (f32[4096]{0:T(1024)S(1)}, f32[4096,1024]{0,1:T(8,128)}) fusion(pred[4096,1024]{0,1:T(32,128)(4,1)} %copy.25, bf16[4096,576]{1,0:T(8,128)(2,1)} %get-tuple-element.720, bf16[4096,576]{0,1:T(8,128)(2,1)} %get-tuple-element.719, s32[]{:T(128)S(6)} %select_n.79), kind=kOutput, calls=%fused_computation.19.clone.1 | convolution fusion | flops 4844417024 | bytes 27410436 | tf_op jit(solution)/shard_map/while/body/eval_jaxpr/qd,kd->qk/dot_general | solution.py:26
  187.1 10.9 %exponential_reduce_fusion.3 = f32[4096]{0:T(1024)S(1)} fusion(f32[4096]{0:T(1024)S(1)} %sub.141, pred[4096,1024]{0,1:T(32,128)(4,1)} %copy.25, f32[4096,1024]{0,1:T(8,128)} %get-tuple-element.679), kind=kLoop, calls=%fused_computation.13.clone.1 | loop fusion | flops 12578816 | bytes 21004288 | tf_op jit(solution)/shard_map/while/body/eval_jaxpr/reduce_sum | solution.py:57
  200.3 9.1 %fusion.44 = f32[64,1,1024]{2,1,0:T(1,128)S(1)} fusion(f32[64,32,1]{1,2,0:T(1,128)S(1)} %bitcast.75, f32[64,32,1024]{2,0,1:T(8,128)S(1)} %maximum_bitcast_fusion.2), kind=kOutput, calls=%fused_computation.15.clone.1 | convolution fusion | flops 25165824 | bytes 8658944 | tf_op jit(solution)/shard_map/while/body/eval_jaxpr/rg,rgk->rk/dot_general | solution.py:63
  209.5 17.4 %copy.26 = f32[4096,1024]{1,0:T(8,128)} copy(f32[4096,1024]{0,1:T(8,128)} %get-tuple-element.679) | data formatting | bytes 33554432 | tf_op jit(solution)/shard_map/while/body/eval_jaxpr/mul | solution.py:26
  226.9 12.4 %select_dynamic-update-slice_fusion.2 = f32[64,64,4096]{2,1,0:T(8,128)} fusion(f32[64,64,4096]{2,1,0:T(8,128)} %get-tuple-element.700, s32[]{:T(128)S(6)} %select_n.79, f32[64,64,1024]{2,1,0:T(8,128)} %bitcast.73, pred[64,1024]{1,0:T(8,128)(4,1)S(1)} %broadcast_compare_fusion.2), kind=kLoop, calls=%fused_computation.12.clone.1 | loop fusion | flops 4194304 | bytes 33619972 | tf_op jit(solution)/shard_map/while/body/eval_jaxpr/dynamic_update_slice | solution.py:55
  247.6 13.3 %fusion.42 = (f32[4096]{0:T(1024)S(1)}, f32[4096,1024]{0,1:T(8,128)}) fusion(pred[4096,1024]{0,1:T(32,128)(4,1)} %copy.25, bf16[4096,576]{1,0:T(8,128)(2,1)} %get-tuple-element.720, bf16[4096,576]{0,1:T(8,128)(2,1)} %get-tuple-element.719, s32[]{:T(128)S(6)} %select_n.79), kind=kOutput, calls=%fused_computation.19.clone.1 | convolution fusion | flops 4844417024 | bytes 27410436 | tf_op jit(solution)/shard_map/while/body/eval_jaxpr/qd,kd->qk/dot_general | solution.py:26
  261.0 10.9 %exponential_reduce_fusion.3 = f32[4096]{0:T(1024)S(1)} fusion(f32[4096]{0:T(1024)S(1)} %sub.141, pred[4096,1024]{0,1:T(32,128)(4,1)} %copy.25, f32[4096,1024]{0,1:T(8,128)} %get-tuple-element.679), kind=kLoop, calls=%fused_computation.13.clone.1 | loop fusion | flops 12578816 | bytes 21004288 | tf_op jit(solution)/shard_map/while/body/eval_jaxpr/reduce_sum | solution.py:57
  274.2 9.1 %fusion.44 = f32[64,1,1024]{2,1,0:T(1,128)S(1)} fusion(f32[64,32,1]{1,2,0:T(1,128)S(1)} %bitcast.75, f32[64,32,1024]{2,0,1:T(8,128)S(1)} %maximum_bitcast_fusion.2), kind=kOutput, calls=%fused_computation.15.clone.1 | convolution fusion | flops 25165824 | bytes 8658944 | tf_op jit(solution)/shard_map/while/body/eval_jaxpr/rg,rgk->rk/dot_general | solution.py:63
  283.4 17.4 %copy.26 = f32[4096,1024]{1,0:T(8,128)} copy(f32[4096,1024]{0,1:T(8,128)} %get-tuple-element.679) | data formatting | bytes 33554432 | tf_op jit(solution)/shard_map/while/body/eval_jaxpr/mul | solution.py:26
  300.9 12.4 %select_dynamic-update-slice_fusion.2 = f32[64,64,4096]{2,1,0:T(8,128)} fusion(f32[64,64,4096]{2,1,0:T(8,128)} %get-tuple-element.700, s32[]{:T(128)S(6)} %select_n.79, f32[64,64,1024]{2,1,0:T(8,128)} %bitcast.73, pred[64,1024]{1,0:T(8,128)(4,1)S(1)} %broadcast_compare_fusion.2), kind=kLoop, calls=%fused_computation.12.clone.1 | loop fusion | flops 4194304 | bytes 33619972 | tf_op jit(solution)/shard_map/while/body/eval_jaxpr/dynamic_update_slice | solution.py:55
  321.5 13.3 %fusion.42 = (f32[4096]{0:T(1024)S(1)}, f32[4096,1024]{0,1:T(8,128)}) fusion(pred[4096,1024]{0,1:T(32,128)(4,1)} %copy.25, bf16[4096,576]{1,0:T(8,128)(2,1)} %get-tuple-element.720, bf16[4096,576]{0,1:T(8,128)(2,1)} %get-tuple-element.719, s32[]{:T(128)S(6)} %select_n.79), kind=kOutput, calls=%fused_computation.19.clone.1 | convolution fusion | flops 4844417024 | bytes 27410436 | tf_op jit(solution)/shard_map/while/body/eval_jaxpr/qd,kd->qk/dot_general | solution.py:26
  335.0 10.9 %exponential_reduce_fusion.3 = f32[4096]{0:T(1024)S(1)} fusion(f32[4096]{0:T(1024)S(1)} %sub.141, pred[4096,1024]{0,1:T(32,128)(4,1)} %copy.25, f32[4096,1024]{0,1:T(8,128)} %get-tuple-element.679), kind=kLoop, calls=%fused_computation.13.clone.1 | loop fusion | flops 12578816 | bytes 21004288 | tf_op jit(solution)/shard_map/while/body/eval_jaxpr/reduce_sum | solution.py:57
  348.1 9.1 %fusion.44 = f32[64,1,1024]{2,1,0:T(1,128)S(1)} fusion(f32[64,32,1]{1,2,0:T(1,128)S(1)} %bitcast.75, f32[64,32,1024]{2,0,1:T(8,128)S(1)} %maximum_bitcast_fusion.2), kind=kOutput, calls=%fused_computation.15.clone.1 | convolution fusion | flops 25165824 | bytes 8658944 | tf_op jit(solution)/shard_map/while/body/eval_jaxpr/rg,rgk->rk/dot_general | solution.py:63
  357.3 17.4 %copy.26 = f32[4096,1024]{1,0:T(8,128)} copy(f32[4096,1024]{0,1:T(8,128)} %get-tuple-element.679) | data formatting | bytes 33554432 | tf_op jit(solution)/shard_map/while/body/eval_jaxpr/mul | solution.py:26
  374.8 12.4 %select_dynamic-update-slice_fusion.2 = f32[64,64,4096]{2,1,0:T(8,128)} fusion(f32[64,64,4096]{2,1,0:T(8,128)} %get-tuple-element.700, s32[]{:T(128)S(6)} %select_n.79, f32[64,64,1024]{2,1,0:T(8,128)} %bitcast.73, pred[64,1024]{1,0:T(8,128)(4,1)S(1)} %broadcast_compare_fusion.2), kind=kLoop, calls=%fused_computation.12.clone.1 | loop fusion | flops 4194304 | bytes 33619972 | tf_op jit(solution)/shard_map/while/body/eval_jaxpr/dynamic_update_slice | solution.py:55
  389.5 20.6 %all-gather = f32[1024,64]{1,0:T(8,128)S(1)} all-gather(f32[64,64]{1,0:T(8,128)S(1)} %get-tuple-element.428), channel_id=2, replica_groups=mesh['ctx'=16,'head'=2] {'ctx'}, dimensions={0}, use_global_device_ids=true | all-gather | bytes 278528 | tf_op jit(solution)/shard_map/all_gather | solution.py:11
  410.1 18.9 %all-gather.1 = f32[1024,64]{1,0:T(8,128)S(1)} all-gather(f32[64,64]{1,0:T(8,128)S(1)} %get-tuple-element.429), channel_id=3, replica_groups=mesh['ctx'=16,'head'=2] {'ctx'}, dimensions={0}, use_global_device_ids=true | all-gather | bytes 278528 | tf_op jit(solution)/shard_map/all_gather | solution.py:11
  431.9 31.1 %all-reduce.2 = (f32[512]{0:T(512)S(1)}, f32[512]{0:T(512)S(1)}) all-reduce(f32[512]{0:T(512)S(1)} %get-tuple-element.539, f32[512]{0:T(512)S(1)} %dynamic-update-slice.1), channel_id=4, replica_groups=mesh['ctx'=16,'head'=2] {'ctx'}, use_global_device_ids=true, to_apply=%add | all-reduce | flops 1024 | bytes 8192
  464.5 22.4 %fusion.17 = f32[64,4096]{1,0:T(8,128)} fusion(f32[64,64,4096]{2,1,0:T(8,128)} %get-tuple-element.427, f32[64,64]{1,0:T(8,128)S(1)} %get-tuple-element.432, f32[64,64]{1,0:T(8,128)S(1)} %get-tuple-element.431), kind=kLoop, calls=%fused_computation.33 | loop fusion | flops 50069504 | bytes 68190208 | tf_op jit(solution)/shard_map/reduce_sum | solution.py:82
  486.9 17.6 %reduce-scatter.5.cloned.1.call-done = f32[32,4096]{1,0:T(8,128)} async-done(((f32[64,4096]{1,0:T(8,128)}), f32[32,4096]{1,0:T(8,128)}) %reduce-scatter.5.cloned.1.call-update) | async-done | bytes 524304 | tf_op jit(solution)/shard_map/reduce_scatter | solution.py:122
  (113 shorter events, 39.3 us)
Async XLA Ops:
  7.2 63.0 %all-gather.7.cloned.1.call-start = ((), (), s32[]{:S(2)}) async-start(), calls=%async_computation.2 | async-start | bytes 5570560 | tf_op jit(solution)/shard_map/all_gather | solution.py:99
  7.9 421.1 %reduce-scatter.3.cloned.1.call-start = ((), (), s32[]{:S(2)}) async-start(), calls=%async_computation.3 | async-start | bytes 1572864 | tf_op jit(solution)/shard_map/reduce_scatter | solution.py:113
  70.2 21.2 %copy-start.2 = (s32[64]{0:T(128)S(1)}, s32[64]{0:T(128)}, u32[]{:S(2)}) copy-start(s32[64]{0:T(128)} %param.15) | copy-start | bytes 772
  91.5 296.8 %copy-start.3 = (u32[32]{0:T(128)S(1)}, u32[32]{0:T(128)}, u32[]{:S(2)}) copy-start(u32[32]{0:T(128)} %constant.146) | copy-start | bytes 388
  387.1 1.0 copy-start.1
  388.1 116.3 %reduce-scatter.5.cloned.1.call-start = ((), (), s32[]{:S(2)}) async-start(), calls=%async_computation.4 | async-start | bytes 1572864 | tf_op jit(solution)/shard_map/reduce_scatter | solution.py:122
  464.5 40.0 %copy-start = (f32[32,4096]{1,0:T(8,128)S(1)}, f32[32,4096]{1,0:T(8,128)}, u32[]{:S(2)}) copy-start(f32[32,4096]{1,0:T(8,128)} %reduce-scatter.3.cloned.1.call-done) | copy-start | bytes 1572868
Sparse Core Ops, SparseCore 0:
  10.3 59.8 all-gather.6
  388.3 18.8 reduce-scatter.2
  487.0 17.3 reduce-scatter.4
where the time goes:
time: 515 us; the launch traced here: 513 us
  local copies, waits for them, and re-layouts  127 us (25%)
  other arithmetic  122 us (24%)
  blocking collectives  114 us (22%)
  matrix products  98.5 us (19%)
  waiting for transfers between devices  36.6 us (7%)
  between operations  14.5 us (3%)
    mul x4, local copies, waits for them, and re-layouts, block_scores(): jnp.einsum('qd,kd->qk', flat_query, cached, preferred_element_type=jnp.fl...  69.8 us
    dot_general x4, matrix products, block_scores(): jnp.einsum('qd,kd->qk', flat_query, cached, preferred_element_type=jnp.fl...  53.1 us
    dynamic_update_slice x4, other arithmetic, advance(): lax.dynamic_update_slice_in_dim(kept, scores, block_index * block_keys, 2)  49.5 us
    reduce_sum x4, other arithmetic, advance(): jnp.sum(jnp.exp(scores - new_max[..., None]), axis=-1)  43.4 us
    all_gather x2, blocking collectives, merged(): gathered = jax.tree.map(lambda a: lax.all_gather(a, axis), part)  39.4 us
    dot_general x4, matrix products, advance(): jnp.einsum('rg,rgk->rk', weight_full, jnp.maximum(inner, 0.0), precision=...  36.6 us
    broadcast_in_dim x8, local copies, waits for them, and re-layouts, block_scores(): return jnp.where(visible[:, None, :], scores, -jnp.inf)  32.6 us
    unnamed x1, blocking collectives  31.1 us
  transfers between devices with their start and end apart: 3, of which 2 were waited for; matrix products, arithmetic and copies ran while one was open for 0% of the time, Pallas kernels for 0%

commit v1 on v0

v1 whole, which is shorter than its diff:
```python
import functools

import jax
import jax.numpy as jnp
from jax import lax
from jax.experimental import pallas as pl
from jax.experimental.pallas import tpu as pltpu
from jax.sharding import PartitionSpec as P

attention_scale = 192.0 ** (-0.5)
log2_e = 1.4426950408889634
far_below = -1e30
levels = 32767.0
lanes = 128
vmem_limit = 56 * 2**20


def sweep_kernel(
    row_count, head_count, idx_heads, latent, tile_keys, count, kept, ids, lengths, start, q_ref, kv_ref, ik_ref, *rest
):
    e_ref, top_ref, stat_ref, part_ref, s_a, s_b, m_a, m_b = rest[kept:]
    step = pl.program_id(0)
    queries = row_count * head_count
    keys = kv_ref.shape[0]
    idx_queries = row_count * idx_heads
    scale = attention_scale * log2_e
    first_row = ids[jnp.minimum(step, count - 1)] * row_count

    def scores(at, s_ref, m_ref, masked):
        y = lax.dot_general(
            q_ref[0, :queries, :],
            kv_ref[at : at + tile_keys, :],
            (((1,), (1,)), ((), ())),
            preferred_element_type=jnp.float32,
        )
        if masked:
            key = lax.broadcasted_iota(jnp.int32, (head_count, tile_keys), 1) + (start[0] + at)
            pieces = []
            for r in range(row_count):
                piece = y[r * head_count : (r + 1) * head_count]
                pieces.append(jnp.where(key < lengths[first_row + r], piece, -jnp.inf))
            y = jnp.concatenate(pieces, axis=0)
        s_ref[:, at : at + tile_keys] = y
        top = y[:, :lanes]
        for j in range(lanes, tile_keys, lanes):
            top = jnp.maximum(top, y[:, j : j + lanes])
        m_ref[...] = jnp.maximum(top, far_below if at == 0 else m_ref[...])

    def index_part(at):
        packed = q_ref[0, :, latent:]
        half = packed.shape[1]
        idx_query = jnp.concatenate([packed[:idx_queries], packed[idx_queries : 2 * idx_queries]], axis=1)
        weight = q_ref[0, queries : queries + 8, :lanes].astype(jnp.float32)[0:1]
        weight = jnp.transpose(jnp.broadcast_to(weight, (lanes, lanes)))
        inner = lax.dot_general(
            idx_query, ik_ref[at : at + tile_keys, :], (((1,), (1,)), ((), ())), preferred_element_type=jnp.float32
        )
        inner = jnp.maximum(inner, 0.0)
        for r in range(row_count):
            mine = slice(r * idx_heads, (r + 1) * idx_heads)
            for j in range(0, tile_keys, lanes):
                product = inner[mine, j : j + lanes] * weight[mine]
                part_ref[0, r : r + 1, at + j : at + j + lanes] = jnp.sum(product, axis=0, keepdims=True)

    def exponentials(at, s_ref, m_ref):
        for q in range(0, queries, 16):
            top = m_ref[q : q + 16, :]
            total = None
            for j in range(at, at + tile_keys, lanes):
                e = jnp.exp2((s_ref[q : q + 16, j : j + lanes] - top) * scale)
                total = e if total is None else total + e
                e_ref[0, q : q + 16, j : j + lanes] = jnp.round(e * levels).astype(jnp.int32).astype(jnp.int16)
            if at == 0:
                top_ref[0, q : q + 16, :] = total
            else:
                top_ref[0, q : q + 16, :] += total

    def finish(m_ref):
        top = jnp.transpose(m_ref[...])
        total = jnp.transpose(top_ref[0])
        largest = jnp.max(top, axis=0, keepdims=True)
        stat_ref[0, 0:1, :] = largest
        stat_ref[0, 1:2, :] = jnp.sum(total * jnp.exp2((top - largest) * scale), axis=0, keepdims=True)
        top_ref[0] = m_ref[...]

    def work(new, old, masked):
        for at in range(0, keys, tile_keys):
            if new is not None:
                scores(at, *new, masked)
                index_part(at)
            if old is not None:
                exponentials(at, *old)
        if old is not None:
            finish(old[1])

    shortest = lengths[first_row]
    for r in range(1, row_count):
        shortest = jnp.minimum(shortest, lengths[first_row + r])
    clear = shortest >= start[0] + keys
    odd = lax.rem(step, 2) == 1
    inside = jnp.logical_and(step > 0, step < count)
    a, b = (s_a, m_a), (s_b, m_b)
    pl.when(step == 0)(lambda: work(a, None, True))
    for parity, new, old in ((odd, b, a), (jnp.logical_not(odd), a, b)):
        here = jnp.logical_and(inside, parity)
        pl.when(jnp.logical_and(here, clear))(functools.partial(work, new, old, False))
        pl.when(jnp.logical_and(here, jnp.logical_not(clear)))(functools.partial(work, new, old, True))
    pl.when(step == count)(lambda: work(None, a if count % 2 == 1 else b, False))


def sweep(blocks, ids, kv, idx_keys, lengths, start, buffers, row_count, head_count, idx_heads, latent, total):
    count, block_rows, width = blocks.shape
    keys = kv.shape[0]
    queries = row_count * head_count
    outs = (
        jax.ShapeDtypeStruct((total, queries, keys), jnp.int16),
        jax.ShapeDtypeStruct((total, queries, lanes), jnp.float32),
        jax.ShapeDtypeStruct((total, 2, queries), jnp.float32),
        jax.ShapeDtypeStruct((total, row_count, keys), jnp.float32),
    )

    def now(step, ids, lengths, start):
        return (ids[jnp.minimum(step, count - 1)], 0, 0)

    def before(step, ids, lengths, start):
        return (ids[jnp.maximum(step - 1, 0)], 0, 0)

    kept = len(buffers)
    kernel = functools.partial(
        sweep_kernel, row_count, head_count, idx_heads, latent, min(512, keys), count, kept
    )
    return pl.pallas_call(
        kernel,
        out_shape=outs,
        grid_spec=pltpu.PrefetchScalarGridSpec(
            num_scalar_prefetch=3,
            grid=(count + 1,),
            in_specs=[
                pl.BlockSpec((1, block_rows, width), lambda step, *_: (jnp.minimum(step, count - 1), 0, 0)),
                pl.BlockSpec(kv.shape, lambda step, *_: (0, 0), pipeline_mode=pl.Buffered(1)),
                pl.BlockSpec(idx_keys.shape, lambda step, *_: (0, 0), pipeline_mode=pl.Buffered(1)),
            ]
            + [pl.BlockSpec(memory_space=pl.ANY)] * kept,
            out_specs=[
                pl.BlockSpec((1, queries, keys), before),
                pl.BlockSpec((1, queries, lanes), before),
                pl.BlockSpec((1, 2, queries), before),
                pl.BlockSpec((1, row_count, keys), now),
            ],
            scratch_shapes=[pltpu.VMEM((queries, keys), jnp.float32)] * 2
            + [pltpu.VMEM((queries, lanes), jnp.float32)] * 2,
        ),
        input_output_aliases={6 + k: k for k in range(kept)},
        compiler_params=pltpu.CompilerParams(vmem_limit_bytes=vmem_limit),
        cost_estimate=pl.CostEstimate(
            flops=2 * count * queries * keys * 1024,
            bytes_accessed=count * queries * keys * 2,
            transcendentals=count * queries * keys,
        ),
    )(ids, lengths, start, blocks, kv, idx_keys, *buffers)


def second_kernel(row_count, head_count, scale, whole, e_ref, top_ref, att_ref, logits_ref, idx_ref, t_ref, g_ref, c_ref):
    parts, groups, queries, keys = e_ref.shape

    @pl.when(pl.program_id(1) == 0)
    def _():
        for p in range(parts):
            for g in range(groups):
                largest = jnp.transpose(jnp.broadcast_to(att_ref[0, p, 0, g : g + 1, :], (lanes, queries)))
                factor = jnp.transpose(jnp.broadcast_to(att_ref[1, p, 0, g : g + 1, :], (lanes, queries)))
                c_ref[p, g] = jnp.exp2((top_ref[p, g] - largest) * scale) * factor

    for g in range(groups):
        for r in range(row_count):
            for j in range(0, keys, lanes):
                acc = None
                for p in range(parts):
                    for q in range(r * head_count, (r + 1) * head_count, 16):
                        term = e_ref[p, g, q : q + 16, j : j + lanes].astype(jnp.float32) * c_ref[p, g, q : q + 16, :]
                        acc = term if acc is None else acc + term
                row = g * row_count + r
                t_ref[row : row + 1, j : j + lanes] = jnp.sum(acc, axis=0, keepdims=True)
    predicted = jnp.exp(logits_ref[...] - idx_ref[0, :, 0:1]) * idx_ref[1, :, 0:1]
    g_ref[...] = predicted - t_ref[...]


def second(e, top, att, logits, idx, row_count, head_count, scale):
    parts, blocks, queries, keys = e.shape
    rows = blocks * row_count
    step_rows = min(8, rows)
    groups = step_rows // row_count
    tile_keys = min(1024, keys)
    shape = jax.ShapeDtypeStruct((rows, keys), jnp.float32)
    return pl.pallas_call(
        functools.partial(second_kernel, row_count, head_count, scale, keys),
        out_shape=(shape, shape),
        grid=(rows // step_rows, keys // tile_keys),
        in_specs=[
            pl.BlockSpec((parts, groups, queries, tile_keys), lambda i, u: (0, i, 0, u)),
            pl.BlockSpec((parts, groups, queries, lanes), lambda i, u: (0, i, 0, 0)),
            pl.BlockSpec((2, parts, 1, groups, queries), lambda i, u: (0, 0, i, 0, 0)),
            pl.BlockSpec((step_rows, tile_keys), lambda i, u: (i, u)),
            pl.BlockSpec((2, step_rows, lanes), lambda i, u: (0, i, 0)),
        ],
        out_specs=[pl.BlockSpec((step_rows, tile_keys), lambda i, u: (i, u))] * 2,
        scratch_shapes=[pltpu.VMEM((parts, groups, queries, lanes), jnp.float32)],
        compiler_params=pltpu.CompilerParams(vmem_limit_bytes=vmem_limit),
        cost_estimate=pl.CostEstimate(
            flops=2 * parts * blocks * queries * keys,
            bytes_accessed=parts * blocks * queries * keys * 2,
            transcendentals=rows * keys,
        ),
    )(e, top, att.reshape(2, parts, blocks // groups, groups, queries), logits, idx)


def swap(x, bit):
    size = lax.axis_size("ctx")
    return lax.ppermute(x, "ctx", [(i, i ^ bit) for i in range(size)])


def gathered(block):
    size = lax.axis_size("ctx")
    if size != 16:
        held, far, bit = block, [0], 1
        while bit < size:
            held = jnp.concatenate([held, swap(held, bit)])
            far = far + [k ^ bit for k in far]
            bit *= 2
        return [(held, far)]
    two = swap(block, 2)
    eight = swap(block, 8)
    near = jnp.concatenate([block, two])
    four = swap(near, 4)
    ten = swap(eight, 2)
    away = jnp.concatenate([eight, ten])
    twelve = swap(away, 4)
    groups = []
    for part, far in (
        (near, [0, 2]),
        (eight, [8]),
        (jnp.concatenate([four, ten]), [4, 6, 10]),
        (twelve, [12, 14]),
    ):
        both = jnp.concatenate([part, swap(part, 1)])
        groups.append((both, far + [k ^ 1 for k in far]))
    return groups


def body(absorbed_query, index_query, index_weight, kv_cache, index_keys, lengths):
    row_count, head_count, latent = absorbed_query.shape
    idx_heads, idx_width = index_query.shape[1:]
    ctx, head = lax.axis_size("ctx"), lax.axis_size("head")
    keys = kv_cache.shape[0]
    me, plane = lax.axis_index("ctx"), lax.axis_index("head")
    start = jnp.reshape(me * keys, (1,)).astype(jnp.int32)
    per = ctx // head
    own_rows = per * row_count
    own_lengths = lax.dynamic_slice_in_dim(lengths, plane * own_rows, own_rows)

    half = idx_width // 2
    idx_flat = index_query.reshape(row_count * idx_heads, idx_width)
    idx_packed = jnp.concatenate([idx_flat[:, :half], idx_flat[:, half:]])
    query = jnp.concatenate([absorbed_query.reshape(row_count * head_count, latent), idx_packed], axis=1)
    width = latent + half
    weight = index_weight.reshape(1, row_count * idx_heads)
    weight = jnp.pad(weight, ((0, 15), (0, width - weight.shape[1])))
    block = jnp.concatenate([query, weight])[None]

    moves = []
    for c in range(ctx):
        for h in range(head):
            moves.append((c * head + h, (h * per + c % per) * head + c // per))
    block = lax.ppermute(block, ("ctx", "head"), moves)

    kv = jnp.pad(kv_cache, ((0, 0), (0, half)))
    buffers = ()
    row_lengths = jnp.concatenate([own_lengths] * head)
    for blocks, far in gathered(block):
        ids = jnp.bitwise_xor(me, jnp.array(far, jnp.int32)).astype(jnp.int32)
        buffers = sweep(
            blocks, ids, kv, index_keys, row_lengths, start, buffers, row_count, head_count, idx_heads, latent, ctx
        )
    e, top, stat, part = buffers
    queries = row_count * head_count

    key = start[0] + jnp.arange(keys, dtype=jnp.int32)
    logits = jnp.sum(part.reshape(head, own_rows, keys), axis=0) * idx_width ** (-0.5)
    logits = jnp.where(key[None, :] < own_lengths[:, None], logits, -jnp.inf)
    idx_max = jnp.maximum(jnp.max(logits, axis=-1), far_below)
    idx_total = jnp.sum(jnp.exp(logits - idx_max[:, None]), axis=-1)

    largest = jnp.concatenate([stat[:, 0, :].reshape(-1) * attention_scale, idx_max])
    total = jnp.concatenate([stat[:, 1, :].reshape(-1), idx_total])
    state = jnp.stack([largest, total])
    bit = 1
    while bit < ctx:
        other = swap(state, bit)
        top_two = jnp.maximum(state[0], other[0])
        merged = state[1] * jnp.exp(state[0] - top_two) + other[1] * jnp.exp(other[0] - top_two)
        state = jnp.stack([top_two, merged])
        bit *= 2
    whole = float(keys * ctx)
    factor = whole / (levels * head * head_count)
    att = jnp.stack([state[0, : ctx * queries] * (1.0 / attention_scale), factor / state[1, : ctx * queries]])
    att = att.reshape(2, head, per, queries)
    idx = jnp.stack([state[0, ctx * queries :], whole / state[1, ctx * queries :]])
    idx = jnp.broadcast_to(idx[:, :, None], idx.shape + (lanes,))
    shape = (head, per, queries)
    return second(
        e.reshape(shape + (keys,)),
        top.reshape(shape + (lanes,)),
        att,
        logits,
        idx,
        row_count,
        head_count,
        attention_scale * log2_e,
    )


def solution(mesh):
    return jax.shard_map(
        body,
        mesh=mesh,
        in_specs=(
            P("ctx", "head", None),
            P("ctx", "head", None),
            P("ctx", "head"),
            P("ctx", None),
            P("ctx", None),
            P(),
        ),
        out_specs=(P("head", "ctx"), P("head", "ctx")),
        check_vma=False,
    )
```

time: 515 us -> 189 us (0.37)
  blocking collectives: 114 us -> 0 us
  other arithmetic: 122 us -> 12.4 us
  local copies, waits for them, and re-layouts: 127 us -> 18.6 us
  Pallas kernels: 0 us -> 100 us
  matrix products: 98.5 us -> 0 us
  starting transfers between devices: 0.12 us -> 37 us
  waiting for transfers between devices: 36.6 us -> 16.1 us
  between operations: 14.5 us -> 1.14 us
    pallas_call x0 -> x5, Pallas kernels: none -> 100 us  [the longest x4 79.1 us: sweep(): pl.pallas_call(kernel, out_shape=outs, grid_spec=pltpu.PrefetchScalarGrid...]
    dot_general x12 -> x0, matrix products: 98.5 us -> none  [the longest x4 53.1 us: block_scores(): jnp.einsum('qd,kd->qk', flat_query, cached, preferred_element_type=jnp.fl...]
    all_gather x4 -> x0, blocking collectives: 83 us -> none  [the longest x2 39.4 us: merged(): gathered = jax.tree.map(lambda a: lax.all_gather(a, axis), part)]
    mul x4 -> x0, local copies, waits for them, and re-layouts: 69.8 us -> none  [block_scores(): jnp.einsum('qd,kd->qk', flat_query, cached, preferred_element_type=jnp.fl...]
    reduce_sum x5 -> x1, other arithmetic: 65.8 us -> 0.1 us  [body(): jnp.sum(part.reshape(head, own_rows, keys), axis=0) * idx_width ** (-0.5)]
    broadcast_in_dim x10 -> x1, local copies, waits for them, and re-layouts: 53.9 us -> 0.69 us  [body(): idx = jnp.broadcast_to(idx[:, :, None], idx.shape + (lanes,))]
    dynamic_update_slice x8 -> x0, other arithmetic: 49.7 us -> none  [the longest x4 49.5 us: advance(): lax.dynamic_update_slice_in_dim(kept, scores, block_index * block_keys, 2)]
    ppermute x0 -> x14, starting transfers between devices: none -> 37 us  [the longest x13 36.3 us: swap(): return lax.ppermute(x, 'ctx', [(i, i ^ bit) for i in range(size)])]
  transfers between devices with their start and end apart: 3 -> 14, of which waited for: 2 -> 5; matrix products, arithmetic and copies ran while one was open for 0% -> 12% of each run, Pallas kernels for 0% -> 32%
where the time goes in v1:
time: 189 us; the launch traced here: 186 us
  Pallas kernels  100 us (53%)
  starting transfers between devices  37 us (20%)
  local copies, waits for them, and re-layouts  18.6 us (10%)
  waiting for transfers between devices  16.1 us (9%)
  other arithmetic  12.4 us (7%)
    pallas_call x4, Pallas kernels, sweep(): pl.pallas_call(kernel, out_shape=outs, grid_spec=pltpu.PrefetchScalarGrid...  79.1 us
    ppermute x13, starting transfers between devices, swap(): return lax.ppermute(x, 'ctx', [(i, i ^ bit) for i in range(size)])  36.3 us
    pallas_call x1, Pallas kernels, second(): pl.pallas_call(functools.partial(second_kernel, row_count, head_count, sc...  21.2 us
    ppermute x13, waiting for transfers between devices, swap(): return lax.ppermute(x, 'ctx', [(i, i ^ bit) for i in range(size)])  16.1 us
    unnamed x12, local copies, waits for them, and re-layouts  8.42 us
    pad x1, local copies, waits for them, and re-layouts, body(): kv = jnp.pad(kv_cache, ((0, 0), (0, half)))  5.36 us
    concatenate x4, other arithmetic, gathered(): both = jnp.concatenate([part, swap(part, 1)])  5.24 us
  transfers between devices with their start and end apart: 14, of which 5 were waited for; matrix products, arithmetic and copies ran while one was open for 12% of the time, Pallas kernels for 32%

profile of v1, /device:TPU:0, one launch (start us, length us, event | category | flops | bytes accessed | tf_op | source)
XLA Modules:
  0.0 185.6 jit_solution(3283598262713849801)
XLA Ops:
  0.7 0.9 fusion.11
  1.6 0.8 reshape.85
  2.3 1.1 fusion.2
  3.4 0.7 collective-permute-start
  4.1 3.0 %collective-permute-start.5 = (bf16[1,272,640]{2,1,0:T(8,128)(2,1)S(1)}, bf16[1,272,640]{2,1,0:T(8,128)(2,1)S(1)}, u32[]{:S(2)}, u32[]{:S(2)}) collective-permute-start(bf16[1,272,640]{2,1,0:T(8,128)(2,1)S(1)} %collective-permute-done), channel_id=1, source_target_pairs={{0,4},{2,6},{4,0},{6,2},{8,12},{10,14},{12,8},{14,10},{16,20},{18,... | collective-permute-start | bytes 1044488 | tf_op jit(solution)/shard_map/ppermute | solution.py:219
  7.1 1.2 broadcast_xor_fusion.2.ids
  8.3 1.2 broadcast_xor_fusion.ids
  9.5 19.9 %collective-permute-start.1 = (bf16[1,272,640]{2,1,0:T(8,128)(2,1)S(1)}, bf16[1,272,640]{2,1,0:T(8,128)(2,1)S(1)}, u32[]{:S(2)}, u32[]{:S(2)}) collective-permute-start(bf16[1,272,640]{2,1,0:T(8,128)(2,1)S(1)} %collective-permute-done), channel_id=1, source_target_pairs={{0,16},{2,18},{4,20},{6,22},{8,24},{10,26},{12,28},{14,30},{16,0},... | collective-permute-start | bytes 1044488 | tf_op jit(solution)/shard_map/ppermute | solution.py:219
  29.4 0.8 constant_dynamic-update-slice_fusion.1
  30.2 0.8 constant_dynamic-update-slice_fusion
  30.9 4.5 %collective-permute-start.6 = (bf16[2,272,640]{2,1,0:T(8,128)(2,1)}, bf16[2,272,640]{2,1,0:T(8,128)(2,1)S(1)}, u32[]{:S(2)}, u32[]{:S(2)}) collective-permute-start(bf16[2,272,640]{2,1,0:T(8,128)(2,1)} %constant_dynamic-update-slice_fusion), channel_id=1, source_target_pairs={{0,8},{2,10},{4,12},{6,14},{8,0},{10,2},{12,4},{14,6},{16,24},{18,... | collective-permute-start | bytes 2088968 | tf_op jit(solution)/shard_map/ppermute | solution.py:219
  36.0 7.9 %collective-permute-done.1 = bf16[1,272,640]{2,1,0:T(8,128)(2,1)S(1)} collective-permute-done((bf16[1,272,640]{2,1,0:T(8,128)(2,1)S(1)}, bf16[1,272,640]{2,1,0:T(8,128)(2,1)S(1)}, u32[]{:S(2)}, u32[]{:S(2)}) %collective-permute-start.1) | collective-permute-done | bytes 348192 | tf_op jit(solution)/shard_map/ppermute | solution.py:219
  45.2 7.6 %copy.24 = bf16[4096,576]{1,0:T(8,128)(2,1)} copy(bf16[4096,576]{0,1:T(8,128)(2,1)} %param.13) | data formatting | bytes 9437184 | tf_op args[3]
  52.8 5.4 %pad.9.kv_ref = bf16[4096,640]{1,0:T(8,128)(2,1)} pad(bf16[4096,576]{1,0:T(8,128)(2,1)} %copy.24, bf16[]{:T(256)} %constant.14.clone.1), padding=0_0x0_64 | pad | bytes 9961474 | tf_op jit(solution)/shard_map/jit(_pad)/pad | solution.py:276
  58.7 1.0 pad_maximum_fusion.4
  60.8 1.3 pad_maximum_fusion.2.q_ref
  62.1 19.7 %shard_map.113 = (s16[16,256,4096]{2,1,0:T(8,128)(2,1)}, f32[16,256,128]{2,1,0:T(8,128)}, f32[16,2,256]{2,1,0:T(2,128)}, f32[16,4,4096]{2,1,0:T(4,128)}) custom-call(s32[4]{0:T(128)} %broadcast_xor_fusion.2.ids, s32[64]{0:T(128)} %pad_add_fusion.lengths, s32[1]{0:T(128)} %bitcast.start, bf16[4,272,640]{2,1,0:T(8,128)(2,1)} %pad_maximum_fusion.2.q_ref, ...), custom_call_target="tpu_custom_call" | custom-call | flops 8589934592 | bytes 8388608 | tf_op jit(solution)/shard_map/pallas_call | solution.py:132
  81.8 12.8 %shard_map.114 = (s16[16,256,4096]{2,1,0:T(8,128)(2,1)}, f32[16,256,128]{2,1,0:T(8,128)}, f32[16,2,256]{2,1,0:T(2,128)}, f32[16,4,4096]{2,1,0:T(4,128)}) custom-call(s32[2]{0:T(128)} %broadcast_xor_fusion.ids, s32[64]{0:T(128)} %pad_add_fusion.lengths, s32[1]{0:T(128)} %bitcast.start, ...), custom_call_target="tpu_custom_call", output_to_operand_aliasing={{0}: (6, {}), {1}: (7, {}), {2}: (8, {}), {3}: (9, {})} | custom-call | flops 4294967296 | bytes 4194304 | tf_op jit(solution)/shard_map/pallas_call | solution.py:132
  95.0 1.6 pad_maximum_fusion.q_ref
  96.6 26.7 %shard_map.115 = (s16[16,256,4096]{2,1,0:T(8,128)(2,1)}, f32[16,256,128]{2,1,0:T(8,128)}, f32[16,2,256]{2,1,0:T(2,128)}, f32[16,4,4096]{2,1,0:T(4,128)}) custom-call(s32[6]{0:T(128)} %broadcast_xor_fusion.1.ids, s32[64]{0:T(128)} %pad_add_fusion.lengths, s32[1]{0:T(128)} %bitcast.start, ...), custom_call_target="tpu_custom_call", output_to_operand_aliasing={{0}: (6, {}), {1}: (7, {}), {2}: (8, {}), {3}: (9, {})} | custom-call | flops 12884901888 | bytes 12582912 | tf_op jit(solution)/shard_map/pallas_call | solution.py:132
  123.3 1.3 pad_maximum_fusion.1.q_ref
  124.6 19.9 %shard_map.116 = (s16[16,256,4096]{2,1,0:T(8,128)(2,1)}, f32[16,256,128]{2,1,0:T(8,128)}, f32[16,2,256]{2,1,0:T(2,128)}, f32[16,4,4096]{2,1,0:T(4,128)}) custom-call(s32[4]{0:T(128)} %broadcast_xor_fusion.3.ids, s32[64]{0:T(128)} %pad_add_fusion.lengths, s32[1]{0:T(128)} %bitcast.start, ...), custom_call_target="tpu_custom_call", output_to_operand_aliasing={{0}: (6, {}), {1}: (7, {}), {2}: (8, {}), {3}: (9, {})} | custom-call | flops 8589934592 | bytes 8388608 | tf_op jit(solution)/shard_map/pallas_call | solution.py:132
  144.5 1.6 reshape.88
  147.2 1.0 collective-permute-done.10
  148.3 1.5 collective-permute-start.11
  149.8 2.5 %collective-permute-done.11 = f32[2,4128]{1,0:T(2,128)S(1)} collective-permute-done((f32[2,4128]{1,0:T(2,128)S(1)}, f32[2,4128]{1,0:T(2,128)S(1)}, u32[]{:S(2)}, u32[]{:S(2)}) %collective-permute-start.11) | collective-permute-done | bytes 33056 | tf_op jit(solution)/shard_map/ppermute | solution.py:219
  152.4 1.5 collective-permute-start.12
  153.9 2.4 %collective-permute-done.12 = f32[2,4128]{1,0:T(2,128)S(1)} collective-permute-done((f32[2,4128]{1,0:T(2,128)S(1)}, f32[2,4128]{1,0:T(2,128)S(1)}, u32[]{:S(2)}, u32[]{:S(2)}) %collective-permute-start.12) | collective-permute-done | bytes 33056 | tf_op jit(solution)/shard_map/ppermute | solution.py:219
  156.5 3.8 %collective-permute-start.13 = (f32[2,4128]{1,0:T(2,128)S(1)}, f32[2,4128]{1,0:T(2,128)S(1)}, u32[]{:S(2)}, u32[]{:S(2)}) collective-permute-start(f32[2,4128]{1,0:T(2,128)S(1)} %pad_maximum_fusion.9), channel_id=1, source_target_pairs={{0,16},{2,18},{4,20},{6,22},{8,24},{10,26},{12,28},{14,30},{16,0},... | collective-permute-start | bytes 99080 | tf_op jit(solution)/shard_map/ppermute | solution.py:219
  160.3 2.3 %collective-permute-done.13 = f32[2,4128]{1,0:T(2,128)S(1)} collective-permute-done((f32[2,4128]{1,0:T(2,128)S(1)}, f32[2,4128]{1,0:T(2,128)S(1)}, u32[]{:S(2)}, u32[]{:S(2)}) %collective-permute-start.13) | collective-permute-done | bytes 33056 | tf_op jit(solution)/shard_map/ppermute | solution.py:219
  163.4 0.7 broadcast_in_dim.18.idx_ref
  164.1 21.2 %shard_map.117 = (f32[32,4096]{1,0:T(8,128)}, f32[32,4096]{1,0:T(8,128)}) custom-call(s16[2,8,256,4096]{3,2,1,0:T(8,128)(2,1)} %bitcast.14, f32[2,8,256,128]{3,2,1,0:T(8,128)} %bitcast.15, f32[2,2,4,2,256]{4,3,2,1,0:T(2,128)} %pad_maximum_fusion.10.att_ref, f32[32,4096]{1,0:T(8,128)} %copy-done, f32[2,32,128]{2,1,0:T(8,128)} %broadcast_in_dim.18.idx_ref), custom_call_target="tpu_custom_call" | custom-call | flops 33554432 | bytes 33554432 | tf_op jit(solution)/shard_map/pallas_call | solution.py:195
  (56 shorter events, 6.0 us)
Async XLA Ops:
  0.6 34.7 %copy-start.4 = (s32[6]{0:T(128)S(1)}, s32[6]{0:T(128)}, u32[]{:S(2)}) copy-start(s32[6]{0:T(128)} %constant.44.clone) | copy-start | bytes 76
  0.6 35.3 %copy-start.2 = (s32[64]{0:T(128)S(1)}, s32[64]{0:T(128)}, u32[]{:S(2)}) copy-start(s32[64]{0:T(128)} %param.15) | copy-start | bytes 772
  3.4 0.7 collective-permute-start
  4.1 26.0 %collective-permute-start.5 = (bf16[1,272,640]{2,1,0:T(8,128)(2,1)S(1)}, bf16[1,272,640]{2,1,0:T(8,128)(2,1)S(1)}, u32[]{:S(2)}, u32[]{:S(2)}) collective-permute-start(bf16[1,272,640]{2,1,0:T(8,128)(2,1)S(1)} %collective-permute-done), channel_id=1, source_target_pairs={{0,4},{2,6},{4,0},{6,2},{8,12},{10,14},{12,8},{14,10},{16,20},{18,... | collective-permute-start | bytes 1044488 | tf_op jit(solution)/shard_map/ppermute | solution.py:219
  9.5 34.5 %collective-permute-start.1 = (bf16[1,272,640]{2,1,0:T(8,128)(2,1)S(1)}, bf16[1,272,640]{2,1,0:T(8,128)(2,1)S(1)}, u32[]{:S(2)}, u32[]{:S(2)}) collective-permute-start(bf16[1,272,640]{2,1,0:T(8,128)(2,1)S(1)} %collective-permute-done), channel_id=1, source_target_pairs={{0,16},{2,18},{4,20},{6,22},{8,24},{10,26},{12,28},{14,30},{16,0},... | collective-permute-start | bytes 1044488 | tf_op jit(solution)/shard_map/ppermute | solution.py:219
  30.9 29.4 %collective-permute-start.6 = (bf16[2,272,640]{2,1,0:T(8,128)(2,1)}, bf16[2,272,640]{2,1,0:T(8,128)(2,1)S(1)}, u32[]{:S(2)}, u32[]{:S(2)}) collective-permute-start(bf16[2,272,640]{2,1,0:T(8,128)(2,1)} %constant_dynamic-update-slice_fusion), channel_id=1, source_target_pairs={{0,8},{2,10},{4,12},{6,14},{8,0},{10,2},{12,4},{14,6},{16,24},{18,... | collective-permute-start | bytes 2088968 | tf_op jit(solution)/shard_map/ppermute | solution.py:219
  36.0 24.7 %collective-permute-start.9 = (bf16[2,272,640]{2,1,0:T(8,128)(2,1)}, bf16[2,272,640]{2,1,0:T(8,128)(2,1)S(1)}, u32[]{:S(2)}, u32[]{:S(2)}) collective-permute-start(bf16[2,272,640]{2,1,0:T(8,128)(2,1)} %constant_dynamic-update-slice_fusion), channel_id=1, source_target_pairs={{0,2},{2,0},{4,6},{6,4},{8,10},{10,8},{12,14},{14,12},{16,18},{18,... | collective-permute-start | bytes 2088968 | tf_op jit(solution)/shard_map/ppermute | solution.py:219
  44.0 14.7 %collective-permute-start.2 = (bf16[1,272,640]{2,1,0:T(8,128)(2,1)S(1)}, bf16[1,272,640]{2,1,0:T(8,128)(2,1)S(1)}, u32[]{:S(2)}, u32[]{:S(2)}) collective-permute-start(bf16[1,272,640]{2,1,0:T(8,128)(2,1)S(1)} %collective-permute-done.1), channel_id=1, source_target_pairs={{0,4},{2,6},{4,0},{6,2},{8,12},{10,14},{12,8},{14,10},{16,20},{18,... | collective-permute-start | bytes 1044488 | tf_op jit(solution)/shard_map/ppermute | solution.py:219
  44.5 14.2 %collective-permute-start.8 = (bf16[1,272,640]{2,1,0:T(8,128)(2,1)S(1)}, bf16[1,272,640]{2,1,0:T(8,128)(2,1)S(1)}, u32[]{:S(2)}, u32[]{:S(2)}) collective-permute-start(bf16[1,272,640]{2,1,0:T(8,128)(2,1)S(1)} %collective-permute-done.1), channel_id=1, source_target_pairs={{0,2},{2,0},{4,6},{6,4},{8,10},{10,8},{12,14},{14,12},{16,18},{18,... | collective-permute-start | bytes 1044488 | tf_op jit(solution)/shard_map/ppermute | solution.py:219
  52.8 5.4 %copy-start.3 = (s32[4]{0:T(128)S(1)}, s32[4]{0:T(128)}, u32[]{:S(2)}) copy-start(s32[4]{0:T(128)} %constant.45.clone) | copy-start | bytes 52
  59.7 34.9 %collective-permute-start.3 = (bf16[2,272,640]{2,1,0:T(8,128)(2,1)S(1)}, bf16[2,272,640]{2,1,0:T(8,128)(2,1)S(1)}, u32[]{:S(2)}, u32[]{:S(2)}) collective-permute-start(bf16[2,272,640]{2,1,0:T(8,128)(2,1)S(1)} %get-tuple-element.43), channel_id=1, source_target_pairs={{0,8},{2,10},{4,12},{6,14},{8,0},{10,2},{12,4},{14,6},{16,24},{18,... | collective-permute-start | bytes 2088968 | tf_op jit(solution)/shard_map/ppermute | solution.py:219
  60.5 34.5 %collective-permute-start.7 = (bf16[3,272,640]{2,1,0:T(8,128)(2,1)S(1)}, bf16[3,272,640]{2,1,0:T(8,128)(2,1)S(1)}, u32[]{:S(2)}, u32[]{:S(2)}) collective-permute-start(bf16[3,272,640]{2,1,0:T(8,128)(2,1)S(1)} %pad_maximum_fusion.3), channel_id=1, source_target_pairs={{0,2},{2,0},{4,6},{6,4},{8,10},{10,8},{12,14},{14,12},{16,18},{18,... | collective-permute-start | bytes 3133448 | tf_op jit(solution)/shard_map/ppermute | solution.py:219
  94.6 28.7 %collective-permute-start.4 = (bf16[2,272,640]{2,1,0:T(8,128)(2,1)S(1)}, bf16[2,272,640]{2,1,0:T(8,128)(2,1)S(1)}, u32[]{:S(2)}, u32[]{:S(2)}) collective-permute-start(bf16[2,272,640]{2,1,0:T(8,128)(2,1)S(1)} %collective-permute-done.3), channel_id=1, source_target_pairs={{0,2},{2,0},{4,6},{6,4},{8,10},{10,8},{12,14},{14,12},{16,18},{18,... | collective-permute-start | bytes 2088968 | tf_op jit(solution)/shard_map/ppermute | solution.py:219
  144.5 2.0 %copy-start.1 = (f32[16,2,256]{2,1,0:T(2,128)S(1)}, f32[16,2,256]{2,1,0:T(2,128)}, u32[]{:S(2)}) copy-start(f32[16,2,256]{2,1,0:T(2,128)} %get-tuple-element.32) | copy-start | bytes 98308
  146.5 17.7 %copy-start = (f32[32,4096]{1,0:T(8,128)}, f32[32,4096]{1,0:T(8,128)S(1)}, u32[]{:S(2)}) copy-start(f32[32,4096]{1,0:T(8,128)S(1)} %get-tuple-element.41.logits_ref) | copy-start | bytes 1572868
  146.9 1.3 collective-permute-start.10
  148.3 4.0 %collective-permute-start.11 = (f32[2,4128]{1,0:T(2,128)S(1)}, f32[2,4128]{1,0:T(2,128)S(1)}, u32[]{:S(2)}, u32[]{:S(2)}) collective-permute-start(f32[2,4128]{1,0:T(2,128)S(1)} %pad_maximum_fusion.7), channel_id=1, source_target_pairs={{0,4},{2,6},{4,0},{6,2},{8,12},{10,14},{12,8},{14,10},{16,20},{18,... | collective-permute-start | bytes 99080 | tf_op jit(solution)/shard_map/ppermute | solution.py:219
  152.4 4.0 %collective-permute-start.12 = (f32[2,4128]{1,0:T(2,128)S(1)}, f32[2,4128]{1,0:T(2,128)S(1)}, u32[]{:S(2)}, u32[]{:S(2)}) collective-permute-start(f32[2,4128]{1,0:T(2,128)S(1)} %pad_maximum_fusion.8), channel_id=1, source_target_pairs={{0,8},{2,10},{4,12},{6,14},{8,0},{10,2},{12,4},{14,6},{16,24},{18,... | collective-permute-start | bytes 99080 | tf_op jit(solution)/shard_map/ppermute | solution.py:219
  156.5 6.1 %collective-permute-start.13 = (f32[2,4128]{1,0:T(2,128)S(1)}, f32[2,4128]{1,0:T(2,128)S(1)}, u32[]{:S(2)}, u32[]{:S(2)}) collective-permute-start(f32[2,4128]{1,0:T(2,128)S(1)} %pad_maximum_fusion.9), channel_id=1, source_target_pairs={{0,16},{2,18},{4,20},{6,22},{8,24},{10,26},{12,28},{14,30},{16,0},... | collective-permute-start | bytes 99080 | tf_op jit(solution)/shard_map/ppermute | solution.py:219

commit v2 on v0

v2 whole, which is shorter than its diff:
```python
import functools

import jax
import jax.numpy as jnp
from jax import lax
from jax.experimental import pallas as pl
from jax.experimental.pallas import tpu as pltpu
from jax.sharding import PartitionSpec as P

attention_scale = 192.0 ** (-0.5)
log2_e = 1.4426950408889634
far_below = -1e30
levels = 32767.0
lanes = 128
vmem_limit = 20 * 2**20
second_vmem = 57 * 2**20


def sweep_kernel(row_count, head_count, idx_heads, latent, spans, sizes, resident, info, kv_ref, ik_ref, *rest):
    sources, rest = rest[: len(sizes)], rest[len(sizes) :]
    e_ref, e_last, top_ref, top_last, stat_ref, part_ref, done_ref, *rest = rest
    s_a, s_b, m_a, m_b, run_m, run_t, turn_m, turn_t, q_slots, q_sems = rest
    count = sum(sizes)
    step = pl.program_id(0)
    queries = row_count * head_count
    keys = kv_ref.shape[1]
    span = keys // spans
    idx_queries = row_count * idx_heads
    scale = attention_scale * log2_e
    start = info[0]
    place = info[1 + jnp.minimum(step, count - 1)]
    before = info[1 + jnp.maximum(step - 1, 0)]
    first_row = 1 + count + place * row_count
    pairs = ((s_a, m_a), (s_b, m_b))

    def scores(u, masked):
        s_ref, m_ref = pairs[u % 2]
        for at in range(0, span, min(512, span)):
            size = min(512, span)
            y = jnp.dot(
                q_ref[:queries, :latent],
                kv_ref[:, u * span + at : u * span + at + size],
                preferred_element_type=jnp.float32,
            )
            if masked:
                key = lax.broadcasted_iota(jnp.int32, (head_count, size), 1) + (start + u * span + at)
                pieces = []
                for r in range(row_count):
                    piece = y[r * head_count : (r + 1) * head_count]
                    pieces.append(jnp.where(key < info[first_row + r], piece, -jnp.inf))
                y = jnp.concatenate(pieces, axis=0)
            s_ref[:, at : at + size] = y
            top = y[:, :lanes]
            for j in range(lanes, size, lanes):
                top = jnp.maximum(top, y[:, j : j + lanes])
            m_ref[...] = jnp.maximum(top, far_below if at == 0 else m_ref[...])

    def index_part(u):
        packed = q_ref[: 2 * idx_queries, latent:]
        idx_query = jnp.concatenate([packed[:idx_queries], packed[idx_queries:]], axis=1)
        weight = q_ref[queries : queries + 8, :lanes].astype(jnp.float32)[0:1]
        weight = jnp.transpose(jnp.broadcast_to(weight, (lanes, lanes)))[:idx_queries]
        for at in range(u * span, (u + 1) * span, min(256, span)):
            size = min(256, span)
            inner = lax.dot_general(
                idx_query, ik_ref[at : at + size, :], (((1,), (1,)), ((), ())), preferred_element_type=jnp.float32
            )
            for j in range(0, size, lanes):
                product = jnp.maximum(inner[:, j : j + lanes], 0.0) * weight
                product = jnp.sum(product.reshape(row_count, idx_heads, lanes), axis=1)
                part_ref[0, :, at + j : at + j + lanes] = product

    def exponentials(u, where):
        s_ref, m_ref = pairs[u % 2]
        if resident:
            out, top_out, shift, column = e_ref.at[where], top_ref.at[where], u * span, u * lanes
        elif u < spans - 1:
            out, top_out, shift, column = e_ref.at[0], top_ref.at[0], u * span, u * lanes
        else:
            out, top_out, shift, column = e_last.at[0], top_last.at[0], 0, 0
        for q in range(0, queries, 16):
            top = m_ref[q : q + 16, :]
            total = None
            for j in range(0, span, lanes):
                e = jnp.exp2((s_ref[q : q + 16, j : j + lanes] - top) * scale)
                total = e if total is None else total + e
                out[q : q + 16, shift + j : shift + j + lanes] = jnp.round(e * levels).astype(jnp.int32).astype(jnp.int16)
            top_out[q : q + 16, column : column + lanes] = top
            if u == 0:
                run_m[q : q + 16, :] = top
                run_t[q : q + 16, :] = total
            else:
                held = run_m[q : q + 16, :]
                larger = jnp.maximum(held, top)
                run_m[q : q + 16, :] = larger
                run_t[q : q + 16, :] = run_t[q : q + 16, :] * jnp.exp2((held - larger) * scale) + total * jnp.exp2(
                    (top - larger) * scale
                )

    def turn():
        turn_m[...] = jnp.transpose(run_m[...])
        turn_t[...] = jnp.transpose(run_t[...])

    def finish():
        top = turn_m[...]
        largest = jnp.max(top, axis=0, keepdims=True)
        stat_ref[0, 0:1, :] = largest
        stat_ref[0, 1:2, :] = jnp.sum(turn_t[...] * jnp.exp2((top - largest) * scale), axis=0, keepdims=True)

    def work(masked):
        scores(0, masked)
        index_part(0)
        exponentials(spans - 1, before)
        for u in range(1, spans):
            scores(u, masked)
            if u == 1:
                turn()
            if u == 2:
                finish()
            index_part(u)
            exponentials(u - 1, place)

    def last():
        exponentials(spans - 1, before)
        turn()
        finish()
        done_ref[0] = 0

    shortest = info[first_row]
    for r in range(1, row_count):
        shortest = jnp.minimum(shortest, info[first_row + r])
    clear = shortest >= start + keys
    inside = step < count
    slot = lax.rem(step, 2)
    q_ref = q_slots.at[slot]

    def query_copy(tile, act):
        passed = 0
        for source, size in zip(sources, sizes):

            @pl.when(jnp.logical_and(tile >= passed, tile < passed + size))
            def _(source=source, passed=passed):
                into = lax.rem(tile, 2)
                act(pltpu.make_async_copy(source.at[tile - passed], q_slots.at[into], q_sems.at[into]))

            passed += size

    pl.when(step == 0)(lambda: query_copy(step, lambda copy: copy.start()))
    query_copy(step, lambda copy: copy.wait())
    query_copy(step + 1, lambda copy: copy.start())
    pl.when(jnp.logical_and(inside, clear))(lambda: work(False))
    pl.when(jnp.logical_and(inside, jnp.logical_not(clear)))(lambda: work(True))
    pl.when(step == count)(last)


def sweep(blocks, info, kv, idx_keys, resident, row_count, head_count, idx_heads, latent):
    sizes = [a.shape[0] for a in blocks]
    count = sum(sizes)
    block_rows, width = blocks[0].shape[1:]
    keys = kv.shape[1]
    queries = row_count * head_count
    spans = 4
    span = keys // spans
    kept, tops = (span, lanes) if not resident else (0, 0)
    space = pltpu.VMEM if resident else pltpu.HBM
    outs = (
        space((count, queries, keys - kept), jnp.int16),
        pltpu.HBM((count, queries, span) if kept else (1, 16, lanes), jnp.int16),
        space((count, queries, spans * lanes - tops), jnp.float32),
        pltpu.HBM((count, queries, lanes) if kept else (1, 8, lanes), jnp.float32),
        pltpu.HBM((count, 2, queries), jnp.float32),
        pltpu.HBM((count, row_count, keys), jnp.float32),
        jax.ShapeDtypeStruct((1,), jnp.int32),
    )

    def now(step, info):
        return (info[1 + jnp.minimum(step, count - 1)], 0, 0)

    def before(step, info):
        return (info[1 + jnp.maximum(step - 1, 0)], 0, 0)

    kernel = functools.partial(sweep_kernel, row_count, head_count, idx_heads, latent, spans, sizes, resident)
    whole = pl.BlockSpec(memory_space=pltpu.VMEM)
    unused = pl.BlockSpec(memory_space=pl.ANY)
    return pl.pallas_call(
        kernel,
        out_shape=outs,
        grid_spec=pltpu.PrefetchScalarGridSpec(
            num_scalar_prefetch=1,
            grid=(count + 1,),
            in_specs=[whole, whole] + [pl.BlockSpec(memory_space=pltpu.HBM)] * len(blocks),
            out_specs=[
                whole if resident else pl.BlockSpec((1, queries, keys - span), now),
                unused if resident else pl.BlockSpec((1, queries, span), before),
                whole if resident else pl.BlockSpec((1, queries, (spans - 1) * lanes), now),
                unused if resident else pl.BlockSpec((1, queries, lanes), before),
                pl.BlockSpec((1, 2, queries), before),
                pl.BlockSpec((1, row_count, keys), now),
                pl.BlockSpec(memory_space=pltpu.SMEM),
            ],
            scratch_shapes=[pltpu.VMEM((queries, span), jnp.float32)] * 2
            + [pltpu.VMEM((queries, lanes), jnp.float32)] * 4
            + [pltpu.VMEM((lanes, queries), jnp.float32)] * 2
            + [pltpu.VMEM((2, block_rows, width), jnp.bfloat16), pltpu.SemaphoreType.DMA((2,))],
        ),
        compiler_params=pltpu.CompilerParams(vmem_limit_bytes=vmem_limit),
        cost_estimate=pl.CostEstimate(
            flops=2 * count * queries * keys * 1024,
            bytes_accessed=count * queries * keys * 2,
            transcendentals=count * queries * keys,
        ),
    )(info, kv, idx_keys, *blocks)


def second_kernel(row_count, head_count, scale, spans, per, layout, *refs):
    sets = []
    for parts, resident in layout:
        sets.append((parts, resident, refs[: 2 if resident else 4]))
        refs = refs[2 if resident else 4 :]
    att_ref, logits_ref, idx_ref, t_ref, g_ref, c_ref, turn_ref, sum_ref = refs
    queries = c_ref.shape[2]
    keys = t_ref.shape[1]
    span = keys // spans
    groups = t_ref.shape[0] // row_count
    group = pl.program_id(1)
    first = pl.program_id(0) * groups + group

    members = []
    for parts, resident, arrays in sets:
        for p in range(parts):
            index = len(members)
            if resident:

                def take(u, p=p, arrays=arrays):
                    e, top = arrays
                    return e.at[p * per + first], u * span, top[p * per + first, :, u * lanes : (u + 1) * lanes]

            else:

                def take(u, p=p, arrays=arrays):
                    e, e_last, top, top_last = arrays
                    if u < spans - 1:
                        return e.at[p, 0], u * span, top[p, 0, :, u * lanes : (u + 1) * lanes]
                    return e_last.at[p, 0], 0, top_last[p, 0]

            members.append((index * per + first, take))

    for p, (place, _) in enumerate(members):
        turn_ref[0, p] = jnp.transpose(jnp.broadcast_to(att_ref[0, place], (lanes, queries)))
        turn_ref[1, p] = jnp.transpose(jnp.broadcast_to(att_ref[1, place], (lanes, queries)))

    def factors(u):
        for p, (_, take) in enumerate(members):
            c_ref[u, p] = jnp.exp2((take(u)[2] - turn_ref[0, p]) * scale) * turn_ref[1, p]

    factors(0)
    for u in range(spans):
        if u + 1 < spans:
            factors(u + 1)
        for r in range(row_count):
            acc = [None] * (span // lanes)
            for p, (_, take) in enumerate(members):
                source, shift, _ = take(u)
                for q in range(r * head_count, (r + 1) * head_count, 16):
                    c = c_ref[u, p, q : q + 16, :]
                    for k in range(len(acc)):
                        at = shift + k * lanes
                        term = source[q : q + 16, at : at + lanes].astype(jnp.float32) * c
                        term = term[:8] + term[8:]
                        acc[k] = term if acc[k] is None else acc[k] + term
            for k in range(len(acc)):
                at = u * span + k * lanes
                sum_ref[group, r : r + 1, at : at + lanes] = jnp.sum(acc[k], axis=0, keepdims=True)

    @pl.when(group == groups - 1)
    def _():
        target = jnp.concatenate([sum_ref[g] for g in range(groups)], axis=0)
        predicted = jnp.exp(logits_ref[...] - idx_ref[0, :, 0:1]) * idx_ref[1, :, 0:1]
        t_ref[...] = target
        g_ref[...] = predicted - target


def second(sets, att, logits, idx, row_count, head_count, scale):
    rows, keys = logits.shape
    queries = row_count * head_count
    spans = 4
    span = keys // spans
    per = rows // row_count
    step_rows = min(8, rows)
    groups = step_rows // row_count
    shape = jax.ShapeDtypeStruct((rows, keys), jnp.float32)
    whole = pl.BlockSpec(memory_space=pltpu.VMEM)

    def mine(i, g):
        return (0, i * groups + g, 0, 0)

    operands, specs, total = [], [], 0
    for (e, e_last, top, top_last), parts, resident in sets:
        total += parts
        if resident:
            operands += [e, top]
            specs += [whole, whole]
        else:
            for a in (e, e_last, top, top_last):
                operands.append(a.reshape((parts, per) + a.shape[1:]))
                specs.append(pl.BlockSpec((parts, 1) + a.shape[1:], mine))
    return pl.pallas_call(
        functools.partial(
            second_kernel, row_count, head_count, scale, spans, per, [(parts, resident) for _, parts, resident in sets]
        ),
        out_shape=(shape, shape),
        grid=(rows // step_rows, groups),
        in_specs=specs
        + [
            pl.BlockSpec((2, total * per, 1, queries), lambda i, g: (0, 0, 0, 0)),
            pl.BlockSpec((step_rows, keys), lambda i, g: (i, 0)),
            pl.BlockSpec((2, step_rows, lanes), lambda i, g: (0, i, 0)),
        ],
        out_specs=[pl.BlockSpec((step_rows, keys), lambda i, g: (i, 0))] * 2,
        scratch_shapes=[
            pltpu.VMEM((spans, total, queries, lanes), jnp.float32),
            pltpu.VMEM((2, total, queries, lanes), jnp.float32),
            pltpu.VMEM((groups, row_count, keys), jnp.float32),
        ],
        compiler_params=pltpu.CompilerParams(vmem_limit_bytes=second_vmem),
        cost_estimate=pl.CostEstimate(
            flops=2 * total * per * queries * keys,
            bytes_accessed=total * per * queries * keys * 2,
            transcendentals=rows * keys,
        ),
    )(*operands, att[:, :, None, :], logits, idx)


def logits_kernel(row_count, scale, lengths, start, *refs):
    *part_refs, logits_ref, idx_ref = refs
    rows, keys = logits_ref.shape
    per = rows // row_count
    key = lax.broadcasted_iota(jnp.int32, (row_count, keys), 1) + start[0]
    row = lax.broadcasted_iota(jnp.int32, (row_count, keys), 0)
    for i in range(per):
        value = None
        for part in part_refs:
            for p in range(i, part.shape[0], per):
                value = part[p] if value is None else value + part[p]
        length = jnp.full((row_count, keys), lengths[i * row_count], jnp.int32)
        for r in range(1, row_count):
            length = jnp.where(row == r, lengths[i * row_count + r], length)
        value = jnp.where(key < length, value * scale, -jnp.inf)
        logits_ref[i * row_count : (i + 1) * row_count, :] = value
        largest = jnp.maximum(jnp.max(value, axis=1, keepdims=True), far_below)
        rest = jnp.sum(jnp.exp(value - largest), axis=1, keepdims=True)
        idx_ref[0, i * row_count : (i + 1) * row_count, :] = jnp.broadcast_to(largest, (row_count, lanes))
        idx_ref[1, i * row_count : (i + 1) * row_count, :] = jnp.broadcast_to(rest, (row_count, lanes))


def index_logits(parts, lengths, start, scale):
    row_count, keys = parts[0].shape[1:]
    rows = lengths.shape[0]
    scalars = pl.BlockSpec(memory_space=pltpu.SMEM)
    return pl.pallas_call(
        functools.partial(logits_kernel, row_count, scale),
        out_shape=(
            jax.ShapeDtypeStruct((rows, keys), jnp.float32),
            jax.ShapeDtypeStruct((2, rows, lanes), jnp.float32),
        ),
        in_specs=[scalars, scalars] + [pl.BlockSpec(memory_space=pltpu.VMEM)] * len(parts),
        compiler_params=pltpu.CompilerParams(vmem_limit_bytes=32 * 2**20),
    )(lengths, start, *parts)


def swap(x, bit):
    size = lax.axis_size("ctx")
    return lax.ppermute(x, "ctx", [(i, i ^ bit) for i in range(size)])


def across(x):
    return lax.ppermute(x, "head", [(0, 1), (1, 0)])


def bring_and_sweep(block, sweep_blocks):
    ctx, head = lax.axis_size("ctx"), lax.axis_size("head")
    me, plane = lax.axis_index("ctx"), lax.axis_index("head")
    per = ctx // head
    if ctx != 16 or head != 2:
        moves = []
        for c in range(ctx):
            for h in range(head):
                moves.append((c * head + h, (h * per + c % per) * head + c // per))
        held, far, bit = lax.ppermute(block, ("ctx", "head"), moves), [0], 1
        while bit < ctx:
            held = jnp.concatenate([held, swap(held, bit)])
            far = far + [k ^ bit for k in far]
            bit *= 2
        return [sweep_blocks([held], [jnp.bitwise_xor(me, k) for k in far], False, head)]
    half = ctx // 2
    home = me // half == plane
    mine = lax.rem(me, half)

    def place(distance):
        return mine ^ distance

    away = swap(block, half)
    beside = across(block)
    away_beside = across(away)
    one = jnp.where(home, block, away)
    one_x, one_z = swap(one, 2), swap(one, 4)
    two = jnp.where(home, beside, away_beside)
    two_x, two_z = swap(two, 2), swap(two, 4)
    one_zx = swap(one_z, 2)
    two_xz = swap(two_x, 4)
    swept = []
    for part in ([one, one_x, one_z, one_zx], [two, two_x, two_z, two_xz]):
        blocks = part + [swap(a, 1) for a in part]
        swept.append(sweep_blocks(blocks, [place(k) for k in (0, 2, 4, 6, 1, 3, 5, 7)], False, 1))
    return swept


def body(absorbed_query, index_query, index_weight, kv_cache, index_keys, lengths):
    row_count, head_count, latent = absorbed_query.shape
    idx_heads, idx_width = index_query.shape[1:]
    ctx, head = lax.axis_size("ctx"), lax.axis_size("head")
    keys = kv_cache.shape[0]
    me, plane = lax.axis_index("ctx"), lax.axis_index("head")
    start = jnp.reshape(me * keys, (1,)).astype(jnp.int32)
    per = ctx // head
    own_rows = per * row_count
    own_lengths = lax.dynamic_slice_in_dim(lengths, plane * own_rows, own_rows)

    half = idx_width // 2
    idx_flat = index_query.reshape(row_count * idx_heads, idx_width)
    idx_packed = jnp.concatenate([idx_flat[:, :half], idx_flat[:, half:]])
    query = jnp.concatenate([absorbed_query.reshape(row_count * head_count, latent), idx_packed], axis=1)
    width = latent + half
    weight = index_weight.reshape(1, row_count * idx_heads)
    weight = jnp.pad(weight, ((0, 15), (0, width - weight.shape[1])))
    block = jnp.concatenate([query, weight])[None]

    kv = kv_cache.T

    def sweep_blocks(blocks, places, resident, parts):
        info = jnp.concatenate([start, jnp.stack(places).astype(jnp.int32)] + [own_lengths] * parts)
        return sweep(blocks, info, kv, index_keys, resident, row_count, head_count, idx_heads, latent)

    swept = bring_and_sweep(block, sweep_blocks)
    sets = []
    for arrays in swept:
        parts = arrays[4].shape[0] // per
        sets.append((arrays[:4], parts, arrays[0].shape[-1] == keys))
    stat = jnp.concatenate([arrays[4] for arrays in swept])
    queries = row_count * head_count

    logits, idx = index_logits([arrays[5] for arrays in swept], own_lengths, start, idx_width ** (-0.5))
    idx_max, idx_total = idx[0, :, 0], idx[1, :, 0]

    largest = jnp.concatenate([stat[:, 0, :].reshape(-1) * attention_scale, idx_max])
    total = jnp.concatenate([stat[:, 1, :].reshape(-1), idx_total])
    state = jnp.stack([largest, total])
    bit = 1
    while bit < ctx:
        other = swap(state, bit)
        top_two = jnp.maximum(state[0], other[0])
        merged = state[1] * jnp.exp(state[0] - top_two) + other[1] * jnp.exp(other[0] - top_two)
        state = jnp.stack([top_two, merged])
        bit *= 2
    whole = float(keys * ctx)
    factor = whole / (levels * head * head_count)
    att = jnp.stack([state[0, : ctx * queries] * (1.0 / attention_scale), factor / state[1, : ctx * queries]])
    att = att.reshape(2, ctx, queries)
    idx = jnp.stack([state[0, ctx * queries :], whole / state[1, ctx * queries :]])
    idx = jnp.broadcast_to(idx[:, :, None], idx.shape + (lanes,))
    return second(sets, att, logits, idx, row_count, head_count, attention_scale * log2_e)


def solution(mesh):
    return jax.shard_map(
        body,
        mesh=mesh,
        in_specs=(
            P("ctx", "head", None),
            P("ctx", "head", None),
            P("ctx", "head"),
            P("ctx", None),
            P("ctx", None),
            P(),
        ),
        out_specs=(P("head", "ctx"), P("head", "ctx")),
        check_vma=False,
    )
```

time: 515 us -> 153 us (0.30)
  other arithmetic: 122 us -> 3.36 us
  local copies, waits for them, and re-layouts: 127 us -> 10.2 us
  blocking collectives: 114 us -> 0 us
  matrix products: 98.5 us -> 0 us
  Pallas kernels: 0 us -> 70.9 us
  starting transfers between devices: 0.12 us -> 26.4 us
  between operations: 14.5 us -> 0.97 us
    dot_general x12 -> x0, matrix products: 98.5 us -> none  [the longest x4 53.1 us: block_scores(): jnp.einsum('qd,kd->qk', flat_query, cached, preferred_element_type=jnp.fl...]
    all_gather x4 -> x0, blocking collectives: 83 us -> none  [the longest x2 39.4 us: merged(): gathered = jax.tree.map(lambda a: lax.all_gather(a, axis), part)]
    pallas_call x0 -> x4, Pallas kernels: none -> 70.9 us  [the longest x2 50.2 us: sweep(): pl.pallas_call(kernel, out_shape=outs, grid_spec=pltpu.PrefetchScalarGrid...]
    mul x4 -> x0, local copies, waits for them, and re-layouts: 69.8 us -> none  [block_scores(): jnp.einsum('qd,kd->qk', flat_query, cached, preferred_element_type=jnp.fl...]
    reduce_sum x6 -> x0, other arithmetic: 67.2 us -> none  [the longest x4 43.4 us: advance(): jnp.sum(jnp.exp(scores - new_max[..., None]), axis=-1)]
    broadcast_in_dim x10 -> x1, local copies, waits for them, and re-layouts: 53.9 us -> 0.68 us  [body(): idx = jnp.broadcast_to(idx[:, :, None], idx.shape + (lanes,))]
    dynamic_update_slice x8 -> x0, other arithmetic: 49.7 us -> none  [the longest x4 49.5 us: advance(): lax.dynamic_update_slice_in_dim(kept, scores, block_index * block_keys, 2)]
    ppermute x0 -> x21, waiting for transfers between devices: none -> 41.2 us  [the longest x19 36.8 us: swap(): return lax.ppermute(x, 'ctx', [(i, i ^ bit) for i in range(size)])]
  transfers between devices with their start and end apart: 3 -> 21, of which waited for: 2 -> 11; matrix products, arithmetic and copies ran while one was open for 0% -> 2% of each run, Pallas kernels for 0% -> 16%
where the time goes in v2:
time: 153 us
  Pallas kernels  70.9 us (46%)
  waiting for transfers between devices  41.2 us (27%)
  starting transfers between devices  26.4 us (17%)
  local copies, waits for them, and re-layouts  10.2 us (7%)
  other arithmetic  3.36 us (2%)
    pallas_call x2, Pallas kernels, sweep(): pl.pallas_call(kernel, out_shape=outs, grid_spec=pltpu.PrefetchScalarGrid...  50.2 us
    ppermute x19, waiting for transfers between devices, swap(): return lax.ppermute(x, 'ctx', [(i, i ^ bit) for i in range(size)])  36.8 us
    ppermute x19, starting transfers between devices, swap(): return lax.ppermute(x, 'ctx', [(i, i ^ bit) for i in range(size)])  23.3 us
    pallas_call x1, Pallas kernels, second(): pl.pallas_call(functools.partial(second_kernel, row_count, head_count, sc...  19.6 us
    unnamed x11, local copies, waits for them, and re-layouts  6.12 us
    ppermute x2, waiting for transfers between devices, across(): return lax.ppermute(x, 'head', [(0, 1), (1, 0)])  4.42 us
    ppermute x2, starting transfers between devices, across(): return lax.ppermute(x, 'head', [(0, 1), (1, 0)])  3.09 us
  transfers between devices with their start and end apart: 21, of which 11 were waited for; matrix products, arithmetic and copies ran while one was open for 2% of the time, Pallas kernels for 16%

profile of v2, /device:TPU:0, one launch (start us, length us, event | category | flops | bytes accessed | tf_op | source)
XLA Modules:
  0.0 153.0 jit_solution(18336489693434530068)
XLA Ops:
  1.4 0.9 fusion.7
  2.3 1.1 fusion.2
  3.4 4.1 %collective-permute-start = (bf16[1,272,640]{2,1,0:T(8,128)(2,1)S(1)}, bf16[1,272,640]{2,1,0:T(8,128)(2,1)S(1)}, u32[]{:S(2)}, u32[]{:S(2)}) collective-permute-start(bf16[1,272,640]{2,1,0:T(8,128)(2,1)S(1)} %fusion.2), channel_id=1, source_target_pairs={{0,16},{2,18},{4,20},{6,22},{8,24},{10,26},{12,28},{14,30},{16,0},... | collective-permute-start | bytes 1044488 | tf_op jit(solution)/shard_map/ppermute | solution.py:373
  7.5 1.5 collective-permute-start.8
  9.0 14.1 %collective-permute-done = bf16[1,272,640]{2,1,0:T(8,128)(2,1)S(1)} collective-permute-done((bf16[1,272,640]{2,1,0:T(8,128)(2,1)S(1)}, bf16[1,272,640]{2,1,0:T(8,128)(2,1)S(1)}, u32[]{:S(2)}, u32[]{:S(2)}) %collective-permute-start) | collective-permute-done | bytes 348192 | tf_op jit(solution)/shard_map/ppermute | solution.py:373
  23.1 1.6 %collective-permute-start.9 = (bf16[1,272,640]{2,1,0:T(8,128)(2,1)S(1)}, bf16[1,272,640]{2,1,0:T(8,128)(2,1)S(1)}, u32[]{:S(2)}, u32[]{:S(2)}) collective-permute-start(bf16[1,272,640]{2,1,0:T(8,128)(2,1)S(1)} %collective-permute-done), channel_id=1, source_target_pairs={{0,1},{1,0},{2,3},{3,2},{4,5},{5,4},{6,7},{7,6},{8,9},{9,8},{10,11... | collective-permute-start | bytes 1044488 | tf_op jit(solution)/shard_map/ppermute | solution.py:377
  24.7 1.1 broadcast_select_fusion.1.rest_0_
  26.5 1.5 collective-permute-start.1
  28.0 4.4 %collective-permute-done.9 = bf16[1,272,640]{2,1,0:T(8,128)(2,1)S(1)} collective-permute-done((bf16[1,272,640]{2,1,0:T(8,128)(2,1)S(1)}, bf16[1,272,640]{2,1,0:T(8,128)(2,1)S(1)}, u32[]{:S(2)}, u32[]{:S(2)}) %collective-permute-start.9) | collective-permute-done | bytes 348192 | tf_op jit(solution)/shard_map/ppermute | solution.py:377
  32.5 1.3 collective-permute-start.10
  34.6 1.5 collective-permute-start.3
  36.1 1.4 collective-permute-done.1.rest_1_
  37.5 1.4 collective-permute-start.11
  38.8 6.1 %collective-permute-done.10.rest_1_ = bf16[1,272,640]{2,1,0:T(8,128)(2,1)S(1)} collective-permute-done((bf16[1,272,640]{2,1,0:T(8,128)(2,1)S(1)}, bf16[1,272,640]{2,1,0:T(8,128)(2,1)S(1)}, u32[]{:S(2)}, u32[]{:S(2)}) %collective-permute-start.10) | collective-permute-done | bytes 348192 | tf_op jit(solution)/shard_map/ppermute | solution.py:373
  44.9 1.4 collective-permute-start.12
  46.3 5.7 %collective-permute-done.3.rest_3_ = bf16[1,272,640]{2,1,0:T(8,128)(2,1)S(1)} collective-permute-done((bf16[1,272,640]{2,1,0:T(8,128)(2,1)S(1)}, bf16[1,272,640]{2,1,0:T(8,128)(2,1)S(1)}, u32[]{:S(2)}, u32[]{:S(2)}) %collective-permute-start.3) | collective-permute-done | bytes 348192 | tf_op jit(solution)/shard_map/ppermute | solution.py:373
  53.9 1.6 %collective-permute-done.12.rest_3_ = bf16[1,272,640]{2,1,0:T(8,128)(2,1)S(1)} collective-permute-done((bf16[1,272,640]{2,1,0:T(8,128)(2,1)S(1)}, bf16[1,272,640]{2,1,0:T(8,128)(2,1)S(1)}, u32[]{:S(2)}, u32[]{:S(2)}) %collective-permute-start.12) | collective-permute-done | bytes 348192 | tf_op jit(solution)/shard_map/ppermute | solution.py:373
  55.5 2.3 %copy-done.3 = bf16[4096,576]{0,1:T(8,128)(2,1)S(1)} copy-done((bf16[4096,576]{0,1:T(8,128)(2,1)S(1)}, bf16[4096,576]{0,1:T(8,128)(2,1)}, u32[]{:S(2)}) %copy-start.3) | copy-done | bytes 4718616
  57.8 1.2 copy-done.4
  59.1 24.9 %shard_map.77 = (s16[8,256,3072]{2,1,0:T(8,128)(2,1)}, s16[8,256,1024]{2,1,0:T(8,128)(2,1)}, f32[8,256,384]{2,1,0:T(8,128)}, f32[8,256,128]{2,1,0:T(8,128)}, f32...) custom-call(s32[41]{0:T(128)S(1)} %concatenate.45.info, bf16[576,4096]{1,0:T(8,128)(2,1)S(1)} %bitcast.32, ...), custom_call_target="tpu_custom_call" | custom-call | flops 17179869184 | bytes 16777216 | tf_op jit(solution)/shard_map/pallas_call | solution.py:185
  84.7 25.3 %shard_map.78 = (s16[8,256,3072]{2,1,0:T(8,128)(2,1)}, s16[8,256,1024]{2,1,0:T(8,128)(2,1)}, f32[8,256,384]{2,1,0:T(8,128)}, f32[8,256,128]{2,1,0:T(8,128)}, f32...) custom-call(s32[41]{0:T(128)S(1)} %concatenate.45.info, bf16[576,4096]{1,0:T(8,128)(2,1)S(1)} %bitcast.33, ...), custom_call_target="tpu_custom_call" | custom-call | flops 17179869184 | bytes 16777216 | tf_op jit(solution)/shard_map/pallas_call | solution.py:185
  110.0 1.0 copy-done.1
  111.1 1.1 shard_map.79
  112.2 0.8 copy-done.2
  114.5 0.9 collective-permute-done.17
  115.4 1.5 %collective-permute-start.18 = (f32[2,4128]{1,0:T(2,128)S(1)}, f32[2,4128]{1,0:T(2,128)S(1)}, u32[]{:S(2)}, u32[]{:S(2)}) collective-permute-start(f32[2,4128]{1,0:T(2,128)S(1)} %pad_maximum_fusion.1), channel_id=1, source_target_pairs={{0,4},{2,6},{4,0},{6,2},{8,12},{10,14},{12,8},{14,10},{16,20},{18,... | collective-permute-start | bytes 99080 | tf_op jit(solution)/shard_map/ppermute | solution.py:373
  117.0 2.4 %collective-permute-done.18 = f32[2,4128]{1,0:T(2,128)S(1)} collective-permute-done((f32[2,4128]{1,0:T(2,128)S(1)}, f32[2,4128]{1,0:T(2,128)S(1)}, u32[]{:S(2)}, u32[]{:S(2)}) %collective-permute-start.18) | collective-permute-done | bytes 33056 | tf_op jit(solution)/shard_map/ppermute | solution.py:373
  119.5 2.8 %collective-permute-start.19 = (f32[2,4128]{1,0:T(2,128)S(1)}, f32[2,4128]{1,0:T(2,128)S(1)}, u32[]{:S(2)}, u32[]{:S(2)}) collective-permute-start(f32[2,4128]{1,0:T(2,128)S(1)} %pad_maximum_fusion.2), channel_id=1, source_target_pairs={{0,8},{2,10},{4,12},{6,14},{8,0},{10,2},{12,4},{14,6},{16,24},{18,... | collective-permute-start | bytes 99080 | tf_op jit(solution)/shard_map/ppermute | solution.py:373
  122.4 1.9 %collective-permute-done.19 = f32[2,4128]{1,0:T(2,128)S(1)} collective-permute-done((f32[2,4128]{1,0:T(2,128)S(1)}, f32[2,4128]{1,0:T(2,128)S(1)}, u32[]{:S(2)}, u32[]{:S(2)}) %collective-permute-start.19) | collective-permute-done | bytes 33056 | tf_op jit(solution)/shard_map/ppermute | solution.py:373
  124.4 5.4 %collective-permute-start.20 = (f32[2,4128]{1,0:T(2,128)S(1)}, f32[2,4128]{1,0:T(2,128)S(1)}, u32[]{:S(2)}, u32[]{:S(2)}) collective-permute-start(f32[2,4128]{1,0:T(2,128)S(1)} %pad_maximum_fusion.3), channel_id=1, source_target_pairs={{0,16},{2,18},{4,20},{6,22},{8,24},{10,26},{12,28},{14,30},{16,0},... | collective-permute-start | bytes 99080 | tf_op jit(solution)/shard_map/ppermute | solution.py:373
  129.8 1.9 %collective-permute-done.20 = f32[2,4128]{1,0:T(2,128)S(1)} collective-permute-done((f32[2,4128]{1,0:T(2,128)S(1)}, f32[2,4128]{1,0:T(2,128)S(1)}, u32[]{:S(2)}, u32[]{:S(2)}) %collective-permute-start.20) | collective-permute-done | bytes 33056 | tf_op jit(solution)/shard_map/ppermute | solution.py:373
  133.2 19.6 %shard_map.80 = (f32[32,4096]{1,0:T(8,128)}, f32[32,4096]{1,0:T(8,128)}) custom-call(s16[1,8,256,3072]{3,2,1,0:T(8,128)(2,1)} %bitcast.34, s16[1,8,256,1024]{3,2,1,0:T(8,128)(2,1)} %bitcast.36, f32[1,8,256,384]{3,2,1,0:T(8,128)} %bitcast.38, f32[1,8,256,128]{3,2,1,0:T(8,128)} %bitcast.42, s16[1,8,256,3072]{3,2,1,0:T(8,128)(2,1)} %bitcast.35, ...), custom_call_target="tpu_custom_call" | custom-call | flops 33554432 | bytes 33554432 | tf_op jit(solution)/shard_map/pallas_call | solution.py:307
  (53 shorter events, 8.2 us)
Async XLA Ops:
  3.4 19.7 %collective-permute-start = (bf16[1,272,640]{2,1,0:T(8,128)(2,1)S(1)}, bf16[1,272,640]{2,1,0:T(8,128)(2,1)S(1)}, u32[]{:S(2)}, u32[]{:S(2)}) collective-permute-start(bf16[1,272,640]{2,1,0:T(8,128)(2,1)S(1)} %fusion.2), channel_id=1, source_target_pairs={{0,16},{2,18},{4,20},{6,22},{8,24},{10,26},{12,28},{14,30},{16,0},... | collective-permute-start | bytes 1044488 | tf_op jit(solution)/shard_map/ppermute | solution.py:373
  7.5 20.5 %collective-permute-start.8 = (bf16[1,272,640]{2,1,0:T(8,128)(2,1)S(1)}, bf16[1,272,640]{2,1,0:T(8,128)(2,1)S(1)}, u32[]{:S(2)}, u32[]{:S(2)}) collective-permute-start(bf16[1,272,640]{2,1,0:T(8,128)(2,1)S(1)} %fusion.2), channel_id=1, source_target_pairs={{0,1},{1,0},{2,3},{3,2},{4,5},{5,4},{6,7},{7,6},{8,9},{9,8},{10,11... | collective-permute-start | bytes 1044488 | tf_op jit(solution)/shard_map/ppermute | solution.py:377
  23.1 9.3 %collective-permute-start.9 = (bf16[1,272,640]{2,1,0:T(8,128)(2,1)S(1)}, bf16[1,272,640]{2,1,0:T(8,128)(2,1)S(1)}, u32[]{:S(2)}, u32[]{:S(2)}) collective-permute-start(bf16[1,272,640]{2,1,0:T(8,128)(2,1)S(1)} %collective-permute-done), channel_id=1, source_target_pairs={{0,1},{1,0},{2,3},{3,2},{4,5},{5,4},{6,7},{7,6},{8,9},{9,8},{10,11... | collective-permute-start | bytes 1044488 | tf_op jit(solution)/shard_map/ppermute | solution.py:377
  25.8 8.8 %collective-permute-start.2 = (bf16[1,272,640]{2,1,0:T(8,128)(2,1)S(1)}, bf16[1,272,640]{2,1,0:T(8,128)(2,1)S(1)}, u32[]{:S(2)}, u32[]{:S(2)}) collective-permute-start(bf16[1,272,640]{2,1,0:T(8,128)(2,1)S(1)} %broadcast_select_fusion.1.rest_0_), channel_id=1, source_target_pairs={{0,8},{2,10},{4,12},{6,14},{8,0},{10,2},{12,4},{14,6},{16,24},{18,... | collective-permute-start | bytes 1044488 | tf_op jit(solution)/shard_map/ppermute | solution.py:373
  26.5 11.0 %collective-permute-start.4 = (bf16[1,272,640]{2,1,0:T(8,128)(2,1)S(1)}, bf16[1,272,640]{2,1,0:T(8,128)(2,1)S(1)}, u32[]{:S(2)}, u32[]{:S(2)}) collective-permute-start(bf16[1,272,640]{2,1,0:T(8,128)(2,1)S(1)} %broadcast_select_fusion.1.rest_0_), channel_id=1, source_target_pairs={{0,2},{2,0},{4,6},{6,4},{8,10},{10,8},{12,14},{14,12},{16,18},{18,... | collective-permute-start | bytes 1044488 | tf_op jit(solution)/shard_map/ppermute | solution.py:373
  26.5 10.9 %collective-permute-start.1 = (bf16[1,272,640]{2,1,0:T(8,128)(2,1)S(1)}, bf16[1,272,640]{2,1,0:T(8,128)(2,1)S(1)}, u32[]{:S(2)}, u32[]{:S(2)}) collective-permute-start(bf16[1,272,640]{2,1,0:T(8,128)(2,1)S(1)} %broadcast_select_fusion.1.rest_0_), channel_id=1, source_target_pairs={{0,4},{2,6},{4,0},{6,2},{8,12},{10,14},{12,8},{14,10},{16,20},{18,... | collective-permute-start | bytes 1044488 | tf_op jit(solution)/shard_map/ppermute | solution.py:373
  32.5 12.4 %collective-permute-start.10 = (bf16[1,272,640]{2,1,0:T(8,128)(2,1)S(1)}, bf16[1,272,640]{2,1,0:T(8,128)(2,1)S(1)}, u32[]{:S(2)}, u32[]{:S(2)}) collective-permute-start(bf16[1,272,640]{2,1,0:T(8,128)(2,1)S(1)} %broadcast_select_fusion.rest_0_), channel_id=1, source_target_pairs={{0,4},{2,6},{4,0},{6,2},{8,12},{10,14},{12,8},{14,10},{16,20},{18,... | collective-permute-start | bytes 1044488 | tf_op jit(solution)/shard_map/ppermute | solution.py:373
  34.6 17.4 %collective-permute-start.3 = (bf16[1,272,640]{2,1,0:T(8,128)(2,1)S(1)}, bf16[1,272,640]{2,1,0:T(8,128)(2,1)S(1)}, u32[]{:S(2)}, u32[]{:S(2)}) collective-permute-start(bf16[1,272,640]{2,1,0:T(8,128)(2,1)S(1)} %collective-permute-done.2.rest_2_), channel_id=1, source_target_pairs={{0,4},{2,6},{4,0},{6,2},{8,12},{10,14},{12,8},{14,10},{16,20},{18,... | collective-permute-start | bytes 1044488 | tf_op jit(solution)/shard_map/ppermute | solution.py:373
  36.1 16.7 %collective-permute-start.6 = (bf16[1,272,640]{2,1,0:T(8,128)(2,1)S(1)}, bf16[1,272,640]{2,1,0:T(8,128)(2,1)S(1)}, u32[]{:S(2)}, u32[]{:S(2)}) collective-permute-start(bf16[1,272,640]{2,1,0:T(8,128)(2,1)S(1)} %collective-permute-done.2.rest_2_), channel_id=1, source_target_pairs={{0,2},{2,0},{4,6},{6,4},{8,10},{10,8},{12,14},{14,12},{16,18},{18,... | collective-permute-start | bytes 1044488 | tf_op jit(solution)/shard_map/ppermute | solution.py:373
  37.5 15.9 %collective-permute-start.5 = (bf16[1,272,640]{2,1,0:T(8,128)(2,1)S(1)}, bf16[1,272,640]{2,1,0:T(8,128)(2,1)}, u32[]{:S(2)}, u32[]{:S(2)}) collective-permute-start(bf16[1,272,640]{2,1,0:T(8,128)(2,1)S(1)} %collective-permute-done.1.rest_1_), channel_id=1, source_target_pairs={{0,2},{2,0},{4,6},{6,4},{8,10},{10,8},{12,14},{14,12},{16,18},{18,... | collective-permute-start | bytes 1044488 | tf_op jit(solution)/shard_map/ppermute | solution.py:373
  37.5 16.0 %collective-permute-start.11 = (bf16[1,272,640]{2,1,0:T(8,128)(2,1)S(1)}, bf16[1,272,640]{2,1,0:T(8,128)(2,1)S(1)}, u32[]{:S(2)}, u32[]{:S(2)}) collective-permute-start(bf16[1,272,640]{2,1,0:T(8,128)(2,1)S(1)} %broadcast_select_fusion.rest_0_), channel_id=1, source_target_pairs={{0,8},{2,10},{4,12},{6,14},{8,0},{10,2},{12,4},{14,6},{16,24},{18,... | collective-permute-start | bytes 1044488 | tf_op jit(solution)/shard_map/ppermute | solution.py:373
  44.9 10.6 %collective-permute-start.12 = (bf16[1,272,640]{2,1,0:T(8,128)(2,1)S(1)}, bf16[1,272,640]{2,1,0:T(8,128)(2,1)S(1)}, u32[]{:S(2)}, u32[]{:S(2)}) collective-permute-start(bf16[1,272,640]{2,1,0:T(8,128)(2,1)S(1)} %collective-permute-done.10.rest_1_), channel_id=1, source_target_pairs={{0,8},{2,10},{4,12},{6,14},{8,0},{10,2},{12,4},{14,6},{16,24},{18,... | collective-permute-start | bytes 1044488 | tf_op jit(solution)/shard_map/ppermute | solution.py:373
  52.0 3.5 %collective-permute-start.7 = (bf16[1,272,640]{2,1,0:T(8,128)(2,1)S(1)}, bf16[1,272,640]{2,1,0:T(8,128)(2,1)}, u32[]{:S(2)}, u32[]{:S(2)}) collective-permute-start(bf16[1,272,640]{2,1,0:T(8,128)(2,1)S(1)} %collective-permute-done.3.rest_3_), channel_id=1, source_target_pairs={{0,2},{2,0},{4,6},{6,4},{8,10},{10,8},{12,14},{14,12},{16,18},{18,... | collective-permute-start | bytes 1044488 | tf_op jit(solution)/shard_map/ppermute | solution.py:373
  52.8 31.8 %collective-permute-start.13 = (bf16[1,272,640]{2,1,0:T(8,128)(2,1)S(1)}, bf16[1,272,640]{2,1,0:T(8,128)(2,1)S(1)}, u32[]{:S(2)}, u32[]{:S(2)}) collective-permute-start(bf16[1,272,640]{2,1,0:T(8,128)(2,1)S(1)} %broadcast_select_fusion.rest_0_), channel_id=1, source_target_pairs={{0,2},{2,0},{4,6},{6,4},{8,10},{10,8},{12,14},{14,12},{16,18},{18,... | collective-permute-start | bytes 1044488 | tf_op jit(solution)/shard_map/ppermute | solution.py:373
  53.4 31.3 %collective-permute-start.14 = (bf16[1,272,640]{2,1,0:T(8,128)(2,1)S(1)}, bf16[1,272,640]{2,1,0:T(8,128)(2,1)S(1)}, u32[]{:S(2)}, u32[]{:S(2)}) collective-permute-start(bf16[1,272,640]{2,1,0:T(8,128)(2,1)S(1)} %collective-permute-done.10.rest_1_), channel_id=1, source_target_pairs={{0,2},{2,0},{4,6},{6,4},{8,10},{10,8},{12,14},{14,12},{16,18},{18,... | collective-permute-start | bytes 1044488 | tf_op jit(solution)/shard_map/ppermute | solution.py:373
  53.5 31.2 %collective-permute-start.15 = (bf16[1,272,640]{2,1,0:T(8,128)(2,1)S(1)}, bf16[1,272,640]{2,1,0:T(8,128)(2,1)S(1)}, u32[]{:S(2)}, u32[]{:S(2)}) collective-permute-start(bf16[1,272,640]{2,1,0:T(8,128)(2,1)S(1)} %collective-permute-done.11.rest_2_), channel_id=1, source_target_pairs={{0,2},{2,0},{4,6},{6,4},{8,10},{10,8},{12,14},{14,12},{16,18},{18,... | collective-permute-start | bytes 1044488 | tf_op jit(solution)/shard_map/ppermute | solution.py:373
  55.5 29.2 %collective-permute-start.16 = (bf16[1,272,640]{2,1,0:T(8,128)(2,1)S(1)}, bf16[1,272,640]{2,1,0:T(8,128)(2,1)S(1)}, u32[]{:S(2)}, u32[]{:S(2)}) collective-permute-start(bf16[1,272,640]{2,1,0:T(8,128)(2,1)S(1)} %collective-permute-done.12.rest_3_), channel_id=1, source_target_pairs={{0,2},{2,0},{4,6},{6,4},{8,10},{10,8},{12,14},{14,12},{16,18},{18,... | collective-permute-start | bytes 1044488 | tf_op jit(solution)/shard_map/ppermute | solution.py:373
  55.5 2.3 %copy-start.3 = (bf16[4096,576]{0,1:T(8,128)(2,1)S(1)}, bf16[4096,576]{0,1:T(8,128)(2,1)}, u32[]{:S(2)}) copy-start(bf16[4096,576]{0,1:T(8,128)(2,1)} %param.9) | copy-start | bytes 14155780
  57.8 1.2 copy-start.4
  84.7 25.3 %copy-start = (f32[8,4,4096]{2,1,0:T(4,128)S(1)}, f32[8,4,4096]{2,1,0:T(4,128)}, u32[]{:S(2)}) copy-start(f32[8,4,4096]{2,1,0:T(4,128)} %get-tuple-element.26.refs_0_) | copy-start | bytes 1572868
  110.0 1.0 copy-start.1
  112.2 0.8 copy-start.2
  113.9 1.4 collective-permute-start.17
  115.4 4.0 %collective-permute-start.18 = (f32[2,4128]{1,0:T(2,128)S(1)}, f32[2,4128]{1,0:T(2,128)S(1)}, u32[]{:S(2)}, u32[]{:S(2)}) collective-permute-start(f32[2,4128]{1,0:T(2,128)S(1)} %pad_maximum_fusion.1), channel_id=1, source_target_pairs={{0,4},{2,6},{4,0},{6,2},{8,12},{10,14},{12,8},{14,10},{16,20},{18,... | collective-permute-start | bytes 99080 | tf_op jit(solution)/shard_map/ppermute | solution.py:373
  119.5 4.7 %collective-permute-start.19 = (f32[2,4128]{1,0:T(2,128)S(1)}, f32[2,4128]{1,0:T(2,128)S(1)}, u32[]{:S(2)}, u32[]{:S(2)}) collective-permute-start(f32[2,4128]{1,0:T(2,128)S(1)} %pad_maximum_fusion.2), channel_id=1, source_target_pairs={{0,8},{2,10},{4,12},{6,14},{8,0},{10,2},{12,4},{14,6},{16,24},{18,... | collective-permute-start | bytes 99080 | tf_op jit(solution)/shard_map/ppermute | solution.py:373
  124.4 7.4 %collective-permute-start.20 = (f32[2,4128]{1,0:T(2,128)S(1)}, f32[2,4128]{1,0:T(2,128)S(1)}, u32[]{:S(2)}, u32[]{:S(2)}) collective-permute-start(f32[2,4128]{1,0:T(2,128)S(1)} %pad_maximum_fusion.3), channel_id=1, source_target_pairs={{0,16},{2,18},{4,20},{6,22},{8,24},{10,26},{12,28},{14,30},{16,0},... | collective-permute-start | bytes 99080 | tf_op jit(solution)/shard_map/ppermute | solution.py:373

commit v3 on v2

v3 whole, which is shorter than its diff:
```python
import functools

import jax
import jax.numpy as jnp
from jax import lax
from jax.experimental import pallas as pl
from jax.experimental.pallas import tpu as pltpu
from jax.sharding import PartitionSpec as P

attention_scale = 192.0 ** (-0.5)
log2_e = 1.4426950408889634
far_below = -1e30
levels = 32767.0
lanes = 128
span_count = 4
lag = 2
vmem_limit = 32 * 2**20
second_vmem = 57 * 2**20


def sweep_kernel(row_count, head_count, idx_heads, latent, spans, pack, sizes, info, kv_ref, ik_ref, *rest):
    sources, rest = rest[: len(sizes)], rest[len(sizes) :]
    e_hbm, top_hbm, stat_ref, part_ref, *rest = rest
    e_slots, top_slots, s_all, m_all, run_m, run_t, turn_m, turn_t, iq_ref, w_ref, q_slots, e_sems, top_sems, q_sems = rest
    count = sum(sizes)
    queries = row_count * head_count
    keys = kv_ref.shape[1]
    span = keys // spans
    idx_queries = row_count * idx_heads
    scale = attention_scale * log2_e
    start = info[0]

    def query_copy(tile, act):
        passed = 0
        for source, size in zip(sources, sizes):

            @pl.when(jnp.logical_and(tile >= passed, tile < passed + size))
            def _(source=source, passed=passed):
                into = lax.rem(tile, 2 * pack)
                act(pltpu.make_async_copy(source.at[tile - passed], q_slots.at[into], q_sems.at[into]))

            passed += size

    def result_copies(tile, act):
        slot, place = lax.rem(tile, 3 * pack), info[1 + tile]
        act(pltpu.make_async_copy(e_slots.at[slot], e_hbm.at[place], e_sems.at[slot]))
        act(pltpu.make_async_copy(top_slots.at[slot], top_hbm.at[place], top_sems.at[slot]))

    def begin(copy):
        copy.start()

    def await_end(copy):
        copy.wait()

    def scores(u, q_ref, first_row, masked):
        s_ref, m_ref = s_all.at[u], m_all.at[u]
        for at in range(0, span, min(512, span)):
            size = min(512, span)
            y = jnp.dot(
                q_ref[:queries, :latent],
                kv_ref[:, u * span + at : u * span + at + size],
                preferred_element_type=jnp.float32,
            )
            if masked:
                key = lax.broadcasted_iota(jnp.int32, (head_count, size), 1) + (start + u * span + at)
                pieces = []
                for r in range(row_count):
                    piece = y[r * head_count : (r + 1) * head_count]
                    pieces.append(jnp.where(key < info[first_row + r], piece, -jnp.inf))
                y = jnp.concatenate(pieces, axis=0)
            s_ref[:, at : at + size] = y
            top = y[:, :lanes]
            for j in range(lanes, size, lanes):
                top = jnp.maximum(top, y[:, j : j + lanes])
            m_ref[...] = jnp.maximum(top, far_below if at == 0 else m_ref[...])

    def index_part(u, q_ref, place):
        if u == 0:
            packed = q_ref[: 2 * idx_queries, latent:]
            iq_ref[...] = jnp.concatenate([packed[:idx_queries], packed[idx_queries:]], axis=1)
            weight = q_ref[queries : queries + 8, :lanes].astype(jnp.float32)[0:1]
            w_ref[...] = jnp.transpose(jnp.broadcast_to(weight, (lanes, lanes)))[:idx_queries]
        for at in range(u * span, (u + 1) * span, min(256, span)):
            size = min(256, span)
            inner = lax.dot_general(
                iq_ref[...], ik_ref[at : at + size, :], (((1,), (1,)), ((), ())), preferred_element_type=jnp.float32
            )
            for j in range(0, size, lanes):
                product = jnp.maximum(inner[:, j : j + lanes], 0.0) * w_ref[...]
                product = jnp.sum(product.reshape(row_count, idx_heads, lanes), axis=1)
                part_ref[place, :, at + j : at + j + lanes] = product

    def exponentials(u, slot):
        s_ref, m_ref = s_all.at[u], m_all.at[u]
        out, top_out = e_slots.at[slot], top_slots.at[slot]
        for q in range(0, queries, 16):
            top = m_ref[q : q + 16, :]
            total = None
            for j in range(0, span, lanes):
                e = jnp.exp2((s_ref[q : q + 16, j : j + lanes] - top) * scale)
                total = e if total is None else total + e
                out[q : q + 16, u * span + j : u * span + j + lanes] = jnp.round(e * levels).astype(jnp.int32).astype(jnp.int16)
            top_out[q : q + 16, u * lanes : (u + 1) * lanes] = top
            if u == 0:
                run_m[q : q + 16, :] = top
                run_t[q : q + 16, :] = total
            else:
                held = run_m[q : q + 16, :]
                larger = jnp.maximum(held, top)
                run_m[q : q + 16, :] = larger
                run_t[q : q + 16, :] = run_t[q : q + 16, :] * jnp.exp2((held - larger) * scale) + total * jnp.exp2(
                    (top - larger) * scale
                )

    def turn():
        turn_m[...] = jnp.transpose(run_m[...])
        turn_t[...] = jnp.transpose(run_t[...])

    def finish(place):
        top = turn_m[...]
        largest = jnp.max(top, axis=0, keepdims=True)
        stat_ref[place, 0:1, :] = largest
        stat_ref[place, 1:2, :] = jnp.sum(turn_t[...] * jnp.exp2((top - largest) * scale), axis=0, keepdims=True)

    def guarded(tile, action):
        pl.when(jnp.logical_and(tile >= 0, tile < count))(action)

    def boundary(i):
        for k in range(pack):
            old, done = pack * (i - 2) - 1 + k, pack * (i - 1) - 1 + k
            guarded(old, functools.partial(result_copies, old, await_end))
            guarded(done, functools.partial(result_copies, done, begin))

    def step(i, _):
        tiles = [i * pack + k for k in range(pack)]
        rows = [1 + count + info[1 + tile] * row_count for tile in tiles]
        shortest = info[rows[0]]
        for first_row in rows:
            for r in range(row_count):
                shortest = jnp.minimum(shortest, info[first_row + r])
        clear = shortest >= start + keys
        for tile in tiles:
            query_copy(tile, await_end)
        for tile in tiles:
            query_copy(tile + pack, begin)
        boundary(i)

        def work(masked):
            for tile, first_row in zip(tiles, rows):
                slot = lax.rem(tile, 3 * pack)
                other = lax.rem(tile + 3 * pack - 1, 3 * pack)
                q_ref = q_slots.at[lax.rem(tile, 2 * pack)]
                place = info[1 + tile]
                before = info[1 + jnp.maximum(tile - 1, 0)]
                for u in range(spans):
                    scores(u, q_ref, first_row, masked)
                    if u == lag:
                        turn()
                    index_part(u, q_ref, place)
                    exponentials((u - lag) % spans, other if u < lag else slot)
                    if u == min(lag + 1, spans - 1):
                        finish(before)

        pl.when(clear)(lambda: work(False))
        pl.when(jnp.logical_not(clear))(lambda: work(True))
        return 0

    steps = count // pack
    for tile in range(pack):
        query_copy(tile, begin)
    lax.fori_loop(0, steps, step, 0)
    boundary(steps)
    for u in range(spans - lag, spans):
        exponentials(u, (count - 1) % (3 * pack))
    result_copies(count - 1, begin)
    turn()
    finish(info[count])
    for tile in range(max(0, count - 1 - pack), count):
        result_copies(tile, await_end)


def sweep(blocks, info, kv, idx_keys, row_count, head_count, idx_heads, latent):
    sizes = [a.shape[0] for a in blocks]
    count = sum(sizes)
    block_rows, width = blocks[0].shape[1:]
    keys = kv.shape[1]
    queries = row_count * head_count
    spans = span_count
    span = keys // spans
    pack = 1
    kernel = functools.partial(sweep_kernel, row_count, head_count, idx_heads, latent, spans, pack, sizes)
    whole = pl.BlockSpec(memory_space=pltpu.VMEM)
    far = pl.BlockSpec(memory_space=pltpu.HBM)
    return pl.pallas_call(
        kernel,
        out_shape=(
            pltpu.HBM((count, queries, keys), jnp.int16),
            pltpu.HBM((count, queries, spans * lanes), jnp.float32),
            jax.ShapeDtypeStruct((count, 2, queries), jnp.float32),
            jax.ShapeDtypeStruct((count, row_count, keys), jnp.float32),
        ),
        in_specs=[pl.BlockSpec(memory_space=pltpu.SMEM), whole, whole] + [far] * len(blocks),
        out_specs=[far, far, whole, whole],
        scratch_shapes=[
            pltpu.VMEM((3 * pack, queries, keys), jnp.int16),
            pltpu.VMEM((3 * pack, queries, spans * lanes), jnp.float32),
        ]
        + [pltpu.VMEM((spans, queries, span), jnp.float32), pltpu.VMEM((spans, queries, lanes), jnp.float32)]
        + [pltpu.VMEM((queries, lanes), jnp.float32)] * 2
        + [pltpu.VMEM((lanes, queries), jnp.float32)] * 2
        + [pltpu.VMEM((row_count * idx_heads, idx_keys.shape[1]), jnp.bfloat16)]
        + [pltpu.VMEM((row_count * idx_heads, lanes), jnp.float32)]
        + [pltpu.VMEM((2 * pack, block_rows, width), jnp.bfloat16)]
        + [pltpu.SemaphoreType.DMA((3 * pack,))] * 2
        + [pltpu.SemaphoreType.DMA((2 * pack,))],
        compiler_params=pltpu.CompilerParams(vmem_limit_bytes=vmem_limit),
        cost_estimate=pl.CostEstimate(
            flops=2 * count * queries * keys * 1024,
            bytes_accessed=count * queries * keys * 2,
            transcendentals=count * queries * keys,
        ),
    )(info, kv, idx_keys, *blocks)


def second_kernel(row_count, head_count, scale, spans, per, layout, *refs):
    arrays, refs = refs[: 2 * len(layout)], refs[2 * len(layout) :]
    att_ref, logits_ref, idx_ref, t_ref, g_ref, c_ref, turn_ref, sum_ref = refs
    queries = c_ref.shape[2]
    keys = t_ref.shape[1]
    span = keys // spans
    groups = t_ref.shape[0] // row_count
    group = pl.program_id(1)
    first = pl.program_id(0) * groups + group

    members = []
    for k, parts in enumerate(layout):
        for p in range(parts):
            members.append((len(members) * per + first, arrays[2 * k].at[p, 0], arrays[2 * k + 1].at[p, 0]))

    for p, (place, _, _) in enumerate(members):
        turn_ref[0, p] = jnp.transpose(jnp.broadcast_to(att_ref[0, place], (lanes, queries)))
        turn_ref[1, p] = jnp.transpose(jnp.broadcast_to(att_ref[1, place], (lanes, queries)))

    def factors(u):
        for p, (_, _, top) in enumerate(members):
            top_u = top[:, u * lanes : (u + 1) * lanes]
            c_ref[u, p] = jnp.exp2((top_u - turn_ref[0, p]) * scale) * turn_ref[1, p]

    factors(0)
    for u in range(spans):
        if u + 1 < spans:
            factors(u + 1)
        for r in range(row_count):
            acc = [None] * (span // lanes)
            for p, (_, source, _) in enumerate(members):
                for q in range(r * head_count, (r + 1) * head_count, 16):
                    c = c_ref[u, p, q : q + 16, :]
                    for k in range(len(acc)):
                        at = u * span + k * lanes
                        term = source[q : q + 16, at : at + lanes].astype(jnp.float32) * c
                        term = term[:8] + term[8:]
                        acc[k] = term if acc[k] is None else acc[k] + term
            for k in range(len(acc)):
                at = u * span + k * lanes
                sum_ref[group, r : r + 1, at : at + lanes] = jnp.sum(acc[k], axis=0, keepdims=True)

    @pl.when(group == groups - 1)
    def _():
        target = jnp.concatenate([sum_ref[g] for g in range(groups)], axis=0)
        predicted = jnp.exp(logits_ref[...] - idx_ref[0, :, 0:1]) * idx_ref[1, :, 0:1]
        t_ref[...] = target
        g_ref[...] = predicted - target


def second(sets, att, logits, idx, row_count, head_count, scale):
    rows, keys = logits.shape
    queries = row_count * head_count
    spans = span_count
    per = rows // row_count
    step_rows = min(8, rows)
    groups = step_rows // row_count
    shape = jax.ShapeDtypeStruct((rows, keys), jnp.float32)

    def mine(i, g):
        return (0, i * groups + g, 0, 0)

    operands, specs, total = [], [], 0
    for e, top, parts in sets:
        total += parts
        for a in (e, top):
            operands.append(a.reshape((parts, per) + a.shape[1:]))
            specs.append(pl.BlockSpec((parts, 1) + a.shape[1:], mine))
    layout = [parts for _, _, parts in sets]
    return pl.pallas_call(
        functools.partial(second_kernel, row_count, head_count, scale, spans, per, layout),
        out_shape=(shape, shape),
        grid=(rows // step_rows, groups),
        in_specs=specs
        + [
            pl.BlockSpec((2, total * per, 1, queries), lambda i, g: (0, 0, 0, 0)),
            pl.BlockSpec((step_rows, keys), lambda i, g: (i, 0)),
            pl.BlockSpec((2, step_rows, lanes), lambda i, g: (0, i, 0)),
        ],
        out_specs=[pl.BlockSpec((step_rows, keys), lambda i, g: (i, 0))] * 2,
        scratch_shapes=[
            pltpu.VMEM((spans, total, queries, lanes), jnp.float32),
            pltpu.VMEM((2, total, queries, lanes), jnp.float32),
            pltpu.VMEM((groups, row_count, keys), jnp.float32),
        ],
        compiler_params=pltpu.CompilerParams(vmem_limit_bytes=second_vmem),
        cost_estimate=pl.CostEstimate(
            flops=2 * total * per * queries * keys,
            bytes_accessed=total * per * queries * keys * 2,
            transcendentals=rows * keys,
        ),
    )(*operands, att[:, :, None, :], logits, idx)


def logits_kernel(row_count, scale, lengths, start, *refs):
    *part_refs, logits_ref, idx_ref = refs
    rows, keys = logits_ref.shape
    per = rows // row_count
    key = lax.broadcasted_iota(jnp.int32, (row_count, keys), 1) + start[0]
    row = lax.broadcasted_iota(jnp.int32, (row_count, keys), 0)
    for i in range(per):
        value = None
        for part in part_refs:
            for p in range(i, part.shape[0], per):
                value = part[p] if value is None else value + part[p]
        length = jnp.full((row_count, keys), lengths[i * row_count], jnp.int32)
        for r in range(1, row_count):
            length = jnp.where(row == r, lengths[i * row_count + r], length)
        value = jnp.where(key < length, value * scale, -jnp.inf)
        logits_ref[i * row_count : (i + 1) * row_count, :] = value
        largest = jnp.maximum(jnp.max(value, axis=1, keepdims=True), far_below)
        rest = jnp.sum(jnp.exp(value - largest), axis=1, keepdims=True)
        idx_ref[0, i * row_count : (i + 1) * row_count, :] = jnp.broadcast_to(largest, (row_count, lanes))
        idx_ref[1, i * row_count : (i + 1) * row_count, :] = jnp.broadcast_to(rest, (row_count, lanes))


def index_logits(parts, lengths, start, scale):
    row_count, keys = parts[0].shape[1:]
    rows = lengths.shape[0]
    scalars = pl.BlockSpec(memory_space=pltpu.SMEM)
    return pl.pallas_call(
        functools.partial(logits_kernel, row_count, scale),
        out_shape=(
            jax.ShapeDtypeStruct((rows, keys), jnp.float32),
            jax.ShapeDtypeStruct((2, rows, lanes), jnp.float32),
        ),
        in_specs=[scalars, scalars] + [pl.BlockSpec(memory_space=pltpu.VMEM)] * len(parts),
        compiler_params=pltpu.CompilerParams(vmem_limit_bytes=32 * 2**20),
    )(lengths, start, *parts)


def swap(x, bit):
    size = lax.axis_size("ctx")
    return lax.ppermute(x, "ctx", [(i, i ^ bit) for i in range(size)])


def bring_and_sweep(block, sweep_blocks):
    ctx, head = lax.axis_size("ctx"), lax.axis_size("head")
    me, plane = lax.axis_index("ctx"), lax.axis_index("head")
    per = ctx // head
    if ctx != 16 or head != 2:
        moves = []
        for c in range(ctx):
            for h in range(head):
                moves.append((c * head + h, (h * per + c % per) * head + c // per))
        held, far, bit = lax.ppermute(block, ("ctx", "head"), moves), [0], 1
        while bit < ctx:
            held = jnp.concatenate([held, swap(held, bit)])
            far = far + [k ^ bit for k in far]
            bit *= 2
        return [sweep_blocks([held], [jnp.bitwise_xor(me, k) for k in far], head)]
    half = ctx // 2
    home = me // half == plane
    mine = lax.rem(me, half)

    def place(distance):
        return mine ^ distance

    to_away, to_beside, to_both = [], [], []
    for c in range(ctx):
        for h in range(head):
            if c // half == h:
                to_away.append((c * head + h, (c ^ half) * head + h))
            else:
                to_beside.append((c * head + h, c * head + (1 - h)))
                to_both.append((c * head + h, (c ^ half) * head + (1 - h)))
    away = lax.ppermute(block, ("ctx", "head"), to_away)
    beside = lax.ppermute(block, ("ctx", "head"), to_beside)
    away_beside = lax.ppermute(block, ("ctx", "head"), to_both)
    one = jnp.where(home, block, away)
    one_x, one_z = swap(one, 2), swap(one, 4)
    two = jnp.where(home, beside, away_beside)
    two_x, two_z = swap(two, 2), swap(two, 4)
    one_zx = swap(one_z, 2)
    two_xz = swap(two_x, 4)
    swept = []
    for part in ([one, one_x, one_z, one_zx], [two, two_x, two_z, two_xz]):
        blocks = part + [swap(a, 1) for a in part]
        swept.append(sweep_blocks(blocks, [place(k) for k in (0, 2, 4, 6, 1, 3, 5, 7)], 1))
    return swept


def body(absorbed_query, index_query, index_weight, kv_cache, index_keys, lengths):
    row_count, head_count, latent = absorbed_query.shape
    idx_heads, idx_width = index_query.shape[1:]
    ctx, head = lax.axis_size("ctx"), lax.axis_size("head")
    keys = kv_cache.shape[0]
    me, plane = lax.axis_index("ctx"), lax.axis_index("head")
    start = jnp.reshape(me * keys, (1,)).astype(jnp.int32)
    per = ctx // head
    own_rows = per * row_count
    own_lengths = lax.dynamic_slice_in_dim(lengths, plane * own_rows, own_rows)

    half = idx_width // 2
    idx_flat = index_query.reshape(row_count * idx_heads, idx_width)
    idx_packed = jnp.concatenate([idx_flat[:, :half], idx_flat[:, half:]])
    query = jnp.concatenate([absorbed_query.reshape(row_count * head_count, latent), idx_packed], axis=1)
    width = latent + half
    weight = index_weight.reshape(1, row_count * idx_heads)
    weight = jnp.pad(weight, ((0, 15), (0, width - weight.shape[1])))
    block = jnp.concatenate([query, weight])[None]

    kv = kv_cache.T

    def sweep_blocks(blocks, places, parts):
        info = jnp.concatenate([start, jnp.stack(places).astype(jnp.int32)] + [own_lengths] * parts)
        return sweep(blocks, info, kv, index_keys, row_count, head_count, idx_heads, latent)

    swept = bring_and_sweep(block, sweep_blocks)
    sets = [(e, top, e.shape[0] // per) for e, top, _, _ in swept]
    stat = jnp.concatenate([stat for _, _, stat, _ in swept])
    queries = row_count * head_count

    logits, idx = index_logits([part for _, _, _, part in swept], own_lengths, start, idx_width ** (-0.5))
    idx_max, idx_total = idx[0, :, 0], idx[1, :, 0]

    largest = jnp.concatenate([stat[:, 0, :].reshape(-1) * attention_scale, idx_max])
    total = jnp.concatenate([stat[:, 1, :].reshape(-1), idx_total])
    state = jnp.stack([largest, total])
    bit = 1
    while bit < ctx:
        other = swap(state, bit)
        top_two = jnp.maximum(state[0], other[0])
        merged = state[1] * jnp.exp(state[0] - top_two) + other[1] * jnp.exp(other[0] - top_two)
        state = jnp.stack([top_two, merged])
        bit *= 2
    whole = float(keys * ctx)
    factor = whole / (levels * head * head_count)
    att = jnp.stack([state[0, : ctx * queries] * (1.0 / attention_scale), factor / state[1, : ctx * queries]])
    att = att.reshape(2, ctx, queries)
    idx = jnp.stack([state[0, ctx * queries :], whole / state[1, ctx * queries :]])
    idx = jnp.broadcast_to(idx[:, :, None], idx.shape + (lanes,))
    return second(sets, att, logits, idx, row_count, head_count, attention_scale * log2_e)


def solution(mesh):
    return jax.shard_map(
        body,
        mesh=mesh,
        in_specs=(
            P("ctx", "head", None),
            P("ctx", "head", None),
            P("ctx", "head"),
            P("ctx", None),
            P("ctx", None),
            P(),
        ),
        out_specs=(P("head", "ctx"), P("head", "ctx")),
        check_vma=False,
    )
```

time: 153 us -> 150 us (0.980)
  starting transfers between devices: 26.4 us -> 32.9 us
  waiting for transfers between devices: 41.2 us -> 35.7 us
  local copies, waits for them, and re-layouts: 10.2 us -> 7.67 us
  Pallas kernels: 70.9 us -> 68.6 us
    ppermute x19 -> x18, waiting for transfers between devices: 36.8 us -> 30.3 us  [swap(): return lax.ppermute(x, 'ctx', [(i, i ^ bit) for i in range(size)])]
    ppermute x2 -> x3, starting transfers between devices: 3.09 us -> 7.94 us  [the longest x1 5.96 us: bring_and_sweep(): away = lax.ppermute(block, ('ctx', 'head'), to_away)]
    pallas_call x2, Pallas kernels: 50.2 us -> 48.1 us  [sweep(): pl.pallas_call(kernel, out_shape=(pltpu.HBM((count, queries, keys), jnp.i...]
    unnamed x11 -> x7, local copies, waits for them, and re-layouts: 6.12 us -> 4.36 us
    ppermute x19 -> x18, starting transfers between devices: 23.3 us -> 25 us  [swap(): return lax.ppermute(x, 'ctx', [(i, i ^ bit) for i in range(size)])]
    ppermute x2 -> x3, waiting for transfers between devices: 4.42 us -> 5.41 us  [the longest x1 5.4 us: bring_and_sweep(): away = lax.ppermute(block, ('ctx', 'head'), to_away)]
  transfers between devices with their start and end apart: 21 -> 21, of which waited for: 11 -> 9; matrix products, arithmetic and copies ran while one was open for 2% -> 1% of each run, Pallas kernels for 16% -> 16%
where the time goes in v3:
time: 150 us; the launch traced here: 149 us
  Pallas kernels  68.6 us (46%)
  waiting for transfers between devices  35.7 us (24%)
  starting transfers between devices  32.9 us (22%)
  local copies, waits for them, and re-layouts  7.67 us (5%)
  other arithmetic  3.35 us (2%)
    pallas_call x2, Pallas kernels, sweep(): pl.pallas_call(kernel, out_shape=(pltpu.HBM((count, queries, keys), jnp.i...  48.1 us
    ppermute x18, waiting for transfers between devices, swap(): return lax.ppermute(x, 'ctx', [(i, i ^ bit) for i in range(size)])  30.3 us
    ppermute x18, starting transfers between devices, swap(): return lax.ppermute(x, 'ctx', [(i, i ^ bit) for i in range(size)])  25 us
    pallas_call x1, Pallas kernels, second(): pl.pallas_call(functools.partial(second_kernel, row_count, head_count, sc...  19.5 us
    ppermute x1, starting transfers between devices, bring_and_sweep(): away = lax.ppermute(block, ('ctx', 'head'), to_away)  5.96 us
    ppermute x1, waiting for transfers between devices, bring_and_sweep(): away = lax.ppermute(block, ('ctx', 'head'), to_away)  5.4 us
    unnamed x7, local copies, waits for them, and re-layouts  4.36 us
  transfers between devices with their start and end apart: 21, of which 9 were waited for; matrix products, arithmetic and copies ran while one was open for 1% of the time, Pallas kernels for 16%

profile of v3, /device:TPU:0, one launch (start us, length us, event | category | flops | bytes accessed | tf_op | source)
XLA Modules:
  0.0 149.1 jit_solution(7599269416906885273)
XLA Ops:
  0.6 0.9 fusion.7
  1.5 0.8 reshape.85
  2.3 1.1 fusion.2
  3.4 6.0 %collective-permute-start = (bf16[1,272,640]{2,1,0:T(8,128)(2,1)S(1)}, bf16[1,272,640]{2,1,0:T(8,128)(2,1)S(1)}, u32[]{:S(2)}, u32[]{:S(2)}) collective-permute-start(bf16[1,272,640]{2,1,0:T(8,128)(2,1)S(1)} %fusion.2), channel_id=1, source_target_pairs={{0,16},{2,18},{4,20},{6,22},{8,24},{10,26},{12,28},{14,30},{17,1},... | collective-permute-start | bytes 1044488 | tf_op jit(solution)/shard_map/ppermute | solution.py:391
  9.3 1.3 collective-permute-start.8
  10.6 0.7 collective-permute-start.9
  11.4 5.4 %collective-permute-done = bf16[1,272,640]{2,1,0:T(8,128)(2,1)S(1)} collective-permute-done((bf16[1,272,640]{2,1,0:T(8,128)(2,1)S(1)}, bf16[1,272,640]{2,1,0:T(8,128)(2,1)S(1)}, u32[]{:S(2)}, u32[]{:S(2)}) %collective-permute-start) | collective-permute-done | bytes 348192 | tf_op jit(solution)/shard_map/ppermute | solution.py:391
  16.8 1.1 broadcast_select_fusion.1.rest_0_
  17.9 8.9 %collective-permute-start.2 = (bf16[1,272,640]{2,1,0:T(8,128)(2,1)S(1)}, bf16[1,272,640]{2,1,0:T(8,128)(2,1)S(1)}, u32[]{:S(2)}, u32[]{:S(2)}) collective-permute-start(bf16[1,272,640]{2,1,0:T(8,128)(2,1)S(1)} %broadcast_select_fusion.1.rest_0_), channel_id=1, source_target_pairs={{0,8},{2,10},{4,12},{6,14},{8,0},{10,2},{12,4},{14,6},{16,24},{18,... | collective-permute-start | bytes 1044488 | tf_op jit(solution)/shard_map/ppermute | solution.py:358
  26.9 1.6 %collective-permute-start.10 = (bf16[1,272,640]{2,1,0:T(8,128)(2,1)S(1)}, bf16[1,272,640]{2,1,0:T(8,128)(2,1)S(1)}, u32[]{:S(2)}, u32[]{:S(2)}) collective-permute-start(bf16[1,272,640]{2,1,0:T(8,128)(2,1)S(1)} %broadcast_select_fusion.rest_0_), channel_id=1, source_target_pairs={{0,4},{2,6},{4,0},{6,2},{8,12},{10,14},{12,8},{14,10},{16,20},{18,... | collective-permute-start | bytes 1044488 | tf_op jit(solution)/shard_map/ppermute | solution.py:358
  29.0 10.9 %collective-permute-done.2.rest_2_ = bf16[1,272,640]{2,1,0:T(8,128)(2,1)S(1)} collective-permute-done((bf16[1,272,640]{2,1,0:T(8,128)(2,1)S(1)}, bf16[1,272,640]{2,1,0:T(8,128)(2,1)S(1)}, u32[]{:S(2)}, u32[]{:S(2)}) %collective-permute-start.2) | collective-permute-done | bytes 348192 | tf_op jit(solution)/shard_map/ppermute | solution.py:358
  39.8 1.5 %collective-permute-start.3 = (bf16[1,272,640]{2,1,0:T(8,128)(2,1)S(1)}, bf16[1,272,640]{2,1,0:T(8,128)(2,1)S(1)}, u32[]{:S(2)}, u32[]{:S(2)}) collective-permute-start(bf16[1,272,640]{2,1,0:T(8,128)(2,1)S(1)} %collective-permute-done.2.rest_2_), channel_id=1, source_target_pairs={{0,4},{2,6},{4,0},{6,2},{8,12},{10,14},{12,8},{14,10},{16,20},{18,... | collective-permute-start | bytes 1044488 | tf_op jit(solution)/shard_map/ppermute | solution.py:358
  41.4 6.0 %collective-permute-done.11.rest_2_ = bf16[1,272,640]{2,1,0:T(8,128)(2,1)S(1)} collective-permute-done((bf16[1,272,640]{2,1,0:T(8,128)(2,1)S(1)}, bf16[1,272,640]{2,1,0:T(8,128)(2,1)S(1)}, u32[]{:S(2)}, u32[]{:S(2)}) %collective-permute-start.11) | collective-permute-done | bytes 348192 | tf_op jit(solution)/shard_map/ppermute | solution.py:358
  47.8 3.8 %collective-permute-done.3.rest_3_ = bf16[1,272,640]{2,1,0:T(8,128)(2,1)S(1)} collective-permute-done((bf16[1,272,640]{2,1,0:T(8,128)(2,1)S(1)}, bf16[1,272,640]{2,1,0:T(8,128)(2,1)S(1)}, u32[]{:S(2)}, u32[]{:S(2)}) %collective-permute-start.3) | collective-permute-done | bytes 348192 | tf_op jit(solution)/shard_map/ppermute | solution.py:358
  51.6 0.7 dynamic_slice.3.lengths
  53.0 1.7 %collective-permute-done.12.rest_3_ = bf16[1,272,640]{2,1,0:T(8,128)(2,1)S(1)} collective-permute-done((bf16[1,272,640]{2,1,0:T(8,128)(2,1)S(1)}, bf16[1,272,640]{2,1,0:T(8,128)(2,1)S(1)}, u32[]{:S(2)}, u32[]{:S(2)}) %collective-permute-start.12) | collective-permute-done | bytes 348192 | tf_op jit(solution)/shard_map/ppermute | solution.py:358
  55.3 2.3 %copy-done.1 = bf16[4096,576]{0,1:T(8,128)(2,1)S(1)} copy-done((bf16[4096,576]{0,1:T(8,128)(2,1)S(1)}, bf16[4096,576]{0,1:T(8,128)(2,1)}, u32[]{:S(2)}) %copy-start.1) | copy-done | bytes 4718616
  57.6 1.2 copy-done.2
  58.9 23.8 %shard_map.77 = (s16[8,256,4096]{2,1,0:T(8,128)(2,1)}, f32[8,256,512]{2,1,0:T(8,128)}, f32[8,2,256]{2,1,0:T(2,128)S(1)}, f32[8,4,4096]{2,1,0:T(4,128)S(1)}) custom-call(s32[41]{0:T(128)S(1)} %concatenate.45.info, bf16[576,4096]{1,0:T(8,128)(2,1)S(1)} %bitcast.28, bf16[4096,128]{1,0:T(8,128)(2,1)S(1)} %copy-done.2, ...), custom_call_target="tpu_custom_call" | custom-call | flops 17179869184 | bytes 16777216 | tf_op jit(solution)/shard_map/pallas_call | solution.py:194
  82.7 24.3 %shard_map.78 = (s16[8,256,4096]{2,1,0:T(8,128)(2,1)}, f32[8,256,512]{2,1,0:T(8,128)}, f32[8,2,256]{2,1,0:T(2,128)S(1)}, f32[8,4,4096]{2,1,0:T(4,128)S(1)}) custom-call(s32[41]{0:T(128)S(1)} %concatenate.45.info, bf16[576,4096]{1,0:T(8,128)(2,1)S(1)} %bitcast.29, bf16[4096,128]{1,0:T(8,128)(2,1)S(1)} %copy-done.2, ...), custom_call_target="tpu_custom_call" | custom-call | flops 17179869184 | bytes 16777216 | tf_op jit(solution)/shard_map/pallas_call | solution.py:194
  107.0 1.1 shard_map.79
  108.2 0.8 copy-done
  109.7 0.9 collective-permute-done.17
  110.7 1.7 %collective-permute-start.18 = (f32[2,4128]{1,0:T(2,128)S(1)}, f32[2,4128]{1,0:T(2,128)S(1)}, u32[]{:S(2)}, u32[]{:S(2)}) collective-permute-start(f32[2,4128]{1,0:T(2,128)S(1)} %pad_maximum_fusion.1), channel_id=1, source_target_pairs={{0,4},{2,6},{4,0},{6,2},{8,12},{10,14},{12,8},{14,10},{16,20},{18,... | collective-permute-start | bytes 99080 | tf_op jit(solution)/shard_map/ppermute | solution.py:358
  112.4 2.3 %collective-permute-done.18 = f32[2,4128]{1,0:T(2,128)S(1)} collective-permute-done((f32[2,4128]{1,0:T(2,128)S(1)}, f32[2,4128]{1,0:T(2,128)S(1)}, u32[]{:S(2)}, u32[]{:S(2)}) %collective-permute-start.18) | collective-permute-done | bytes 33056 | tf_op jit(solution)/shard_map/ppermute | solution.py:358
  114.8 1.1 collective-permute-start.19
  115.9 2.8 %collective-permute-done.19 = f32[2,4128]{1,0:T(2,128)S(1)} collective-permute-done((f32[2,4128]{1,0:T(2,128)S(1)}, f32[2,4128]{1,0:T(2,128)S(1)}, u32[]{:S(2)}, u32[]{:S(2)}) %collective-permute-start.19) | collective-permute-done | bytes 33056 | tf_op jit(solution)/shard_map/ppermute | solution.py:358
  118.9 7.4 %collective-permute-start.20 = (f32[2,4128]{1,0:T(2,128)S(1)}, f32[2,4128]{1,0:T(2,128)S(1)}, u32[]{:S(2)}, u32[]{:S(2)}) collective-permute-start(f32[2,4128]{1,0:T(2,128)S(1)} %pad_maximum_fusion.3), channel_id=1, source_target_pairs={{0,16},{2,18},{4,20},{6,22},{8,24},{10,26},{12,28},{14,30},{16,0},... | collective-permute-start | bytes 99080 | tf_op jit(solution)/shard_map/ppermute | solution.py:358
  126.2 1.9 %collective-permute-done.20 = f32[2,4128]{1,0:T(2,128)S(1)} collective-permute-done((f32[2,4128]{1,0:T(2,128)S(1)}, f32[2,4128]{1,0:T(2,128)S(1)}, u32[]{:S(2)}, u32[]{:S(2)}) %collective-permute-start.20) | collective-permute-done | bytes 33056 | tf_op jit(solution)/shard_map/ppermute | solution.py:358
  128.3 0.6 pad_maximum_fusion.4.refs_4_
  129.0 0.7 broadcast_in_dim.10.refs_6_
  129.6 19.5 %shard_map.80 = (f32[32,4096]{1,0:T(8,128)}, f32[32,4096]{1,0:T(8,128)}) custom-call(s16[1,8,256,4096]{3,2,1,0:T(8,128)(2,1)} %bitcast.30, f32[1,8,256,512]{3,2,1,0:T(8,128)} %bitcast.32, s16[1,8,256,4096]{3,2,1,0:T(8,128)(2,1)} %bitcast.31, f32[1,8,256,512]{3,2,1,0:T(8,128)} %bitcast.33, f32[2,16,1,256]{3,2,1,0:T(1,128)} %pad_maximum_fusion.4.refs_4_, ...), custom_call_target="tpu_custom_call" | custom-call | flops 33554432 | bytes 33554432 | tf_op jit(solution)/shard_map/pallas_call | solution.py:294
  (49 shorter events, 3.6 us)
Async XLA Ops:
  3.4 13.4 %collective-permute-start = (bf16[1,272,640]{2,1,0:T(8,128)(2,1)S(1)}, bf16[1,272,640]{2,1,0:T(8,128)(2,1)S(1)}, u32[]{:S(2)}, u32[]{:S(2)}) collective-permute-start(bf16[1,272,640]{2,1,0:T(8,128)(2,1)S(1)} %fusion.2), channel_id=1, source_target_pairs={{0,16},{2,18},{4,20},{6,22},{8,24},{10,26},{12,28},{14,30},{17,1},... | collective-permute-start | bytes 1044488 | tf_op jit(solution)/shard_map/ppermute | solution.py:391
  9.3 17.5 %collective-permute-start.8 = (bf16[1,272,640]{2,1,0:T(8,128)(2,1)S(1)}, bf16[1,272,640]{2,1,0:T(8,128)(2,1)S(1)}, u32[]{:S(2)}, u32[]{:S(2)}) collective-permute-start(bf16[1,272,640]{2,1,0:T(8,128)(2,1)S(1)} %fusion.2), channel_id=1, source_target_pairs={{1,0},{3,2},{5,4},{7,6},{9,8},{11,10},{13,12},{15,14},{16,17},{18,... | collective-permute-start | bytes 1044488 | tf_op jit(solution)/shard_map/ppermute | solution.py:392
  10.6 16.2 %collective-permute-start.9 = (bf16[1,272,640]{2,1,0:T(8,128)(2,1)S(1)}, bf16[1,272,640]{2,1,0:T(8,128)(2,1)S(1)}, u32[]{:S(2)}, u32[]{:S(2)}) collective-permute-start(bf16[1,272,640]{2,1,0:T(8,128)(2,1)S(1)} %fusion.2), channel_id=1, source_target_pairs={{1,16},{3,18},{5,20},{7,22},{9,24},{11,26},{13,28},{15,30},{16,1},... | collective-permute-start | bytes 1044488 | tf_op jit(solution)/shard_map/ppermute | solution.py:393
  17.9 22.0 %collective-permute-start.2 = (bf16[1,272,640]{2,1,0:T(8,128)(2,1)S(1)}, bf16[1,272,640]{2,1,0:T(8,128)(2,1)S(1)}, u32[]{:S(2)}, u32[]{:S(2)}) collective-permute-start(bf16[1,272,640]{2,1,0:T(8,128)(2,1)S(1)} %broadcast_select_fusion.1.rest_0_), channel_id=1, source_target_pairs={{0,8},{2,10},{4,12},{6,14},{8,0},{10,2},{12,4},{14,6},{16,24},{18,... | collective-permute-start | bytes 1044488 | tf_op jit(solution)/shard_map/ppermute | solution.py:358
  26.9 14.5 %collective-permute-start.10 = (bf16[1,272,640]{2,1,0:T(8,128)(2,1)S(1)}, bf16[1,272,640]{2,1,0:T(8,128)(2,1)S(1)}, u32[]{:S(2)}, u32[]{:S(2)}) collective-permute-start(bf16[1,272,640]{2,1,0:T(8,128)(2,1)S(1)} %broadcast_select_fusion.rest_0_), channel_id=1, source_target_pairs={{0,4},{2,6},{4,0},{6,2},{8,12},{10,14},{12,8},{14,10},{16,20},{18,... | collective-permute-start | bytes 1044488 | tf_op jit(solution)/shard_map/ppermute | solution.py:358
  28.4 18.9 %collective-permute-start.11 = (bf16[1,272,640]{2,1,0:T(8,128)(2,1)S(1)}, bf16[1,272,640]{2,1,0:T(8,128)(2,1)S(1)}, u32[]{:S(2)}, u32[]{:S(2)}) collective-permute-start(bf16[1,272,640]{2,1,0:T(8,128)(2,1)S(1)} %broadcast_select_fusion.rest_0_), channel_id=1, source_target_pairs={{0,8},{2,10},{4,12},{6,14},{8,0},{10,2},{12,4},{14,6},{16,24},{18,... | collective-permute-start | bytes 1044488 | tf_op jit(solution)/shard_map/ppermute | solution.py:358
  28.5 18.9 %collective-permute-start.1 = (bf16[1,272,640]{2,1,0:T(8,128)(2,1)S(1)}, bf16[1,272,640]{2,1,0:T(8,128)(2,1)S(1)}, u32[]{:S(2)}, u32[]{:S(2)}) collective-permute-start(bf16[1,272,640]{2,1,0:T(8,128)(2,1)S(1)} %broadcast_select_fusion.1.rest_0_), channel_id=1, source_target_pairs={{0,4},{2,6},{4,0},{6,2},{8,12},{10,14},{12,8},{14,10},{16,20},{18,... | collective-permute-start | bytes 1044488 | tf_op jit(solution)/shard_map/ppermute | solution.py:358
  39.8 11.8 %collective-permute-start.3 = (bf16[1,272,640]{2,1,0:T(8,128)(2,1)S(1)}, bf16[1,272,640]{2,1,0:T(8,128)(2,1)S(1)}, u32[]{:S(2)}, u32[]{:S(2)}) collective-permute-start(bf16[1,272,640]{2,1,0:T(8,128)(2,1)S(1)} %collective-permute-done.2.rest_2_), channel_id=1, source_target_pairs={{0,4},{2,6},{4,0},{6,2},{8,12},{10,14},{12,8},{14,10},{16,20},{18,... | collective-permute-start | bytes 1044488 | tf_op jit(solution)/shard_map/ppermute | solution.py:358
  41.3 11.1 %collective-permute-start.4 = (bf16[1,272,640]{2,1,0:T(8,128)(2,1)S(1)}, bf16[1,272,640]{2,1,0:T(8,128)(2,1)S(1)}, u32[]{:S(2)}, u32[]{:S(2)}) collective-permute-start(bf16[1,272,640]{2,1,0:T(8,128)(2,1)S(1)} %broadcast_select_fusion.1.rest_0_), channel_id=1, source_target_pairs={{0,2},{2,0},{4,6},{6,4},{8,10},{10,8},{12,14},{14,12},{16,18},{18,... | collective-permute-start | bytes 1044488 | tf_op jit(solution)/shard_map/ppermute | solution.py:358
  41.3 13.4 %collective-permute-start.12 = (bf16[1,272,640]{2,1,0:T(8,128)(2,1)S(1)}, bf16[1,272,640]{2,1,0:T(8,128)(2,1)S(1)}, u32[]{:S(2)}, u32[]{:S(2)}) collective-permute-start(bf16[1,272,640]{2,1,0:T(8,128)(2,1)S(1)} %collective-permute-done.10.rest_1_), channel_id=1, source_target_pairs={{0,8},{2,10},{4,12},{6,14},{8,0},{10,2},{12,4},{14,6},{16,24},{18,... | collective-permute-start | bytes 1044488 | tf_op jit(solution)/shard_map/ppermute | solution.py:358
  47.3 7.5 %collective-permute-start.6 = (bf16[1,272,640]{2,1,0:T(8,128)(2,1)S(1)}, bf16[1,272,640]{2,1,0:T(8,128)(2,1)S(1)}, u32[]{:S(2)}, u32[]{:S(2)}) collective-permute-start(bf16[1,272,640]{2,1,0:T(8,128)(2,1)S(1)} %collective-permute-done.2.rest_2_), channel_id=1, source_target_pairs={{0,2},{2,0},{4,6},{6,4},{8,10},{10,8},{12,14},{14,12},{16,18},{18,... | collective-permute-start | bytes 1044488 | tf_op jit(solution)/shard_map/ppermute | solution.py:358
  47.3 7.9 %collective-permute-start.5 = (bf16[1,272,640]{2,1,0:T(8,128)(2,1)S(1)}, bf16[1,272,640]{2,1,0:T(8,128)(2,1)}, u32[]{:S(2)}, u32[]{:S(2)}) collective-permute-start(bf16[1,272,640]{2,1,0:T(8,128)(2,1)S(1)} %collective-permute-done.1.rest_1_), channel_id=1, source_target_pairs={{0,2},{2,0},{4,6},{6,4},{8,10},{10,8},{12,14},{14,12},{16,18},{18,... | collective-permute-start | bytes 1044488 | tf_op jit(solution)/shard_map/ppermute | solution.py:358
  51.6 3.7 %collective-permute-start.7 = (bf16[1,272,640]{2,1,0:T(8,128)(2,1)S(1)}, bf16[1,272,640]{2,1,0:T(8,128)(2,1)}, u32[]{:S(2)}, u32[]{:S(2)}) collective-permute-start(bf16[1,272,640]{2,1,0:T(8,128)(2,1)S(1)} %collective-permute-done.3.rest_3_), channel_id=1, source_target_pairs={{0,2},{2,0},{4,6},{6,4},{8,10},{10,8},{12,14},{14,12},{16,18},{18,... | collective-permute-start | bytes 1044488 | tf_op jit(solution)/shard_map/ppermute | solution.py:358
  52.5 30.2 %collective-permute-start.13 = (bf16[1,272,640]{2,1,0:T(8,128)(2,1)S(1)}, bf16[1,272,640]{2,1,0:T(8,128)(2,1)S(1)}, u32[]{:S(2)}, u32[]{:S(2)}) collective-permute-start(bf16[1,272,640]{2,1,0:T(8,128)(2,1)S(1)} %broadcast_select_fusion.rest_0_), channel_id=1, source_target_pairs={{0,2},{2,0},{4,6},{6,4},{8,10},{10,8},{12,14},{14,12},{16,18},{18,... | collective-permute-start | bytes 1044488 | tf_op jit(solution)/shard_map/ppermute | solution.py:358
  54.7 28.0 %collective-permute-start.14 = (bf16[1,272,640]{2,1,0:T(8,128)(2,1)S(1)}, bf16[1,272,640]{2,1,0:T(8,128)(2,1)S(1)}, u32[]{:S(2)}, u32[]{:S(2)}) collective-permute-start(bf16[1,272,640]{2,1,0:T(8,128)(2,1)S(1)} %collective-permute-done.10.rest_1_), channel_id=1, source_target_pairs={{0,2},{2,0},{4,6},{6,4},{8,10},{10,8},{12,14},{14,12},{16,18},{18,... | collective-permute-start | bytes 1044488 | tf_op jit(solution)/shard_map/ppermute | solution.py:358
  54.8 27.9 %collective-permute-start.15 = (bf16[1,272,640]{2,1,0:T(8,128)(2,1)S(1)}, bf16[1,272,640]{2,1,0:T(8,128)(2,1)S(1)}, u32[]{:S(2)}, u32[]{:S(2)}) collective-permute-start(bf16[1,272,640]{2,1,0:T(8,128)(2,1)S(1)} %collective-permute-done.11.rest_2_), channel_id=1, source_target_pairs={{0,2},{2,0},{4,6},{6,4},{8,10},{10,8},{12,14},{14,12},{16,18},{18,... | collective-permute-start | bytes 1044488 | tf_op jit(solution)/shard_map/ppermute | solution.py:358
  55.2 27.5 %collective-permute-start.16 = (bf16[1,272,640]{2,1,0:T(8,128)(2,1)S(1)}, bf16[1,272,640]{2,1,0:T(8,128)(2,1)S(1)}, u32[]{:S(2)}, u32[]{:S(2)}) collective-permute-start(bf16[1,272,640]{2,1,0:T(8,128)(2,1)S(1)} %collective-permute-done.12.rest_3_), channel_id=1, source_target_pairs={{0,2},{2,0},{4,6},{6,4},{8,10},{10,8},{12,14},{14,12},{16,18},{18,... | collective-permute-start | bytes 1044488 | tf_op jit(solution)/shard_map/ppermute | solution.py:358
  55.3 2.3 %copy-start.1 = (bf16[4096,576]{0,1:T(8,128)(2,1)S(1)}, bf16[4096,576]{0,1:T(8,128)(2,1)}, u32[]{:S(2)}) copy-start(bf16[4096,576]{0,1:T(8,128)(2,1)} %param.9) | copy-start | bytes 14155780
  57.6 1.2 copy-start.2
  108.1 0.8 copy-start
  109.1 1.4 collective-permute-start.17
  110.7 4.0 %collective-permute-start.18 = (f32[2,4128]{1,0:T(2,128)S(1)}, f32[2,4128]{1,0:T(2,128)S(1)}, u32[]{:S(2)}, u32[]{:S(2)}) collective-permute-start(f32[2,4128]{1,0:T(2,128)S(1)} %pad_maximum_fusion.1), channel_id=1, source_target_pairs={{0,4},{2,6},{4,0},{6,2},{8,12},{10,14},{12,8},{14,10},{16,20},{18,... | collective-permute-start | bytes 99080 | tf_op jit(solution)/shard_map/ppermute | solution.py:358
  114.8 4.0 %collective-permute-start.19 = (f32[2,4128]{1,0:T(2,128)S(1)}, f32[2,4128]{1,0:T(2,128)S(1)}, u32[]{:S(2)}, u32[]{:S(2)}) collective-permute-start(f32[2,4128]{1,0:T(2,128)S(1)} %pad_maximum_fusion.2), channel_id=1, source_target_pairs={{0,8},{2,10},{4,12},{6,14},{8,0},{10,2},{12,4},{14,6},{16,24},{18,... | collective-permute-start | bytes 99080 | tf_op jit(solution)/shard_map/ppermute | solution.py:358
  118.9 9.3 %collective-permute-start.20 = (f32[2,4128]{1,0:T(2,128)S(1)}, f32[2,4128]{1,0:T(2,128)S(1)}, u32[]{:S(2)}, u32[]{:S(2)}) collective-permute-start(f32[2,4128]{1,0:T(2,128)S(1)} %pad_maximum_fusion.3), channel_id=1, source_target_pairs={{0,16},{2,18},{4,20},{6,22},{8,24},{10,26},{12,28},{14,30},{16,0},... | collective-permute-start | bytes 99080 | tf_op jit(solution)/shard_map/ppermute | solution.py:358

commit v4 on v3

--- a/solution.py
+++ b/solution.py
@@ -54,8 +54,8 @@
 
     def scores(u, q_ref, first_row, masked):
         s_ref, m_ref = s_all.at[u], m_all.at[u]
-        for at in range(0, span, min(512, span)):
-            size = min(512, span)
+        for at in range(0, span, min(256, span)):
+            size = min(256, span)
             y = jnp.dot(
                 q_ref[:queries, :latent],
                 kv_ref[:, u * span + at : u * span + at + size],
@@ -377,8 +377,8 @@
     home = me // half == plane
     mine = lax.rem(me, half)
 
-    def place(distance):
-        return mine ^ distance
+    def place(other, distance):
+        return (plane ^ other) * half + (mine ^ distance)
 
     to_away, to_beside, to_both = [], [], []
     for c in range(ctx):
@@ -397,11 +397,11 @@
     two_x, two_z = swap(two, 2), swap(two, 4)
     one_zx = swap(one_z, 2)
     two_xz = swap(two_x, 4)
-    swept = []
-    for part in ([one, one_x, one_z, one_zx], [two, two_x, two_z, two_xz]):
-        blocks = part + [swap(a, 1) for a in part]
-        swept.append(sweep_blocks(blocks, [place(k) for k in (0, 2, 4, 6, 1, 3, 5, 7)], 1))
-    return swept
+    blocks, places = [], []
+    for other, part in enumerate(([one, one_x, one_z, one_zx], [two, two_x, two_z, two_xz])):
+        blocks += part + [swap(a, 1) for a in part]
+        places += [place(other, k) for k in (0, 2, 4, 6, 1, 3, 5, 7)]
+    return [sweep_blocks(blocks, places, head)]
 
 
 def body(absorbed_query, index_query, index_weight, kv_cache, index_keys, lengths):

time: 150 us -> 148 us (0.987)
  starting transfers between devices: 32.9 us -> 41.3 us
  waiting for transfers between devices: 35.7 us -> 28.4 us
  Pallas kernels: 68.6 us -> 65.7 us
    ppermute x18, waiting for transfers between devices: 30.3 us -> 23.9 us  [swap(): return lax.ppermute(x, 'ctx', [(i, i ^ bit) for i in range(size)])]
    ppermute x18, starting transfers between devices: 25 us -> 30 us  [swap(): return lax.ppermute(x, 'ctx', [(i, i ^ bit) for i in range(size)])]
    ppermute x1, starting transfers between devices: 5.96 us -> 9.35 us  [bring_and_sweep(): away = lax.ppermute(block, ('ctx', 'head'), to_away)]
    pallas_call x2 -> x1, Pallas kernels: 48.1 us -> 45.6 us  [sweep(): pl.pallas_call(kernel, out_shape=(pltpu.HBM((count, queries, keys), jnp.i...]
    ppermute x1, waiting for transfers between devices: 5.4 us -> 3.45 us  [bring_and_sweep(): away = lax.ppermute(block, ('ctx', 'head'), to_away)]
    unnamed x7 -> x6, local copies, waits for them, and re-layouts: 4.36 us -> 4.36 us
  transfers between devices with their start and end apart: 21 -> 21, of which waited for: 9 -> 11; matrix products, arithmetic and copies ran while one was open for 1% -> 1% of each run, Pallas kernels for 16% -> 0%
where the time goes in v4:
time: 148 us; the launch traced here: 147 us
  Pallas kernels  65.7 us (44%)
  starting transfers between devices  41.3 us (28%)
  waiting for transfers between devices  28.4 us (19%)
  local copies, waits for them, and re-layouts  7.68 us (5%)
  other arithmetic  3.37 us (2%)
    pallas_call x1, Pallas kernels, sweep(): pl.pallas_call(kernel, out_shape=(pltpu.HBM((count, queries, keys), jnp.i...  45.6 us
    ppermute x18, starting transfers between devices, swap(): return lax.ppermute(x, 'ctx', [(i, i ^ bit) for i in range(size)])  30 us
    ppermute x18, waiting for transfers between devices, swap(): return lax.ppermute(x, 'ctx', [(i, i ^ bit) for i in range(size)])  23.9 us
    pallas_call x1, Pallas kernels, second(): pl.pallas_call(functools.partial(second_kernel, row_count, head_count, sc...  19 us
    ppermute x1, starting transfers between devices, bring_and_sweep(): away = lax.ppermute(block, ('ctx', 'head'), to_away)  9.35 us
    unnamed x6, local copies, waits for them, and re-layouts  4.36 us
    ppermute x1, waiting for transfers between devices, bring_and_sweep(): away = lax.ppermute(block, ('ctx', 'head'), to_away)  3.45 us
  transfers between devices with their start and end apart: 21, of which 11 were waited for; matrix products, arithmetic and copies ran while one was open for 1% of the time, Pallas kernels for 0%

profile of v4, /device:TPU:0, one launch (start us, length us, event | category | flops | bytes accessed | tf_op | source)
XLA Modules:
  0.0 147.4 jit_solution(18242479815134152130)
XLA Ops:
  0.6 0.8 reshape.79
  1.4 0.9 fusion.7
  2.3 1.1 fusion.2
  3.4 1.3 collective-permute-start.8
  5.4 9.4 %collective-permute-start = (bf16[1,272,640]{2,1,0:T(8,128)(2,1)S(1)}, bf16[1,272,640]{2,1,0:T(8,128)(2,1)S(1)}, u32[]{:S(2)}, u32[]{:S(2)}) collective-permute-start(bf16[1,272,640]{2,1,0:T(8,128)(2,1)S(1)} %fusion.2), channel_id=1, source_target_pairs={{0,16},{2,18},{4,20},{6,22},{8,24},{10,26},{12,28},{14,30},{17,1},... | collective-permute-start | bytes 1044488 | tf_op jit(solution)/shard_map/ppermute | solution.py:391
  14.7 1.0 collective-permute-done.8
  15.9 2.5 %collective-permute-start.11 = (bf16[1,272,640]{2,1,0:T(8,128)(2,1)S(1)}, bf16[1,272,640]{2,1,0:T(8,128)(2,1)S(1)}, u32[]{:S(2)}, u32[]{:S(2)}) collective-permute-start(bf16[1,272,640]{2,1,0:T(8,128)(2,1)S(1)} %broadcast_select_fusion.rest_8_), channel_id=1, source_target_pairs={{0,8},{2,10},{4,12},{6,14},{8,0},{10,2},{12,4},{14,6},{16,24},{18,... | collective-permute-start | bytes 1044488 | tf_op jit(solution)/shard_map/ppermute | solution.py:358
  18.4 1.5 %collective-permute-start.10 = (bf16[1,272,640]{2,1,0:T(8,128)(2,1)S(1)}, bf16[1,272,640]{2,1,0:T(8,128)(2,1)S(1)}, u32[]{:S(2)}, u32[]{:S(2)}) collective-permute-start(bf16[1,272,640]{2,1,0:T(8,128)(2,1)S(1)} %broadcast_select_fusion.rest_8_), channel_id=1, source_target_pairs={{0,4},{2,6},{4,0},{6,2},{8,12},{10,14},{12,8},{14,10},{16,20},{18,... | collective-permute-start | bytes 1044488 | tf_op jit(solution)/shard_map/ppermute | solution.py:358
  19.9 3.4 %collective-permute-done = bf16[1,272,640]{2,1,0:T(8,128)(2,1)S(1)} collective-permute-done((bf16[1,272,640]{2,1,0:T(8,128)(2,1)S(1)}, bf16[1,272,640]{2,1,0:T(8,128)(2,1)S(1)}, u32[]{:S(2)}, u32[]{:S(2)}) %collective-permute-start) | collective-permute-done | bytes 348192 | tf_op jit(solution)/shard_map/ppermute | solution.py:391
  23.3 1.1 broadcast_select_fusion.1.rest_0_
  24.4 7.5 %collective-permute-start.2 = (bf16[1,272,640]{2,1,0:T(8,128)(2,1)S(1)}, bf16[1,272,640]{2,1,0:T(8,128)(2,1)S(1)}, u32[]{:S(2)}, u32[]{:S(2)}) collective-permute-start(bf16[1,272,640]{2,1,0:T(8,128)(2,1)S(1)} %broadcast_select_fusion.1.rest_0_), channel_id=1, source_target_pairs={{0,8},{2,10},{4,12},{6,14},{8,0},{10,2},{12,4},{14,6},{16,24},{18,... | collective-permute-start | bytes 1044488 | tf_op jit(solution)/shard_map/ppermute | solution.py:358
  31.9 1.5 %collective-permute-start.1 = (bf16[1,272,640]{2,1,0:T(8,128)(2,1)S(1)}, bf16[1,272,640]{2,1,0:T(8,128)(2,1)S(1)}, u32[]{:S(2)}, u32[]{:S(2)}) collective-permute-start(bf16[1,272,640]{2,1,0:T(8,128)(2,1)S(1)} %broadcast_select_fusion.1.rest_0_), channel_id=1, source_target_pairs={{0,4},{2,6},{4,0},{6,2},{8,12},{10,14},{12,8},{14,10},{16,20},{18,... | collective-permute-start | bytes 1044488 | tf_op jit(solution)/shard_map/ppermute | solution.py:358
  33.7 7.4 %collective-permute-done.2.rest_2_ = bf16[1,272,640]{2,1,0:T(8,128)(2,1)S(1)} collective-permute-done((bf16[1,272,640]{2,1,0:T(8,128)(2,1)S(1)}, bf16[1,272,640]{2,1,0:T(8,128)(2,1)S(1)}, u32[]{:S(2)}, u32[]{:S(2)}) %collective-permute-start.2) | collective-permute-done | bytes 348192 | tf_op jit(solution)/shard_map/ppermute | solution.py:358
  41.2 1.9 %collective-permute-start.3 = (bf16[1,272,640]{2,1,0:T(8,128)(2,1)S(1)}, bf16[1,272,640]{2,1,0:T(8,128)(2,1)}, u32[]{:S(2)}, u32[]{:S(2)}) collective-permute-start(bf16[1,272,640]{2,1,0:T(8,128)(2,1)S(1)} %collective-permute-done.2.rest_2_), channel_id=1, source_target_pairs={{0,4},{2,6},{4,0},{6,2},{8,12},{10,14},{12,8},{14,10},{16,20},{18,... | collective-permute-start | bytes 1044488 | tf_op jit(solution)/shard_map/ppermute | solution.py:358
  43.7 4.7 %collective-permute-done.12.rest_11_ = bf16[1,272,640]{2,1,0:T(8,128)(2,1)S(1)} collective-permute-done((bf16[1,272,640]{2,1,0:T(8,128)(2,1)S(1)}, bf16[1,272,640]{2,1,0:T(8,128)(2,1)S(1)}, u32[]{:S(2)}, u32[]{:S(2)}) %collective-permute-start.12) | collective-permute-done | bytes 348192 | tf_op jit(solution)/shard_map/ppermute | solution.py:358
  48.4 2.5 %collective-permute-done.3.rest_3_ = bf16[1,272,640]{2,1,0:T(8,128)(2,1)} collective-permute-done((bf16[1,272,640]{2,1,0:T(8,128)(2,1)S(1)}, bf16[1,272,640]{2,1,0:T(8,128)(2,1)}, u32[]{:S(2)}, u32[]{:S(2)}) %collective-permute-start.3) | collective-permute-done | bytes 348192 | tf_op jit(solution)/shard_map/ppermute | solution.py:358
  51.0 0.7 dynamic_slice.3.lengths
  51.8 1.1 collective-permute-done.7.rest_7_
  53.0 2.3 %copy-done.1 = bf16[4096,576]{0,1:T(8,128)(2,1)S(1)} copy-done((bf16[4096,576]{0,1:T(8,128)(2,1)S(1)}, bf16[4096,576]{0,1:T(8,128)(2,1)}, u32[]{:S(2)}) %copy-start.1) | copy-done | bytes 4718616
  55.3 1.2 copy-done.2
  56.5 45.6 %shard_map.77 = (s16[16,256,4096]{2,1,0:T(8,128)(2,1)}, f32[16,256,512]{2,1,0:T(8,128)}, f32[16,2,256]{2,1,0:T(2,128)S(1)}, f32[16,4,4096]{2,1,0:T(4,128)S(1)}) custom-call(s32[81]{0:T(128)S(1)} %concatenate.41.info, bf16[576,4096]{1,0:T(8,128)(2,1)S(1)} %bitcast.34, bf16[4096,128]{1,0:T(8,128)(2,1)S(1)} %copy-done.2, ...), custom_call_target="tpu_custom_call" | custom-call | flops 34359738368 | bytes 33554432 | tf_op jit(solution)/shard_map/pallas_call | solution.py:194
  102.2 1.1 shard_map.78
  103.3 0.8 copy-done
  104.6 1.0 collective-permute-done.17
  105.7 1.6 %collective-permute-start.18 = (f32[2,4128]{1,0:T(2,128)S(1)}, f32[2,4128]{1,0:T(2,128)S(1)}, u32[]{:S(2)}, u32[]{:S(2)}) collective-permute-start(f32[2,4128]{1,0:T(2,128)S(1)} %pad_maximum_fusion.1), channel_id=1, source_target_pairs={{0,4},{2,6},{4,0},{6,2},{8,12},{10,14},{12,8},{14,10},{16,20},{18,... | collective-permute-start | bytes 99080 | tf_op jit(solution)/shard_map/ppermute | solution.py:358
  107.3 2.4 %collective-permute-done.18 = f32[2,4128]{1,0:T(2,128)S(1)} collective-permute-done((f32[2,4128]{1,0:T(2,128)S(1)}, f32[2,4128]{1,0:T(2,128)S(1)}, u32[]{:S(2)}, u32[]{:S(2)}) %collective-permute-start.18) | collective-permute-done | bytes 33056 | tf_op jit(solution)/shard_map/ppermute | solution.py:358
  109.8 1.6 %collective-permute-start.19 = (f32[2,4128]{1,0:T(2,128)S(1)}, f32[2,4128]{1,0:T(2,128)S(1)}, u32[]{:S(2)}, u32[]{:S(2)}) collective-permute-start(f32[2,4128]{1,0:T(2,128)S(1)} %pad_maximum_fusion.2), channel_id=1, source_target_pairs={{0,8},{2,10},{4,12},{6,14},{8,0},{10,2},{12,4},{14,6},{16,24},{18,... | collective-permute-start | bytes 99080 | tf_op jit(solution)/shard_map/ppermute | solution.py:358
  111.4 2.4 %collective-permute-done.19 = f32[2,4128]{1,0:T(2,128)S(1)} collective-permute-done((f32[2,4128]{1,0:T(2,128)S(1)}, f32[2,4128]{1,0:T(2,128)S(1)}, u32[]{:S(2)}, u32[]{:S(2)}) %collective-permute-start.19) | collective-permute-done | bytes 33056 | tf_op jit(solution)/shard_map/ppermute | solution.py:358
  113.9 11.1 %collective-permute-start.20 = (f32[2,4128]{1,0:T(2,128)S(1)}, f32[2,4128]{1,0:T(2,128)S(1)}, u32[]{:S(2)}, u32[]{:S(2)}) collective-permute-start(f32[2,4128]{1,0:T(2,128)S(1)} %pad_maximum_fusion.3), channel_id=1, source_target_pairs={{0,16},{2,18},{4,20},{6,22},{8,24},{10,26},{12,28},{14,30},{16,0},... | collective-permute-start | bytes 99080 | tf_op jit(solution)/shard_map/ppermute | solution.py:358
  125.0 1.9 %collective-permute-done.20 = f32[2,4128]{1,0:T(2,128)S(1)} collective-permute-done((f32[2,4128]{1,0:T(2,128)S(1)}, f32[2,4128]{1,0:T(2,128)S(1)}, u32[]{:S(2)}, u32[]{:S(2)}) %collective-permute-start.20) | collective-permute-done | bytes 33056 | tf_op jit(solution)/shard_map/ppermute | solution.py:358
  127.7 0.7 broadcast_in_dim.10.refs_4_
  128.4 19.0 %shard_map.79 = (f32[32,4096]{1,0:T(8,128)}, f32[32,4096]{1,0:T(8,128)}) custom-call(s16[2,8,256,4096]{3,2,1,0:T(8,128)(2,1)} %bitcast.35, f32[2,8,256,512]{3,2,1,0:T(8,128)} %bitcast.36, f32[2,16,1,256]{3,2,1,0:T(1,128)} %pad_maximum_fusion.4.refs_2_, f32[32,4096]{1,0:T(8,128)} %copy-done, f32[2,32,128]{2,1,0:T(8,128)} %broadcast_in_dim.10.refs_4_), custom_call_target="tpu_custom_call" | custom-call | flops 33554432 | bytes 33554432 | tf_op jit(solution)/shard_map/pallas_call | solution.py:294
  (46 shorter events, 3.4 us)
Async XLA Ops:
  3.4 12.4 %collective-permute-start.8 = (bf16[1,272,640]{2,1,0:T(8,128)(2,1)S(1)}, bf16[1,272,640]{2,1,0:T(8,128)(2,1)S(1)}, u32[]{:S(2)}, u32[]{:S(2)}) collective-permute-start(bf16[1,272,640]{2,1,0:T(8,128)(2,1)S(1)} %fusion.2), channel_id=1, source_target_pairs={{1,0},{3,2},{5,4},{7,6},{9,8},{11,10},{13,12},{15,14},{16,17},{18,... | collective-permute-start | bytes 1044488 | tf_op jit(solution)/shard_map/ppermute | solution.py:392
  4.7 11.1 %collective-permute-start.9 = (bf16[1,272,640]{2,1,0:T(8,128)(2,1)S(1)}, bf16[1,272,640]{2,1,0:T(8,128)(2,1)S(1)}, u32[]{:S(2)}, u32[]{:S(2)}) collective-permute-start(bf16[1,272,640]{2,1,0:T(8,128)(2,1)S(1)} %fusion.2), channel_id=1, source_target_pairs={{1,16},{3,18},{5,20},{7,22},{9,24},{11,26},{13,28},{15,30},{16,1},... | collective-permute-start | bytes 1044488 | tf_op jit(solution)/shard_map/ppermute | solution.py:393
  5.4 18.0 %collective-permute-start = (bf16[1,272,640]{2,1,0:T(8,128)(2,1)S(1)}, bf16[1,272,640]{2,1,0:T(8,128)(2,1)S(1)}, u32[]{:S(2)}, u32[]{:S(2)}) collective-permute-start(bf16[1,272,640]{2,1,0:T(8,128)(2,1)S(1)} %fusion.2), channel_id=1, source_target_pairs={{0,16},{2,18},{4,20},{6,22},{8,24},{10,26},{12,28},{14,30},{17,1},... | collective-permute-start | bytes 1044488 | tf_op jit(solution)/shard_map/ppermute | solution.py:391
  15.8 16.1 %collective-permute-start.13 = (bf16[1,272,640]{2,1,0:T(8,128)(2,1)S(1)}, bf16[1,272,640]{2,1,0:T(8,128)(2,1)S(1)}, u32[]{:S(2)}, u32[]{:S(2)}) collective-permute-start(bf16[1,272,640]{2,1,0:T(8,128)(2,1)S(1)} %broadcast_select_fusion.rest_8_), channel_id=1, source_target_pairs={{0,2},{2,0},{4,6},{6,4},{8,10},{10,8},{12,14},{14,12},{16,18},{18,... | collective-permute-start | bytes 1044488 | tf_op jit(solution)/shard_map/ppermute | solution.py:358
  15.9 17.8 %collective-permute-start.11 = (bf16[1,272,640]{2,1,0:T(8,128)(2,1)S(1)}, bf16[1,272,640]{2,1,0:T(8,128)(2,1)S(1)}, u32[]{:S(2)}, u32[]{:S(2)}) collective-permute-start(bf16[1,272,640]{2,1,0:T(8,128)(2,1)S(1)} %broadcast_select_fusion.rest_8_), channel_id=1, source_target_pairs={{0,8},{2,10},{4,12},{6,14},{8,0},{10,2},{12,4},{14,6},{16,24},{18,... | collective-permute-start | bytes 1044488 | tf_op jit(solution)/shard_map/ppermute | solution.py:358
  18.4 15.4 %collective-permute-start.10 = (bf16[1,272,640]{2,1,0:T(8,128)(2,1)S(1)}, bf16[1,272,640]{2,1,0:T(8,128)(2,1)S(1)}, u32[]{:S(2)}, u32[]{:S(2)}) collective-permute-start(bf16[1,272,640]{2,1,0:T(8,128)(2,1)S(1)} %broadcast_select_fusion.rest_8_), channel_id=1, source_target_pairs={{0,4},{2,6},{4,0},{6,2},{8,12},{10,14},{12,8},{14,10},{16,20},{18,... | collective-permute-start | bytes 1044488 | tf_op jit(solution)/shard_map/ppermute | solution.py:358
  24.4 16.8 %collective-permute-start.2 = (bf16[1,272,640]{2,1,0:T(8,128)(2,1)S(1)}, bf16[1,272,640]{2,1,0:T(8,128)(2,1)S(1)}, u32[]{:S(2)}, u32[]{:S(2)}) collective-permute-start(bf16[1,272,640]{2,1,0:T(8,128)(2,1)S(1)} %broadcast_select_fusion.1.rest_0_), channel_id=1, source_target_pairs={{0,8},{2,10},{4,12},{6,14},{8,0},{10,2},{12,4},{14,6},{16,24},{18,... | collective-permute-start | bytes 1044488 | tf_op jit(solution)/shard_map/ppermute | solution.py:358
  31.9 11.1 %collective-permute-start.4 = (bf16[1,272,640]{2,1,0:T(8,128)(2,1)S(1)}, bf16[1,272,640]{2,1,0:T(8,128)(2,1)S(1)}, u32[]{:S(2)}, u32[]{:S(2)}) collective-permute-start(bf16[1,272,640]{2,1,0:T(8,128)(2,1)S(1)} %broadcast_select_fusion.1.rest_0_), channel_id=1, source_target_pairs={{0,2},{2,0},{4,6},{6,4},{8,10},{10,8},{12,14},{14,12},{16,18},{18,... | collective-permute-start | bytes 1044488 | tf_op jit(solution)/shard_map/ppermute | solution.py:358
  31.9 11.1 %collective-permute-start.1 = (bf16[1,272,640]{2,1,0:T(8,128)(2,1)S(1)}, bf16[1,272,640]{2,1,0:T(8,128)(2,1)S(1)}, u32[]{:S(2)}, u32[]{:S(2)}) collective-permute-start(bf16[1,272,640]{2,1,0:T(8,128)(2,1)S(1)} %broadcast_select_fusion.1.rest_0_), channel_id=1, source_target_pairs={{0,4},{2,6},{4,0},{6,2},{8,12},{10,14},{12,8},{14,10},{16,20},{18,... | collective-permute-start | bytes 1044488 | tf_op jit(solution)/shard_map/ppermute | solution.py:358
  33.7 9.8 %collective-permute-start.15 = (bf16[1,272,640]{2,1,0:T(8,128)(2,1)S(1)}, bf16[1,272,640]{2,1,0:T(8,128)(2,1)S(1)}, u32[]{:S(2)}, u32[]{:S(2)}) collective-permute-start(bf16[1,272,640]{2,1,0:T(8,128)(2,1)S(1)} %collective-permute-done.11.rest_10_), channel_id=1, source_target_pairs={{0,2},{2,0},{4,6},{6,4},{8,10},{10,8},{12,14},{14,12},{16,18},{18,... | collective-permute-start | bytes 1044488 | tf_op jit(solution)/shard_map/ppermute | solution.py:358
  33.7 14.7 %collective-permute-start.12 = (bf16[1,272,640]{2,1,0:T(8,128)(2,1)S(1)}, bf16[1,272,640]{2,1,0:T(8,128)(2,1)S(1)}, u32[]{:S(2)}, u32[]{:S(2)}) collective-permute-start(bf16[1,272,640]{2,1,0:T(8,128)(2,1)S(1)} %collective-permute-done.10.rest_9_), channel_id=1, source_target_pairs={{0,8},{2,10},{4,12},{6,14},{8,0},{10,2},{12,4},{14,6},{16,24},{18,... | collective-permute-start | bytes 1044488 | tf_op jit(solution)/shard_map/ppermute | solution.py:358
  41.2 9.8 %collective-permute-start.3 = (bf16[1,272,640]{2,1,0:T(8,128)(2,1)S(1)}, bf16[1,272,640]{2,1,0:T(8,128)(2,1)}, u32[]{:S(2)}, u32[]{:S(2)}) collective-permute-start(bf16[1,272,640]{2,1,0:T(8,128)(2,1)S(1)} %collective-permute-done.2.rest_2_), channel_id=1, source_target_pairs={{0,4},{2,6},{4,0},{6,2},{8,12},{10,14},{12,8},{14,10},{16,20},{18,... | collective-permute-start | bytes 1044488 | tf_op jit(solution)/shard_map/ppermute | solution.py:358
  43.1 8.7 %collective-permute-start.14 = (bf16[1,272,640]{2,1,0:T(8,128)(2,1)S(1)}, bf16[1,272,640]{2,1,0:T(8,128)(2,1)}, u32[]{:S(2)}, u32[]{:S(2)}) collective-permute-start(bf16[1,272,640]{2,1,0:T(8,128)(2,1)S(1)} %collective-permute-done.10.rest_9_), channel_id=1, source_target_pairs={{0,2},{2,0},{4,6},{6,4},{8,10},{10,8},{12,14},{14,12},{16,18},{18,... | collective-permute-start | bytes 1044488 | tf_op jit(solution)/shard_map/ppermute | solution.py:358
  43.1 8.7 %collective-permute-start.6 = (bf16[1,272,640]{2,1,0:T(8,128)(2,1)S(1)}, bf16[1,272,640]{2,1,0:T(8,128)(2,1)}, u32[]{:S(2)}, u32[]{:S(2)}) collective-permute-start(bf16[1,272,640]{2,1,0:T(8,128)(2,1)S(1)} %collective-permute-done.2.rest_2_), channel_id=1, source_target_pairs={{0,2},{2,0},{4,6},{6,4},{8,10},{10,8},{12,14},{14,12},{16,18},{18,... | collective-permute-start | bytes 1044488 | tf_op jit(solution)/shard_map/ppermute | solution.py:358
  43.6 8.2 %collective-permute-start.5 = (bf16[1,272,640]{2,1,0:T(8,128)(2,1)S(1)}, bf16[1,272,640]{2,1,0:T(8,128)(2,1)}, u32[]{:S(2)}, u32[]{:S(2)}) collective-permute-start(bf16[1,272,640]{2,1,0:T(8,128)(2,1)S(1)} %collective-permute-done.1.rest_1_), channel_id=1, source_target_pairs={{0,2},{2,0},{4,6},{6,4},{8,10},{10,8},{12,14},{14,12},{16,18},{18,... | collective-permute-start | bytes 1044488 | tf_op jit(solution)/shard_map/ppermute | solution.py:358
  48.4 3.4 %collective-permute-start.16 = (bf16[1,272,640]{2,1,0:T(8,128)(2,1)S(1)}, bf16[1,272,640]{2,1,0:T(8,128)(2,1)}, u32[]{:S(2)}, u32[]{:S(2)}) collective-permute-start(bf16[1,272,640]{2,1,0:T(8,128)(2,1)S(1)} %collective-permute-done.12.rest_11_), channel_id=1, source_target_pairs={{0,2},{2,0},{4,6},{6,4},{8,10},{10,8},{12,14},{14,12},{16,18},{18,... | collective-permute-start | bytes 1044488 | tf_op jit(solution)/shard_map/ppermute | solution.py:358
  50.9 2.0 %collective-permute-start.7 = (bf16[1,272,640]{2,1,0:T(8,128)(2,1)}, bf16[1,272,640]{2,1,0:T(8,128)(2,1)}, u32[]{:S(2)}, u32[]{:S(2)}) collective-permute-start(bf16[1,272,640]{2,1,0:T(8,128)(2,1)} %collective-permute-done.3.rest_3_), channel_id=1, source_target_pairs={{0,2},{2,0},{4,6},{6,4},{8,10},{10,8},{12,14},{14,12},{16,18},{18,... | collective-permute-start | bytes 1044488 | tf_op jit(solution)/shard_map/ppermute | solution.py:358
  53.0 2.3 %copy-start.1 = (bf16[4096,576]{0,1:T(8,128)(2,1)S(1)}, bf16[4096,576]{0,1:T(8,128)(2,1)}, u32[]{:S(2)}) copy-start(bf16[4096,576]{0,1:T(8,128)(2,1)} %param.9) | copy-start | bytes 14155780
  55.3 1.2 copy-start.2
  103.3 0.8 copy-start
  104.3 1.3 collective-permute-start.17
  105.7 4.0 %collective-permute-start.18 = (f32[2,4128]{1,0:T(2,128)S(1)}, f32[2,4128]{1,0:T(2,128)S(1)}, u32[]{:S(2)}, u32[]{:S(2)}) collective-permute-start(f32[2,4128]{1,0:T(2,128)S(1)} %pad_maximum_fusion.1), channel_id=1, source_target_pairs={{0,4},{2,6},{4,0},{6,2},{8,12},{10,14},{12,8},{14,10},{16,20},{18,... | collective-permute-start | bytes 99080 | tf_op jit(solution)/shard_map/ppermute | solution.py:358
  109.8 4.0 %collective-permute-start.19 = (f32[2,4128]{1,0:T(2,128)S(1)}, f32[2,4128]{1,0:T(2,128)S(1)}, u32[]{:S(2)}, u32[]{:S(2)}) collective-permute-start(f32[2,4128]{1,0:T(2,128)S(1)} %pad_maximum_fusion.2), channel_id=1, source_target_pairs={{0,8},{2,10},{4,12},{6,14},{8,0},{10,2},{12,4},{14,6},{16,24},{18,... | collective-permute-start | bytes 99080 | tf_op jit(solution)/shard_map/ppermute | solution.py:358
  113.9 13.0 %collective-permute-start.20 = (f32[2,4128]{1,0:T(2,128)S(1)}, f32[2,4128]{1,0:T(2,128)S(1)}, u32[]{:S(2)}, u32[]{:S(2)}) collective-permute-start(f32[2,4128]{1,0:T(2,128)S(1)} %pad_maximum_fusion.3), channel_id=1, source_target_pairs={{0,16},{2,18},{4,20},{6,22},{8,24},{10,26},{12,28},{14,30},{16,0},... | collective-permute-start | bytes 99080 | tf_op jit(solution)/shard_map/ppermute | solution.py:358

commit v5 on v4

--- a/solution.py
+++ b/solution.py
@@ -18,13 +18,13 @@
 second_vmem = 57 * 2**20
 
 
-def sweep_kernel(row_count, head_count, idx_heads, latent, spans, pack, sizes, info, kv_ref, ik_ref, *rest):
+def sweep_kernel(row_count, head_count, idx_heads, latent, spans, pack, sizes, info, kv_hbm, ik_hbm, *rest):
     sources, rest = rest[: len(sizes)], rest[len(sizes) :]
     e_hbm, top_hbm, stat_ref, part_ref, *rest = rest
-    e_slots, top_slots, s_all, m_all, run_m, run_t, turn_m, turn_t, iq_ref, w_ref, q_slots, e_sems, top_sems, q_sems = rest
+    e_slots, top_slots, s_all, m_all, run_m, run_t, turn_m, turn_t, iq_ref, w_ref, q_slots, kv_ref, ik_ref, e_sems, top_sems, q_sems, key_sems = rest
     count = sum(sizes)
     queries = row_count * head_count
-    keys = kv_ref.shape[1]
+    keys = kv_hbm.shape[1]
     span = keys // spans
     idx_queries = row_count * idx_heads
     scale = attention_scale * log2_e
@@ -168,6 +168,15 @@
     steps = count // pack
     for tile in range(pack):
         query_copy(tile, begin)
+    key_copies = []
+    for u in range(spans):
+        part = pl.ds(u * span, span)
+        key_copies.append(pltpu.make_async_copy(kv_hbm.at[:, part], kv_ref.at[:, part], key_sems.at[0, u]))
+        key_copies.append(pltpu.make_async_copy(ik_hbm.at[part, :], ik_ref.at[part, :], key_sems.at[1, u]))
+    for copy in key_copies:
+        copy.start()
+    for copy in key_copies:
+        copy.wait()
     lax.fori_loop(0, steps, step, 0)
     boundary(steps)
     for u in range(spans - lag, spans):
@@ -199,7 +208,7 @@
             jax.ShapeDtypeStruct((count, 2, queries), jnp.float32),
             jax.ShapeDtypeStruct((count, row_count, keys), jnp.float32),
         ),
-        in_specs=[pl.BlockSpec(memory_space=pltpu.SMEM), whole, whole] + [far] * len(blocks),
+        in_specs=[pl.BlockSpec(memory_space=pltpu.SMEM)] + [far] * (2 + len(blocks)),
         out_specs=[far, far, whole, whole],
         scratch_shapes=[
             pltpu.VMEM((3 * pack, queries, keys), jnp.int16),
@@ -211,8 +220,9 @@
         + [pltpu.VMEM((row_count * idx_heads, idx_keys.shape[1]), jnp.bfloat16)]
         + [pltpu.VMEM((row_count * idx_heads, lanes), jnp.float32)]
         + [pltpu.VMEM((2 * pack, block_rows, width), jnp.bfloat16)]
+        + [pltpu.VMEM(kv.shape, jnp.bfloat16), pltpu.VMEM(idx_keys.shape, jnp.bfloat16)]
         + [pltpu.SemaphoreType.DMA((3 * pack,))] * 2
-        + [pltpu.SemaphoreType.DMA((2 * pack,))],
+        + [pltpu.SemaphoreType.DMA((2 * pack,)), pltpu.SemaphoreType.DMA((2, spans))],
         compiler_params=pltpu.CompilerParams(vmem_limit_bytes=vmem_limit),
         cost_estimate=pl.CostEstimate(
             flops=2 * count * queries * keys * 1024,

time: 148 us -> 148 us (level)
  no operation moved by 1% of the time
where the time goes in v5:
time: 148 us
  Pallas kernels  66.2 us (45%)
  starting transfers between devices  42.1 us (28%)
  waiting for transfers between devices  27.9 us (19%)
  local copies, waits for them, and re-layouts  7.68 us (5%)
  other arithmetic  3.37 us (2%)
    pallas_call x1, Pallas kernels, sweep(): pl.pallas_call(kernel, out_shape=(pltpu.HBM((count, queries, keys), jnp.i...  46.1 us
    ppermute x18, starting transfers between devices, swap(): return lax.ppermute(x, 'ctx', [(i, i ^ bit) for i in range(size)])  30.8 us
    ppermute x18, waiting for transfers between devices, swap(): return lax.ppermute(x, 'ctx', [(i, i ^ bit) for i in range(size)])  23.5 us
    pallas_call x1, Pallas kernels, second(): pl.pallas_call(functools.partial(second_kernel, row_count, head_count, sc...  19 us
    ppermute x1, starting transfers between devices, bring_and_sweep(): away = lax.ppermute(block, ('ctx', 'head'), to_away)  9.35 us
    unnamed x6, local copies, waits for them, and re-layouts  4.36 us
    ppermute x1, waiting for transfers between devices, bring_and_sweep(): away = lax.ppermute(block, ('ctx', 'head'), to_away)  3.45 us
  transfers between devices with their start and end apart: 21, of which 11 were waited for; matrix products, arithmetic and copies ran while one was open for 1% of the time, Pallas kernels for 0%

profile of v5, /device:TPU:0, one launch (start us, length us, event | category | flops | bytes accessed | tf_op | source)
XLA Modules:
  0.0 148.1 jit_solution(7820038109026898742)
XLA Ops:
  0.6 0.8 reshape.79
  1.4 0.9 fusion.7
  2.3 1.1 fusion.2
  3.4 1.3 collective-permute-start.8
  5.4 9.4 %collective-permute-start = (bf16[1,272,640]{2,1,0:T(8,128)(2,1)S(1)}, bf16[1,272,640]{2,1,0:T(8,128)(2,1)S(1)}, u32[]{:S(2)}, u32[]{:S(2)}) collective-permute-start(bf16[1,272,640]{2,1,0:T(8,128)(2,1)S(1)} %fusion.2), channel_id=1, source_target_pairs={{0,16},{2,18},{4,20},{6,22},{8,24},{10,26},{12,28},{14,30},{17,1},... | collective-permute-start | bytes 1044488 | tf_op jit(solution)/shard_map/ppermute | solution.py:401
  14.7 1.0 collective-permute-done.8
  15.9 2.5 %collective-permute-start.11 = (bf16[1,272,640]{2,1,0:T(8,128)(2,1)S(1)}, bf16[1,272,640]{2,1,0:T(8,128)(2,1)S(1)}, u32[]{:S(2)}, u32[]{:S(2)}) collective-permute-start(bf16[1,272,640]{2,1,0:T(8,128)(2,1)S(1)} %broadcast_select_fusion.rest_8_), channel_id=1, source_target_pairs={{0,8},{2,10},{4,12},{6,14},{8,0},{10,2},{12,4},{14,6},{16,24},{18,... | collective-permute-start | bytes 1044488 | tf_op jit(solution)/shard_map/ppermute | solution.py:368
  18.4 1.5 %collective-permute-start.10 = (bf16[1,272,640]{2,1,0:T(8,128)(2,1)S(1)}, bf16[1,272,640]{2,1,0:T(8,128)(2,1)S(1)}, u32[]{:S(2)}, u32[]{:S(2)}) collective-permute-start(bf16[1,272,640]{2,1,0:T(8,128)(2,1)S(1)} %broadcast_select_fusion.rest_8_), channel_id=1, source_target_pairs={{0,4},{2,6},{4,0},{6,2},{8,12},{10,14},{12,8},{14,10},{16,20},{18,... | collective-permute-start | bytes 1044488 | tf_op jit(solution)/shard_map/ppermute | solution.py:368
  19.9 3.4 %collective-permute-done = bf16[1,272,640]{2,1,0:T(8,128)(2,1)S(1)} collective-permute-done((bf16[1,272,640]{2,1,0:T(8,128)(2,1)S(1)}, bf16[1,272,640]{2,1,0:T(8,128)(2,1)S(1)}, u32[]{:S(2)}, u32[]{:S(2)}) %collective-permute-start) | collective-permute-done | bytes 348192 | tf_op jit(solution)/shard_map/ppermute | solution.py:401
  23.3 1.1 broadcast_select_fusion.1.rest_0_
  24.4 7.5 %collective-permute-start.2 = (bf16[1,272,640]{2,1,0:T(8,128)(2,1)S(1)}, bf16[1,272,640]{2,1,0:T(8,128)(2,1)S(1)}, u32[]{:S(2)}, u32[]{:S(2)}) collective-permute-start(bf16[1,272,640]{2,1,0:T(8,128)(2,1)S(1)} %broadcast_select_fusion.1.rest_0_), channel_id=1, source_target_pairs={{0,8},{2,10},{4,12},{6,14},{8,0},{10,2},{12,4},{14,6},{16,24},{18,... | collective-permute-start | bytes 1044488 | tf_op jit(solution)/shard_map/ppermute | solution.py:368
  31.9 1.5 %collective-permute-start.1 = (bf16[1,272,640]{2,1,0:T(8,128)(2,1)S(1)}, bf16[1,272,640]{2,1,0:T(8,128)(2,1)S(1)}, u32[]{:S(2)}, u32[]{:S(2)}) collective-permute-start(bf16[1,272,640]{2,1,0:T(8,128)(2,1)S(1)} %broadcast_select_fusion.1.rest_0_), channel_id=1, source_target_pairs={{0,4},{2,6},{4,0},{6,2},{8,12},{10,14},{12,8},{14,10},{16,20},{18,... | collective-permute-start | bytes 1044488 | tf_op jit(solution)/shard_map/ppermute | solution.py:368
  33.7 7.4 %collective-permute-done.2.rest_2_ = bf16[1,272,640]{2,1,0:T(8,128)(2,1)S(1)} collective-permute-done((bf16[1,272,640]{2,1,0:T(8,128)(2,1)S(1)}, bf16[1,272,640]{2,1,0:T(8,128)(2,1)S(1)}, u32[]{:S(2)}, u32[]{:S(2)}) %collective-permute-start.2) | collective-permute-done | bytes 348192 | tf_op jit(solution)/shard_map/ppermute | solution.py:368
  41.2 1.9 %collective-permute-start.3 = (bf16[1,272,640]{2,1,0:T(8,128)(2,1)S(1)}, bf16[1,272,640]{2,1,0:T(8,128)(2,1)}, u32[]{:S(2)}, u32[]{:S(2)}) collective-permute-start(bf16[1,272,640]{2,1,0:T(8,128)(2,1)S(1)} %collective-permute-done.2.rest_2_), channel_id=1, source_target_pairs={{0,4},{2,6},{4,0},{6,2},{8,12},{10,14},{12,8},{14,10},{16,20},{18,... | collective-permute-start | bytes 1044488 | tf_op jit(solution)/shard_map/ppermute | solution.py:368
  43.7 4.7 %collective-permute-done.12.rest_11_ = bf16[1,272,640]{2,1,0:T(8,128)(2,1)S(1)} collective-permute-done((bf16[1,272,640]{2,1,0:T(8,128)(2,1)S(1)}, bf16[1,272,640]{2,1,0:T(8,128)(2,1)S(1)}, u32[]{:S(2)}, u32[]{:S(2)}) %collective-permute-start.12) | collective-permute-done | bytes 348192 | tf_op jit(solution)/shard_map/ppermute | solution.py:368
  48.4 2.5 %collective-permute-done.3.rest_3_ = bf16[1,272,640]{2,1,0:T(8,128)(2,1)} collective-permute-done((bf16[1,272,640]{2,1,0:T(8,128)(2,1)S(1)}, bf16[1,272,640]{2,1,0:T(8,128)(2,1)}, u32[]{:S(2)}, u32[]{:S(2)}) %collective-permute-start.3) | collective-permute-done | bytes 348192 | tf_op jit(solution)/shard_map/ppermute | solution.py:368
  51.0 0.7 dynamic_slice.3.lengths
  51.8 1.1 collective-permute-done.7.rest_7_
  53.0 2.3 %copy-done.1 = bf16[4096,576]{0,1:T(8,128)(2,1)S(1)} copy-done((bf16[4096,576]{0,1:T(8,128)(2,1)S(1)}, bf16[4096,576]{0,1:T(8,128)(2,1)}, u32[]{:S(2)}) %copy-start.1) | copy-done | bytes 4718616
  55.3 1.2 copy-done.2
  56.5 46.1 %shard_map.77 = (s16[16,256,4096]{2,1,0:T(8,128)(2,1)}, f32[16,256,512]{2,1,0:T(8,128)}, f32[16,2,256]{2,1,0:T(2,128)S(1)}, f32[16,4,4096]{2,1,0:T(4,128)S(1)}) custom-call(s32[81]{0:T(128)S(1)} %concatenate.41.info, bf16[576,4096]{1,0:T(8,128)(2,1)S(1)} %bitcast.34, bf16[4096,128]{1,0:T(8,128)(2,1)S(1)} %copy-done.2, ...), custom_call_target="tpu_custom_call" | custom-call | flops 34359738368 | bytes 33554432 | tf_op jit(solution)/shard_map/pallas_call | solution.py:203
  102.7 1.1 shard_map.78
  103.8 0.8 copy-done
  105.0 1.0 collective-permute-done.17
  106.2 1.6 %collective-permute-start.18 = (f32[2,4128]{1,0:T(2,128)S(1)}, f32[2,4128]{1,0:T(2,128)S(1)}, u32[]{:S(2)}, u32[]{:S(2)}) collective-permute-start(f32[2,4128]{1,0:T(2,128)S(1)} %pad_maximum_fusion.1), channel_id=1, source_target_pairs={{0,4},{2,6},{4,0},{6,2},{8,12},{10,14},{12,8},{14,10},{16,20},{18,... | collective-permute-start | bytes 99080 | tf_op jit(solution)/shard_map/ppermute | solution.py:368
  107.7 2.4 %collective-permute-done.18 = f32[2,4128]{1,0:T(2,128)S(1)} collective-permute-done((f32[2,4128]{1,0:T(2,128)S(1)}, f32[2,4128]{1,0:T(2,128)S(1)}, u32[]{:S(2)}, u32[]{:S(2)}) %collective-permute-start.18) | collective-permute-done | bytes 33056 | tf_op jit(solution)/shard_map/ppermute | solution.py:368
  110.3 2.2 %collective-permute-start.19 = (f32[2,4128]{1,0:T(2,128)S(1)}, f32[2,4128]{1,0:T(2,128)S(1)}, u32[]{:S(2)}, u32[]{:S(2)}) collective-permute-start(f32[2,4128]{1,0:T(2,128)S(1)} %pad_maximum_fusion.2), channel_id=1, source_target_pairs={{0,8},{2,10},{4,12},{6,14},{8,0},{10,2},{12,4},{14,6},{16,24},{18,... | collective-permute-start | bytes 99080 | tf_op jit(solution)/shard_map/ppermute | solution.py:368
  112.5 1.9 %collective-permute-done.19 = f32[2,4128]{1,0:T(2,128)S(1)} collective-permute-done((f32[2,4128]{1,0:T(2,128)S(1)}, f32[2,4128]{1,0:T(2,128)S(1)}, u32[]{:S(2)}, u32[]{:S(2)}) %collective-permute-start.19) | collective-permute-done | bytes 33056 | tf_op jit(solution)/shard_map/ppermute | solution.py:368
  114.5 11.3 %collective-permute-start.20 = (f32[2,4128]{1,0:T(2,128)S(1)}, f32[2,4128]{1,0:T(2,128)S(1)}, u32[]{:S(2)}, u32[]{:S(2)}) collective-permute-start(f32[2,4128]{1,0:T(2,128)S(1)} %pad_maximum_fusion.3), channel_id=1, source_target_pairs={{0,16},{2,18},{4,20},{6,22},{8,24},{10,26},{12,28},{14,30},{16,0},... | collective-permute-start | bytes 99080 | tf_op jit(solution)/shard_map/ppermute | solution.py:368
  125.8 1.9 %collective-permute-done.20 = f32[2,4128]{1,0:T(2,128)S(1)} collective-permute-done((f32[2,4128]{1,0:T(2,128)S(1)}, f32[2,4128]{1,0:T(2,128)S(1)}, u32[]{:S(2)}, u32[]{:S(2)}) %collective-permute-start.20) | collective-permute-done | bytes 33056 | tf_op jit(solution)/shard_map/ppermute | solution.py:368
  128.5 0.7 broadcast_in_dim.10.refs_4_
  129.2 19.0 %shard_map.79 = (f32[32,4096]{1,0:T(8,128)}, f32[32,4096]{1,0:T(8,128)}) custom-call(s16[2,8,256,4096]{3,2,1,0:T(8,128)(2,1)} %bitcast.35, f32[2,8,256,512]{3,2,1,0:T(8,128)} %bitcast.36, f32[2,16,1,256]{3,2,1,0:T(1,128)} %pad_maximum_fusion.4.refs_2_, f32[32,4096]{1,0:T(8,128)} %copy-done, f32[2,32,128]{2,1,0:T(8,128)} %broadcast_in_dim.10.refs_4_), custom_call_target="tpu_custom_call" | custom-call | flops 33554432 | bytes 33554432 | tf_op jit(solution)/shard_map/pallas_call | solution.py:304
  (46 shorter events, 3.4 us)
Async XLA Ops:
  3.4 12.4 %collective-permute-start.8 = (bf16[1,272,640]{2,1,0:T(8,128)(2,1)S(1)}, bf16[1,272,640]{2,1,0:T(8,128)(2,1)S(1)}, u32[]{:S(2)}, u32[]{:S(2)}) collective-permute-start(bf16[1,272,640]{2,1,0:T(8,128)(2,1)S(1)} %fusion.2), channel_id=1, source_target_pairs={{1,0},{3,2},{5,4},{7,6},{9,8},{11,10},{13,12},{15,14},{16,17},{18,... | collective-permute-start | bytes 1044488 | tf_op jit(solution)/shard_map/ppermute | solution.py:402
  4.7 11.1 %collective-permute-start.9 = (bf16[1,272,640]{2,1,0:T(8,128)(2,1)S(1)}, bf16[1,272,640]{2,1,0:T(8,128)(2,1)S(1)}, u32[]{:S(2)}, u32[]{:S(2)}) collective-permute-start(bf16[1,272,640]{2,1,0:T(8,128)(2,1)S(1)} %fusion.2), channel_id=1, source_target_pairs={{1,16},{3,18},{5,20},{7,22},{9,24},{11,26},{13,28},{15,30},{16,1},... | collective-permute-start | bytes 1044488 | tf_op jit(solution)/shard_map/ppermute | solution.py:403
  5.4 18.0 %collective-permute-start = (bf16[1,272,640]{2,1,0:T(8,128)(2,1)S(1)}, bf16[1,272,640]{2,1,0:T(8,128)(2,1)S(1)}, u32[]{:S(2)}, u32[]{:S(2)}) collective-permute-start(bf16[1,272,640]{2,1,0:T(8,128)(2,1)S(1)} %fusion.2), channel_id=1, source_target_pairs={{0,16},{2,18},{4,20},{6,22},{8,24},{10,26},{12,28},{14,30},{17,1},... | collective-permute-start | bytes 1044488 | tf_op jit(solution)/shard_map/ppermute | solution.py:401
  15.8 16.1 %collective-permute-start.13 = (bf16[1,272,640]{2,1,0:T(8,128)(2,1)S(1)}, bf16[1,272,640]{2,1,0:T(8,128)(2,1)S(1)}, u32[]{:S(2)}, u32[]{:S(2)}) collective-permute-start(bf16[1,272,640]{2,1,0:T(8,128)(2,1)S(1)} %broadcast_select_fusion.rest_8_), channel_id=1, source_target_pairs={{0,2},{2,0},{4,6},{6,4},{8,10},{10,8},{12,14},{14,12},{16,18},{18,... | collective-permute-start | bytes 1044488 | tf_op jit(solution)/shard_map/ppermute | solution.py:368
  15.9 17.8 %collective-permute-start.11 = (bf16[1,272,640]{2,1,0:T(8,128)(2,1)S(1)}, bf16[1,272,640]{2,1,0:T(8,128)(2,1)S(1)}, u32[]{:S(2)}, u32[]{:S(2)}) collective-permute-start(bf16[1,272,640]{2,1,0:T(8,128)(2,1)S(1)} %broadcast_select_fusion.rest_8_), channel_id=1, source_target_pairs={{0,8},{2,10},{4,12},{6,14},{8,0},{10,2},{12,4},{14,6},{16,24},{18,... | collective-permute-start | bytes 1044488 | tf_op jit(solution)/shard_map/ppermute | solution.py:368
  18.4 15.4 %collective-permute-start.10 = (bf16[1,272,640]{2,1,0:T(8,128)(2,1)S(1)}, bf16[1,272,640]{2,1,0:T(8,128)(2,1)S(1)}, u32[]{:S(2)}, u32[]{:S(2)}) collective-permute-start(bf16[1,272,640]{2,1,0:T(8,128)(2,1)S(1)} %broadcast_select_fusion.rest_8_), channel_id=1, source_target_pairs={{0,4},{2,6},{4,0},{6,2},{8,12},{10,14},{12,8},{14,10},{16,20},{18,... | collective-permute-start | bytes 1044488 | tf_op jit(solution)/shard_map/ppermute | solution.py:368
  24.4 16.8 %collective-permute-start.2 = (bf16[1,272,640]{2,1,0:T(8,128)(2,1)S(1)}, bf16[1,272,640]{2,1,0:T(8,128)(2,1)S(1)}, u32[]{:S(2)}, u32[]{:S(2)}) collective-permute-start(bf16[1,272,640]{2,1,0:T(8,128)(2,1)S(1)} %broadcast_select_fusion.1.rest_0_), channel_id=1, source_target_pairs={{0,8},{2,10},{4,12},{6,14},{8,0},{10,2},{12,4},{14,6},{16,24},{18,... | collective-permute-start | bytes 1044488 | tf_op jit(solution)/shard_map/ppermute | solution.py:368
  31.9 11.1 %collective-permute-start.4 = (bf16[1,272,640]{2,1,0:T(8,128)(2,1)S(1)}, bf16[1,272,640]{2,1,0:T(8,128)(2,1)S(1)}, u32[]{:S(2)}, u32[]{:S(2)}) collective-permute-start(bf16[1,272,640]{2,1,0:T(8,128)(2,1)S(1)} %broadcast_select_fusion.1.rest_0_), channel_id=1, source_target_pairs={{0,2},{2,0},{4,6},{6,4},{8,10},{10,8},{12,14},{14,12},{16,18},{18,... | collective-permute-start | bytes 1044488 | tf_op jit(solution)/shard_map/ppermute | solution.py:368
  31.9 11.1 %collective-permute-start.1 = (bf16[1,272,640]{2,1,0:T(8,128)(2,1)S(1)}, bf16[1,272,640]{2,1,0:T(8,128)(2,1)S(1)}, u32[]{:S(2)}, u32[]{:S(2)}) collective-permute-start(bf16[1,272,640]{2,1,0:T(8,128)(2,1)S(1)} %broadcast_select_fusion.1.rest_0_), channel_id=1, source_target_pairs={{0,4},{2,6},{4,0},{6,2},{8,12},{10,14},{12,8},{14,10},{16,20},{18,... | collective-permute-start | bytes 1044488 | tf_op jit(solution)/shard_map/ppermute | solution.py:368
  33.7 9.8 %collective-permute-start.15 = (bf16[1,272,640]{2,1,0:T(8,128)(2,1)S(1)}, bf16[1,272,640]{2,1,0:T(8,128)(2,1)S(1)}, u32[]{:S(2)}, u32[]{:S(2)}) collective-permute-start(bf16[1,272,640]{2,1,0:T(8,128)(2,1)S(1)} %collective-permute-done.11.rest_10_), channel_id=1, source_target_pairs={{0,2},{2,0},{4,6},{6,4},{8,10},{10,8},{12,14},{14,12},{16,18},{18,... | collective-permute-start | bytes 1044488 | tf_op jit(solution)/shard_map/ppermute | solution.py:368
  33.7 14.7 %collective-permute-start.12 = (bf16[1,272,640]{2,1,0:T(8,128)(2,1)S(1)}, bf16[1,272,640]{2,1,0:T(8,128)(2,1)S(1)}, u32[]{:S(2)}, u32[]{:S(2)}) collective-permute-start(bf16[1,272,640]{2,1,0:T(8,128)(2,1)S(1)} %collective-permute-done.10.rest_9_), channel_id=1, source_target_pairs={{0,8},{2,10},{4,12},{6,14},{8,0},{10,2},{12,4},{14,6},{16,24},{18,... | collective-permute-start | bytes 1044488 | tf_op jit(solution)/shard_map/ppermute | solution.py:368
  41.2 9.8 %collective-permute-start.3 = (bf16[1,272,640]{2,1,0:T(8,128)(2,1)S(1)}, bf16[1,272,640]{2,1,0:T(8,128)(2,1)}, u32[]{:S(2)}, u32[]{:S(2)}) collective-permute-start(bf16[1,272,640]{2,1,0:T(8,128)(2,1)S(1)} %collective-permute-done.2.rest_2_), channel_id=1, source_target_pairs={{0,4},{2,6},{4,0},{6,2},{8,12},{10,14},{12,8},{14,10},{16,20},{18,... | collective-permute-start | bytes 1044488 | tf_op jit(solution)/shard_map/ppermute | solution.py:368
  43.1 8.7 %collective-permute-start.14 = (bf16[1,272,640]{2,1,0:T(8,128)(2,1)S(1)}, bf16[1,272,640]{2,1,0:T(8,128)(2,1)}, u32[]{:S(2)}, u32[]{:S(2)}) collective-permute-start(bf16[1,272,640]{2,1,0:T(8,128)(2,1)S(1)} %collective-permute-done.10.rest_9_), channel_id=1, source_target_pairs={{0,2},{2,0},{4,6},{6,4},{8,10},{10,8},{12,14},{14,12},{16,18},{18,... | collective-permute-start | bytes 1044488 | tf_op jit(solution)/shard_map/ppermute | solution.py:368
  43.1 8.7 %collective-permute-start.6 = (bf16[1,272,640]{2,1,0:T(8,128)(2,1)S(1)}, bf16[1,272,640]{2,1,0:T(8,128)(2,1)}, u32[]{:S(2)}, u32[]{:S(2)}) collective-permute-start(bf16[1,272,640]{2,1,0:T(8,128)(2,1)S(1)} %collective-permute-done.2.rest_2_), channel_id=1, source_target_pairs={{0,2},{2,0},{4,6},{6,4},{8,10},{10,8},{12,14},{14,12},{16,18},{18,... | collective-permute-start | bytes 1044488 | tf_op jit(solution)/shard_map/ppermute | solution.py:368
  43.6 8.2 %collective-permute-start.5 = (bf16[1,272,640]{2,1,0:T(8,128)(2,1)S(1)}, bf16[1,272,640]{2,1,0:T(8,128)(2,1)}, u32[]{:S(2)}, u32[]{:S(2)}) collective-permute-start(bf16[1,272,640]{2,1,0:T(8,128)(2,1)S(1)} %collective-permute-done.1.rest_1_), channel_id=1, source_target_pairs={{0,2},{2,0},{4,6},{6,4},{8,10},{10,8},{12,14},{14,12},{16,18},{18,... | collective-permute-start | bytes 1044488 | tf_op jit(solution)/shard_map/ppermute | solution.py:368
  48.4 3.4 %collective-permute-start.16 = (bf16[1,272,640]{2,1,0:T(8,128)(2,1)S(1)}, bf16[1,272,640]{2,1,0:T(8,128)(2,1)}, u32[]{:S(2)}, u32[]{:S(2)}) collective-permute-start(bf16[1,272,640]{2,1,0:T(8,128)(2,1)S(1)} %collective-permute-done.12.rest_11_), channel_id=1, source_target_pairs={{0,2},{2,0},{4,6},{6,4},{8,10},{10,8},{12,14},{14,12},{16,18},{18,... | collective-permute-start | bytes 1044488 | tf_op jit(solution)/shard_map/ppermute | solution.py:368
  50.9 2.0 %collective-permute-start.7 = (bf16[1,272,640]{2,1,0:T(8,128)(2,1)}, bf16[1,272,640]{2,1,0:T(8,128)(2,1)}, u32[]{:S(2)}, u32[]{:S(2)}) collective-permute-start(bf16[1,272,640]{2,1,0:T(8,128)(2,1)} %collective-permute-done.3.rest_3_), channel_id=1, source_target_pairs={{0,2},{2,0},{4,6},{6,4},{8,10},{10,8},{12,14},{14,12},{16,18},{18,... | collective-permute-start | bytes 1044488 | tf_op jit(solution)/shard_map/ppermute | solution.py:368
  53.0 2.3 %copy-start.1 = (bf16[4096,576]{0,1:T(8,128)(2,1)S(1)}, bf16[4096,576]{0,1:T(8,128)(2,1)}, u32[]{:S(2)}) copy-start(bf16[4096,576]{0,1:T(8,128)(2,1)} %param.9) | copy-start | bytes 14155780
  55.3 1.2 copy-start.2
  103.8 0.8 copy-start
  104.8 1.3 collective-permute-start.17
  106.2 4.0 %collective-permute-start.18 = (f32[2,4128]{1,0:T(2,128)S(1)}, f32[2,4128]{1,0:T(2,128)S(1)}, u32[]{:S(2)}, u32[]{:S(2)}) collective-permute-start(f32[2,4128]{1,0:T(2,128)S(1)} %pad_maximum_fusion.1), channel_id=1, source_target_pairs={{0,4},{2,6},{4,0},{6,2},{8,12},{10,14},{12,8},{14,10},{16,20},{18,... | collective-permute-start | bytes 99080 | tf_op jit(solution)/shard_map/ppermute | solution.py:368
  110.3 4.1 %collective-permute-start.19 = (f32[2,4128]{1,0:T(2,128)S(1)}, f32[2,4128]{1,0:T(2,128)S(1)}, u32[]{:S(2)}, u32[]{:S(2)}) collective-permute-start(f32[2,4128]{1,0:T(2,128)S(1)} %pad_maximum_fusion.2), channel_id=1, source_target_pairs={{0,8},{2,10},{4,12},{6,14},{8,0},{10,2},{12,4},{14,6},{16,24},{18,... | collective-permute-start | bytes 99080 | tf_op jit(solution)/shard_map/ppermute | solution.py:368
  114.5 13.2 %collective-permute-start.20 = (f32[2,4128]{1,0:T(2,128)S(1)}, f32[2,4128]{1,0:T(2,128)S(1)}, u32[]{:S(2)}, u32[]{:S(2)}) collective-permute-start(f32[2,4128]{1,0:T(2,128)S(1)} %pad_maximum_fusion.3), channel_id=1, source_target_pairs={{0,16},{2,18},{4,20},{6,22},{8,24},{10,26},{12,28},{14,30},{16,0},... | collective-permute-start | bytes 99080 | tf_op jit(solution)/shard_map/ppermute | solution.py:368
